TPU v7x, 128 devices: a whole 4x4x4 slice. The times are simulated.
128 devices in a mesh: section: 4 (over z), dp: 32 (over x, y, core).
Axes of the slice: x: 4, y: 4, z: 4, core: 2. Of those that a mesh axis runs over, the one named last changes fastest.
Arguments:
- tokens_in: bfloat16 [2, 192, 8192], P(None, None, 'dp'), may hold values from -6 to 6
- cotangent: bfloat16 [2, 192, 8192], P(None, None, 'dp'), may hold values from -6 to 6
- base_weight: bfloat16 [4, 8192, 8192], P('section', None, 'dp'), may hold values from -0.0625 to 0.0625
- norm_gain: bfloat16 [4, 8192], P('section', 'dp'), may hold values from 0.25 to 5.5, as said below
- adapter_a: bfloat16 [4, 64, 32, 8192], P('section', None, None, 'dp'), may hold values from -0.0625 to 0.0625
- adapter_b: bfloat16 [4, 64, 32, 8192], P('section', None, None, 'dp'), may hold values from -1 to 1
- seg_ids: int32 [2, 192], replicated, may hold values from 0 to 63, never falling along the last dimension, each value on 1 to 48 neighbouring positions
- live_counts: int32 [2, 64], replicated, may hold values from 1 to 48
Outputs:
- section_out: bfloat16 [4, 2, 192, 8192], P('section', None, None, 'dp')
- grad_a: float32 [4, 64, 32, 8192], P('section', None, None, 'dp')
- grad_b: float32 [4, 64, 32, 8192], P('section', None, None, 'dp')
Inputs may be any that keep to these rules, and one draw needn't show every extreme that they name: `seg_ids`: never falling along the rows; every adapter has 1 to 48 rows in each micro-batch, and some adapter exactly 48. `norm_gain`: Positive.
All inputs are finite; a program needn't handle non-finite values.
Results may differ from a plain program's by a relative error of at most 0.018.
Values may be sent and summed in bfloat16 or wider, within the bound.
No kernel may reach another device: no remote copies, remote signals or barrier semaphores. Data moves between devices by JAX's collectives and lax.ppermute only.
A program may use at most 128 MiB of HBM per device.

v0:
```python
import jax
import jax.numpy as jnp
from jax import lax
from jax.sharding import PartitionSpec as P

EPSILON = 1e-06
SCALING = 2.0


def from_behind(shard, axis, by):
    size = lax.axis_size(axis)
    pairs = [(i, i + by) for i in range(size) if 0 <= i + by < size]
    return lax.ppermute(shard, axis, pairs)


def segment_tables(segment_row, live_row, adapter_count):
    row_count = segment_row.shape[0]
    labels = jnp.arange(adapter_count, dtype=jnp.int32)
    member = (segment_row[:, None] == labels[None, :]).astype(jnp.int32)
    counts = jnp.sum(member, axis=0)
    before = (labels[:, None] < labels[None, :]).astype(jnp.int32)
    starts = jnp.sum(counts[:, None] * before, axis=0)
    row_start = jnp.sum(member * starts[None, :], axis=1)
    row_limit = jnp.sum(member * jnp.minimum(live_row, counts)[None, :], axis=1)
    position = jnp.arange(row_count, dtype=jnp.int32) - row_start
    return (member.astype(jnp.float32), position < row_limit)


def spread_rank(values, member):
    joined = member[:, :, None] * values.astype(jnp.float32)[:, None, :]
    return joined.reshape(values.shape[0], -1).astype(jnp.bfloat16)


def select_rank(parts, member, rank):
    shaped = parts.reshape(parts.shape[0], member.shape[1], rank)
    return jnp.einsum("ra,rak->rk", member, shaped)


def forward_layer(inputs, gain_row, weight, down_flat, up_flat, member, rank):
    width = weight.shape[0]
    values = inputs.astype(jnp.float32)
    squares = lax.psum(jnp.sum(values * values, axis=1), "dp")
    inverse = lax.rsqrt(squares / width + EPSILON)
    normed = (values * inverse[:, None] * gain_row.astype(jnp.float32)[None, :]).astype(
        jnp.bfloat16
    )
    frozen_out = jnp.dot(
        lax.all_gather(normed, "dp", axis=1, tiled=True), weight, preferred_element_type=jnp.float32
    )
    down_parts = lax.dot_general(
        normed, down_flat, (((1,), (1,)), ((), ())), preferred_element_type=jnp.float32
    )
    down_proj = lax.psum(select_rank(down_parts, member, rank), "dp").astype(jnp.bfloat16)
    adapter_out = jnp.dot(
        spread_rank(down_proj, member), up_flat, preferred_element_type=jnp.float32
    )
    result = (values + frozen_out + SCALING * adapter_out).astype(jnp.bfloat16)
    return (result, normed, down_proj, inverse)


def backward_layer(
    grad_out, inputs, normed, down_proj, inverse, gain_row, weight, down_flat, up_flat, member, rank
):
    width = weight.shape[0]
    spread_down = spread_rank(down_proj, member)
    grad_up = SCALING * lax.dot_general(
        spread_down, grad_out, (((0,), (0,)), ((), ())), preferred_element_type=jnp.float32
    )
    up_parts = lax.dot_general(
        grad_out, up_flat, (((1,), (1,)), ((), ())), preferred_element_type=jnp.float32
    )
    summed_parts = lax.psum(select_rank(up_parts, member, rank), "dp")
    grad_down_proj = (SCALING * summed_parts).astype(jnp.bfloat16)
    spread_grad = spread_rank(grad_down_proj, member)
    grad_down = lax.dot_general(
        spread_grad, normed, (((0,), (0,)), ((), ())), preferred_element_type=jnp.float32
    )
    adapter_part = jnp.dot(spread_grad, down_flat, preferred_element_type=jnp.float32)
    flipped = lax.psum_scatter(
        lax.dot_general(
            weight, grad_out, (((1,), (1,)), ((), ())), preferred_element_type=jnp.float32
        ).astype(jnp.bfloat16),
        "dp",
        scatter_dimension=0,
        tiled=True,
    ).astype(jnp.float32)
    grad_normed = flipped.T + adapter_part
    values = inputs.astype(jnp.float32)
    gain_f = gain_row.astype(jnp.float32)
    weighted = values * gain_f[None, :] * grad_normed
    norm_stat = lax.psum(jnp.sum(weighted, axis=1), "dp") / width
    cubed = inverse * inverse * inverse
    grad_in = (
        grad_out.astype(jnp.float32)
        + inverse[:, None] * gain_f[None, :] * grad_normed
        - values * cubed[:, None] * norm_stat[:, None]
    )
    return (grad_in.astype(jnp.bfloat16), grad_down, grad_up)


def keep_slot(store, value, slot_index, active):
    return jnp.where(active, store.at[slot_index].set(value), store)


def on_device(
    tokens_in, cotangent, base_weight, norm_gain, adapter_a, adapter_b, seg_ids, live_counts
):
    section_count = lax.axis_size("section")
    section_index = lax.axis_index("section")
    micro_count, row_count, col_count = tokens_in.shape
    adapter_count = adapter_a.shape[1]
    rank = adapter_a.shape[2]
    weight = base_weight[0]
    gain_row = norm_gain[0]
    down_flat = adapter_a[0].reshape(adapter_count * rank, col_count)
    up_flat = adapter_b[0].reshape(adapter_count * rank, col_count)
    tables = [
        segment_tables(seg_ids[slot], live_counts[slot], adapter_count)
        for slot in range(micro_count)
    ]
    members = jnp.stack([table[0] for table in tables])
    lives = jnp.stack([table[1] for table in tables])
    saved_inputs = jnp.zeros((micro_count, row_count, col_count), jnp.bfloat16)
    saved_normed = jnp.zeros((micro_count, row_count, col_count), jnp.bfloat16)
    saved_down = jnp.zeros((micro_count, row_count, rank), jnp.bfloat16)
    saved_inverse = jnp.zeros((micro_count, row_count), jnp.float32)
    saved_results = jnp.zeros((micro_count, row_count, col_count), jnp.bfloat16)
    incoming = jnp.zeros((row_count, col_count), jnp.bfloat16)
    for moment in range(micro_count + section_count - 1):
        position = moment - section_index
        active = (position >= 0) & (position < micro_count)
        slot_index = jnp.clip(position, 0, micro_count - 1)
        fresh = lax.dynamic_index_in_dim(tokens_in, slot_index, 0, keepdims=False)
        inputs = jnp.where(section_index == 0, fresh, incoming)
        member = lax.dynamic_index_in_dim(members, slot_index, 0, keepdims=False)
        result, normed, down_proj, inverse = forward_layer(
            inputs, gain_row, weight, down_flat, up_flat, member, rank
        )
        saved_inputs = keep_slot(saved_inputs, inputs, slot_index, active)
        saved_normed = keep_slot(saved_normed, normed, slot_index, active)
        saved_down = keep_slot(saved_down, down_proj, slot_index, active)
        saved_inverse = keep_slot(saved_inverse, inverse, slot_index, active)
        saved_results = keep_slot(saved_results, result, slot_index, active)
        incoming = from_behind(result, "section", 1)
    total_down = jnp.zeros((adapter_count * rank, col_count), jnp.float32)
    total_up = jnp.zeros((adapter_count * rank, col_count), jnp.float32)
    incoming = jnp.zeros((row_count, col_count), jnp.bfloat16)
    for moment in range(micro_count + section_count - 1):
        position = moment - (section_count - 1 - section_index)
        active = (position >= 0) & (position < micro_count)
        slot_index = jnp.clip(position, 0, micro_count - 1)
        target = lax.dynamic_index_in_dim(cotangent, slot_index, 0, keepdims=False)
        live_rows = lax.dynamic_index_in_dim(lives, slot_index, 0, keepdims=False)
        masked = jnp.where(live_rows[:, None], target, jnp.zeros_like(target))
        grad_out = jnp.where(section_index == section_count - 1, masked, incoming)
        member = lax.dynamic_index_in_dim(members, slot_index, 0, keepdims=False)
        grad_in, grad_down, grad_up = backward_layer(
            grad_out,
            lax.dynamic_index_in_dim(saved_inputs, slot_index, 0, keepdims=False),
            lax.dynamic_index_in_dim(saved_normed, slot_index, 0, keepdims=False),
            lax.dynamic_index_in_dim(saved_down, slot_index, 0, keepdims=False),
            lax.dynamic_index_in_dim(saved_inverse, slot_index, 0, keepdims=False),
            gain_row,
            weight,
            down_flat,
            up_flat,
            member,
            rank,
        )
        total_down = total_down + jnp.where(active, grad_down, jnp.zeros_like(grad_down))
        total_up = total_up + jnp.where(active, grad_up, jnp.zeros_like(grad_up))
        incoming = from_behind(grad_in, "section", -1)
    section_out = saved_results[None]
    grad_a = total_down.reshape(1, adapter_count, rank, col_count)
    grad_b = total_up.reshape(1, adapter_count, rank, col_count)
    return (section_out, grad_a, grad_b)


def solution(mesh):
    in_specs = (
        P(None, None, "dp"),
        P(None, None, "dp"),
        P("section", None, "dp"),
        P("section", "dp"),
        P("section", None, None, "dp"),
        P("section", None, None, "dp"),
        P(),
        P(),
    )
    out_specs = (
        P("section", None, None, "dp"),
        P("section", None, None, "dp"),
        P("section", None, None, "dp"),
    )
    return jax.shard_map(
        on_device, mesh=mesh, in_specs=in_specs, out_specs=out_specs, check_vma=False
    )
```

profile of v0, /device:TPU:0, one launch (start us, length us, event | category | flops | bytes accessed | tf_op | source)
XLA Modules:
  0.0 1729.7 jit_solution(810938081733974441)
XLA Ops:
  9.1 67.4 %psum.133 = f32[192]{0:T(256)S(1)} all-reduce(f32[192]{0:T(256)S(1)} %fusion.99), channel_id=1, replica_groups=mesh['section'=4,'dp'=32] {'dp'}, use_global_device_ids=true, to_apply=%region_2.0 | all-reduce | flops 192 | bytes 1536 | tf_op jit(solution)/shard_map/psum | solution.py:42
  85.1 124.1 %psum.134 = bf16[192,32]{0,1:T(8,128)(2,1)S(1)} all-reduce(f32[192,32]{0,1:T(8,128)S(1)} %multiply_reduce_fusion.9), channel_id=1, replica_groups=mesh['section'=4,'dp'=32] {'dp'}, use_global_device_ids=true, to_apply=%region_3.0 | all-reduce | flops 6144 | bytes 36864 | tf_op jit(solution)/shard_map/psum | solution.py:53
  224.8 62.7 %psum.135 = f32[192]{0:T(256)S(1)} all-reduce(f32[192]{0:T(256)S(1)} %fusion.124), channel_id=1, replica_groups=mesh['section'=4,'dp'=32] {'dp'}, use_global_device_ids=true, to_apply=%region_6.0 | all-reduce | flops 192 | bytes 1536 | tf_op jit(solution)/shard_map/psum | solution.py:42
  291.1 124.0 %psum.136 = bf16[192,32]{0,1:T(8,128)(2,1)S(1)} all-reduce(f32[192,32]{0,1:T(8,128)S(1)} %multiply_reduce_fusion.8), channel_id=1, replica_groups=mesh['section'=4,'dp'=32] {'dp'}, use_global_device_ids=true, to_apply=%region_7.0 | all-reduce | flops 6144 | bytes 36864 | tf_op jit(solution)/shard_map/psum | solution.py:53
  418.0 5.5 fusion.136
  431.0 62.7 %psum.137 = f32[192]{0:T(256)S(1)} all-reduce(f32[192]{0:T(256)S(1)} %fusion.127), channel_id=1, replica_groups=mesh['section'=4,'dp'=32] {'dp'}, use_global_device_ids=true, to_apply=%region_10.11 | all-reduce | flops 192 | bytes 1536 | tf_op jit(solution)/shard_map/psum | solution.py:42
  497.3 124.0 %psum.138 = bf16[192,32]{0,1:T(8,128)(2,1)S(1)} all-reduce(f32[192,32]{0,1:T(8,128)S(1)} %multiply_reduce_fusion.7), channel_id=1, replica_groups=mesh['section'=4,'dp'=32] {'dp'}, use_global_device_ids=true, to_apply=%region_11.12 | all-reduce | flops 6144 | bytes 36864 | tf_op jit(solution)/shard_map/psum | solution.py:53
  624.2 5.5 fusion.137
  637.2 62.7 %psum.139 = f32[192]{0:T(256)S(1)} all-reduce(f32[192]{0:T(256)S(1)} %fusion.130), channel_id=1, replica_groups=mesh['section'=4,'dp'=32] {'dp'}, use_global_device_ids=true, to_apply=%region_14.15 | all-reduce | flops 192 | bytes 1536 | tf_op jit(solution)/shard_map/psum | solution.py:42
  702.9 5.4 fusion
  713.9 124.3 %all-reduce.2 = (bf16[192,32]{0,1:T(8,128)(2,1)S(1)}, f32[192,32]{0,1:T(8,128)S(1)}) all-reduce(f32[192,32]{0,1:T(8,128)S(1)} %multiply_reduce_fusion.6, f32[192,32]{0,1:T(8,128)S(1)} %multiply_reduce_fusion.4), channel_id=1, replica_groups=mesh['section'=4,'dp'=32] {'dp'}, use_global_device_ids=true, to_apply=%region_15.16 | all-reduce | flops 12288 | bytes 86016 | tf_op jit(solution)/shard_map/psum | solution.py:53
  841.4 5.6 fusion.138
  858.3 63.2 %all-reduce.1 = (f32[192]{0:T(256)}, f32[192]{0:T(256)}) all-reduce(f32[192]{0:T(256)S(1)} %fusion.133, f32[192]{0:T(256)S(1)} %get-tuple-element.381), channel_id=1, replica_groups=mesh['section'=4,'dp'=32] {'dp'}, use_global_device_ids=true, to_apply=%region_18.19 | all-reduce | flops 384 | bytes 3072 | tf_op jit(solution)/shard_map/psum | solution.py:42
  927.2 5.9 collective-permute-done.4
  944.2 124.0 %psum.145 = f32[192,32]{0,1:T(8,128)} all-reduce(f32[192,32]{0,1:T(8,128)} %multiply_reduce_fusion.3), channel_id=1, replica_groups=mesh['section'=4,'dp'=32] {'dp'}, use_global_device_ids=true, to_apply=%region_37.38 | all-reduce | flops 6144 | bytes 49152 | tf_op jit(solution)/shard_map/psum | solution.py:72
  1073.9 63.3 %psum.146 = f32[192]{0:T(256)} all-reduce(f32[192]{0:T(256)} %get-tuple-element.383), channel_id=1, replica_groups=mesh['section'=4,'dp'=32] {'dp'}, use_global_device_ids=true, to_apply=%region_40.41 | all-reduce | flops 192 | bytes 1536 | tf_op jit(solution)/shard_map/psum | solution.py:91
  1147.3 5.4 fusion.2
  1155.6 124.0 %psum.147 = f32[192,32]{0,1:T(8,128)} all-reduce(f32[192,32]{0,1:T(8,128)} %multiply_reduce_fusion.2), channel_id=1, replica_groups=mesh['section'=4,'dp'=32] {'dp'}, use_global_device_ids=true, to_apply=%region_41.42 | all-reduce | flops 6144 | bytes 49152 | tf_op jit(solution)/shard_map/psum | solution.py:72
  1285.4 63.2 %psum.148 = f32[192]{0:T(256)} all-reduce(f32[192]{0:T(256)} %get-tuple-element.385), channel_id=1, replica_groups=mesh['section'=4,'dp'=32] {'dp'}, use_global_device_ids=true, to_apply=%region_44.45 | all-reduce | flops 192 | bytes 1536 | tf_op jit(solution)/shard_map/psum | solution.py:91
  1358.7 5.4 fusion.3
  1382.0 124.2 %psum.149 = f32[192,32]{0,1:T(8,128)S(1)} all-reduce(f32[192,32]{0,1:T(8,128)S(1)} %multiply_reduce_fusion.1), channel_id=1, replica_groups=mesh['section'=4,'dp'=32] {'dp'}, use_global_device_ids=true, to_apply=%region_45.46 | all-reduce | flops 6144 | bytes 49152 | tf_op jit(solution)/shard_map/psum | solution.py:72
  1509.4 62.7 %psum.150 = f32[192]{0:T(256)S(1)} all-reduce(f32[192]{0:T(256)S(1)} %get-tuple-element.387), channel_id=1, replica_groups=mesh['section'=4,'dp'=32] {'dp'}, use_global_device_ids=true, to_apply=%region_48.49 | all-reduce | flops 192 | bytes 1536 | tf_op jit(solution)/shard_map/psum | solution.py:91
  1581.4 123.9 %all-reduce = (bf16[192,32]{0,1:T(8,128)(2,1)S(1)}, f32[192,32]{0,1:T(8,128)S(1)}) all-reduce(f32[192,32]{0,1:T(8,128)S(1)} %copy-done.50, f32[192,32]{0,1:T(8,128)S(1)} %multiply_reduce_fusion), channel_id=1, replica_groups=mesh['section'=4,'dp'=32] {'dp'}, use_global_device_ids=true, to_apply=%region_19.20 | all-reduce | flops 12288 | bytes 86016 | tf_op jit(solution)/shard_map/psum | solution.py:53
  1717.3 5.5 fusion.84
  (308 shorter events, 169.9 us)
Async XLA Ops:
  7.2 208.7 %copy-start = (bf16[1,64,32,256]{3,2,1,0:T(8,128)(2,1)S(1)}, bf16[1,64,32,256]{3,2,1,0:T(8,128)(2,1)}, u32[]{:S(2)}) copy-start(bf16[1,64,32,256]{3,2,1,0:T(8,128)(2,1)} %param.63) | copy-start | bytes 3145732
  7.2 202.6 %copy-start.66 = (s32[3]{0:T(128)S(1)}, s32[3]{0:T(128)}, u32[]{:S(2)}) copy-start(s32[3]{0:T(128)} %constant.644.clone.1) | copy-start | bytes 40
  7.2 204.5 %all-gather.6.cloned.1.call-start = ((), (), s32[]{:S(2)}) async-start(), calls=%async_computation.4 | async-start | bytes 3244032 | tf_op jit(solution)/shard_map/all_gather | solution.py:48
  8.0 202.6 %copy-start.5 = (bf16[2,192,256]{2,1,0:T(8,128)(2,1)S(1)}, bf16[2,192,256]{2,1,0:T(8,128)(2,1)}, u32[]{:S(2)}) copy-start(bf16[2,192,256]{2,1,0:T(8,128)(2,1)} %param.58) | copy-start | bytes 589828
  80.8 337.2 %all-gather.8.cloned.1.call-start = ((), (), s32[]{:S(2)}) async-start(), calls=%async_computation.5 | async-start | bytes 3244032 | tf_op jit(solution)/shard_map/all_gather | solution.py:48
  81.6 127.6 %copy-start.34 = (f32[1,192,64]{1,2,0:T(8,128)}, f32[1,192,64]{1,2,0:T(8,128)S(1)}, u32[]{:S(2)}) copy-start(f32[1,192,64]{1,2,0:T(8,128)S(1)} %get-tuple-element.391) | copy-start | bytes 147460
  217.2 6.0 collective-permute-start
  224.6 190.5 %copy-start.24 = (bf16[192,256]{1,0:T(8,128)(2,1)}, bf16[192,256]{1,0:T(8,128)(2,1)S(1)}, u32[]{:S(2)}) copy-start(bf16[192,256]{1,0:T(8,128)(2,1)S(1)} %get-tuple-element.341) | copy-start | bytes 294916
  288.9 335.3 %all-gather.10.cloned.1.call-start = ((), (), s32[]{:S(2)}) async-start(), calls=%async_computation.6 | async-start | bytes 3244032 | tf_op jit(solution)/shard_map/all_gather | solution.py:48
  423.6 6.7 collective-permute-start.1
  430.8 190.4 %copy-start.25 = (bf16[192,256]{1,0:T(8,128)(2,1)}, bf16[192,256]{1,0:T(8,128)(2,1)S(1)}, u32[]{:S(2)}) copy-start(bf16[192,256]{1,0:T(8,128)(2,1)S(1)} %get-tuple-element.339) | copy-start | bytes 294916
  495.0 346.4 %all-gather.12.cloned.1.call-start = ((), (), s32[]{:S(2)}) async-start(), calls=%async_computation.7 | async-start | bytes 3244032 | tf_op jit(solution)/shard_map/all_gather | solution.py:48
  629.6 6.7 collective-permute-start.2
  701.4 154.9 %reduce-scatter.5.cloned.1.call-start = ((), (), s32[]{:S(2)}) async-start(), calls=%async_computation.9 | async-start | bytes 3244032 | tf_op jit(solution)/shard_map/reduce_scatter | solution.py:79
  708.4 362.6 %reduce-scatter.7.cloned.1.call-start = ((), (), s32[]{:S(2)}) async-start(), calls=%async_computation.10 | async-start | bytes 3244032 | tf_op jit(solution)/shard_map/reduce_scatter | solution.py:79
  847.0 6.8 collective-permute-start.3
  925.9 7.2 collective-permute-start.4
  940.1 342.4 %reduce-scatter.9.cloned.1.call-start = ((), (), s32[]{:S(2)}) async-start(), calls=%async_computation.11 | async-start | bytes 3244032 | tf_op jit(solution)/shard_map/reduce_scatter | solution.py:79
  1139.1 6.5 collective-permute-start.5
  1152.7 354.7 %reduce-scatter.11.cloned.1.call-start = ((), (), s32[]{:S(2)}) async-start(), calls=%async_computation.12 | async-start | bytes 3244032 | tf_op jit(solution)/shard_map/reduce_scatter | solution.py:79
  1350.5 6.6 collective-permute-start.6
  1364.1 353.2 %all-gather.14.cloned.1.call-start = ((), (), s32[]{:S(2)}) async-start(), calls=%async_computation.8 | async-start | bytes 3244032 | tf_op jit(solution)/shard_map/all_gather | solution.py:48
  1573.3 6.6 collective-permute-start.7
  1578.4 127.8 %copy-start.41 = (f32[192,64]{0,1:T(8,128)S(1)}, f32[192,64]{0,1:T(8,128)}, u32[]{:S(2)}) copy-start(f32[192,64]{0,1:T(8,128)} %get-tuple-element.348) | copy-start | bytes 147460
  (61 other events, 1450.0 us)
Sparse Core Ops, SparseCore 0:
  80.9 44.0 all-gather.5
  289.0 44.4 all-gather.7
  495.1 44.3 all-gather.9
  701.5 44.2 all-gather.11
  749.3 79.8 reduce-scatter.4
  940.2 76.8 reduce-scatter.6
  1152.9 76.8 reduce-scatter.8
  1364.3 76.9 reduce-scatter.10
  1443.4 46.1 all-gather.13
where the time goes:
time: 1740 us; the launch traced here: 1730 us
  blocking collectives  1500 us (86%)
  matrix products  96.1 us (6%)
  other arithmetic  57.2 us (3%)
  starting transfers between devices  24 us (1%)
  waiting for transfers between devices  23.7 us (1%)
    psum x5, blocking collectives, forward_layer(): lax.psum(select_rank(down_parts, member, rank), 'dp').astype(jnp.bfloat16)  620 us
    psum x3, blocking collectives, backward_layer(): summed_parts = lax.psum(select_rank(up_parts, member, rank), 'dp')  372 us
    psum x5, blocking collectives, forward_layer(): squares = lax.psum(jnp.sum(values * values, axis=1), 'dp')  319 us
    psum x3, blocking collectives, backward_layer(): norm_stat = lax.psum(jnp.sum(weighted, axis=1), 'dp') / width  189 us
  transfers between devices with their start and end apart: 17, of which 8 were waited for; matrix products, arithmetic and copies ran while one was open for 5% of the time, Pallas kernels for 0%

commit v1 on v0

v1 whole, which is shorter than its diff:
```python
import jax
import jax.numpy as jnp
from jax import lax
from jax.sharding import PartitionSpec as P

EPSILON = 1e-06
SCALING = 2.0
XS, YS, CS = 4, 4, 2
BF = jnp.bfloat16
F32 = jnp.float32


def place(x, y, c):
    return (x * YS + y) * CS + c


ALONG_X = [[place(x, y, c) for x in range(XS)] for y in range(YS) for c in range(CS)]
ALONG_Y = [[place(x, y, c) for y in range(YS)] for x in range(XS) for c in range(CS)]
ALONG_XY = [[place(x, y, c) for x in range(XS) for y in range(YS)] for c in range(CS)]
SIBLING = [(i, i ^ 1) for i in range(XS * YS * CS)]


def exchange(chunks, groups):
    return lax.all_to_all(chunks, "dp", 0, 0, axis_index_groups=groups)


def spread_out(block, groups):
    return exchange(jnp.broadcast_to(block[None], (4,) + block.shape), groups)


def swap_cores(block):
    return lax.ppermute(block, "dp", SIBLING)


def split_pair(row):
    high = row.astype(BF)
    low = (row - high.astype(F32)).astype(BF)
    return high, low


def pack(main, ranks, row):
    high, low = split_pair(row)
    filler = jnp.zeros((14, row.shape[-1]), BF)
    return jnp.concatenate([main.astype(BF), ranks.astype(BF), high, low, filler], axis=0)


def extras(chunks, width):
    rest = chunks[..., width:, :].astype(F32)
    rank = rest.shape[-2] - 16
    return rest[..., :rank, :], rest[..., rank : rank + 1, :] + rest[..., rank + 1 : rank + 2, :]


def tables_of(seg_ids, live_counts, adapters):
    micro, rows = seg_ids.shape
    labels = jnp.arange(adapters, dtype=jnp.int32)
    member = (seg_ids[:, None, :] == labels[None, :, None]).astype(jnp.int32)
    counts = jnp.sum(member, axis=2)
    before = (labels[:, None] < labels[None, :]).astype(jnp.int32)
    starts = jnp.sum(counts[:, :, None] * before[None], axis=1)
    row_start = jnp.sum(member * starts[:, :, None], axis=1)
    row_limit = jnp.sum(member * jnp.minimum(live_counts, counts)[:, :, None], axis=1)
    live = jnp.arange(rows, dtype=jnp.int32)[None] - row_start < row_limit
    whole = member.astype(F32).transpose(1, 0, 2).reshape(adapters, micro * rows)
    return whole, live.reshape(micro * rows)


def select_rank(parts, member):
    shaped = parts.reshape(member.shape[0], -1, parts.shape[-1])
    return jnp.sum(shaped * member[:, None, :], axis=0)


def spread_rank(values, member):
    joined = member[:, None, :] * values.astype(F32)[None]
    return joined.reshape(-1, values.shape[-1]).astype(BF)


def dot(left, right, dims):
    return lax.dot_general(left, right, (dims, ((), ())), preferred_element_type=F32)


def on_device(
    tokens_in, cotangent, base_weight, norm_gain, adapter_a, adapter_b, seg_ids, live_counts
):
    section = lax.axis_index("section")
    core = lax.axis_index("dp") % CS
    micro, rows, cols = tokens_in.shape
    total = micro * rows
    adapters, rank = adapter_a.shape[1:3]
    width = base_weight.shape[1]
    gain = norm_gain[0].astype(F32)[:, None]
    a_flat = adapter_a[0].reshape(adapters * rank, cols)
    b_flat = adapter_b[0].reshape(adapters * rank, cols)
    member, live = tables_of(seg_ids, live_counts, adapters)
    block = exchange(base_weight[0].reshape(XS, width // XS, cols), ALONG_X)
    block = block.reshape(XS, YS, CS, cols, cols)
    own_rows = lax.dynamic_index_in_dim(block, core, 2, keepdims=False)
    sib_rows = lax.dynamic_index_in_dim(block, 1 - core, 2, keepdims=False)
    tokens = tokens_in.reshape(total, cols).T
    target = jnp.where(live[None, :], cotangent.reshape(total, cols).T, jnp.zeros((), BF))

    def forward(current):
        values = current.astype(F32)
        scaled = (values * gain).astype(BF)
        ranks = select_rank(dot(a_flat, scaled, ((1,), (0,))), member)
        squares = jnp.sum(values * values, axis=0, keepdims=True)
        got = spread_out(pack(scaled, ranks, squares), ALONG_Y)
        other = swap_cores(got)
        partial = dot(own_rows, got[:, :cols], ((1, 2), (0, 1))) + dot(
            sib_rows, other[:, :cols], ((1, 2), (0, 1))
        )
        ranks, squares = extras(got, cols)
        ranks_o, squares_o = extras(other, cols)
        ranks = jnp.sum(ranks + ranks_o, axis=0)
        squares = jnp.sum(squares + squares_o, axis=0)
        send = jnp.stack([pack(partial[i], ranks, squares) for i in range(XS)])
        got = exchange(send, ALONG_X)
        frozen = jnp.sum(got[:, :cols].astype(F32), axis=0)
        ranks, squares = extras(got, cols)
        ranks = jnp.sum(ranks, axis=0)
        inverse = lax.rsqrt(jnp.sum(squares, axis=0) / width + EPSILON)
        down = (ranks * inverse).astype(BF)
        adapter = dot(b_flat, spread_rank(down, member), ((0,), (0,)))
        result = (values + frozen * inverse + SCALING * adapter).astype(BF)
        return result, frozen, ranks, inverse, down

    def backward(grad, values, frozen, down_raw, inverse):
        ranks = select_rank(dot(b_flat, grad, ((1,), (0,))), member)
        stat = jnp.sum(grad.astype(F32) * frozen, axis=0, keepdims=True)
        got = spread_out(pack(grad, ranks, stat), ALONG_X)
        mains = got[:, :cols]
        own = dot(own_rows, mains, ((0, 3), (0, 1)))
        sib = dot(sib_rows, mains, ((0, 3), (0, 1)))
        ranks, stat = extras(got, cols)
        ranks, stat = jnp.sum(ranks, axis=0), jnp.sum(stat, axis=0)
        other = swap_cores(jnp.stack([pack(sib[i], ranks, stat) for i in range(YS)]))
        ranks_o, stat_o = extras(other[0], cols)
        ranks, stat = ranks + ranks_o, stat + stat_o
        both = own + other[:, :cols].astype(F32)
        got = exchange(jnp.stack([pack(both[i], ranks, stat) for i in range(YS)]), ALONG_Y)
        frozen_back = jnp.sum(got[:, :cols].astype(F32), axis=0)
        ranks, stat = extras(got, cols)
        grad_down = (SCALING * jnp.sum(ranks, axis=0)).astype(BF)
        stat = jnp.sum(stat, axis=0) + jnp.sum(
            grad_down.astype(F32) * down_raw, axis=0, keepdims=True
        )
        adapter = dot(a_flat, spread_rank(grad_down, member), ((0,), (0,)))
        normed_grad = frozen_back + adapter
        cubed = inverse * inverse * inverse
        grad_in = (
            grad.astype(F32) + inverse * gain * normed_grad - values * cubed * (stat / width)
        )
        return grad_in.astype(BF)

    current = jnp.where(section == 0, tokens, jnp.zeros_like(tokens))
    for moment in range(4):
        result, frozen, down_raw, inverse, down = forward(current)
        if moment < 3:
            received = lax.ppermute(result, "section", [(i, i + 1) for i in range(3)])
            current = jnp.where(section == moment + 1, received, current)
    values = current.astype(F32)
    grad = jnp.where(section == 3, target, jnp.zeros_like(target))
    for moment in range(3):
        grad_in = backward(grad, values, frozen, down_raw, inverse)
        received = lax.ppermute(grad_in, "section", [(i + 1, i) for i in range(3)])
        grad = jnp.where(section == 2 - moment, received, grad)
    ranks = select_rank(dot(b_flat, grad, ((1,), (0,))), member)
    ranks = ranks + lax.ppermute(ranks, "dp", SIBLING)
    ranks = ranks.astype(BF)
    ranks = exchange(jnp.broadcast_to(ranks[None], (XS * YS,) + ranks.shape), ALONG_XY)
    grad_down = (SCALING * jnp.sum(ranks.astype(F32), axis=0)).astype(BF)
    normed = (values * inverse * gain).astype(BF)
    grad_a = dot(spread_rank(grad_down, member), normed, ((1,), (1,)))
    grad_b = SCALING * dot(spread_rank(down, member), grad, ((1,), (1,)))
    section_out = result.T.reshape(1, micro, rows, cols)
    shape = (1, adapters, rank, cols)
    return section_out, grad_a.reshape(shape), grad_b.reshape(shape)


def solution(mesh):
    in_specs = (
        P(None, None, "dp"),
        P(None, None, "dp"),
        P("section", None, "dp"),
        P("section", "dp"),
        P("section", None, None, "dp"),
        P("section", None, None, "dp"),
        P(),
        P(),
    )
    out_specs = (
        P("section", None, None, "dp"),
        P("section", None, None, "dp"),
        P("section", None, None, "dp"),
    )
    return jax.shard_map(
        on_device, mesh=mesh, in_specs=in_specs, out_specs=out_specs, check_vma=False
    )
```

time: 1740 us -> 645 us (0.37)
  blocking collectives: 1500 us -> 177 us
  local copies, waits for them, and re-layouts: 13.1 us -> 154 us
  waiting for transfers between devices: 23.7 us -> 130 us
    psum x16 -> x0, blocking collectives: 1500 us -> none  [the longest x5 620 us: forward_layer(): lax.psum(select_rank(down_parts, member, rank), 'dp').astype(jnp.bfloat16)]
    all_to_all x0 -> x11, blocking collectives: none -> 177 us  [exchange(): return lax.all_to_all(chunks, 'dp', 0, 0, axis_index_groups=groups)]
    concatenate x0 -> x54, local copies, waits for them, and re-layouts: none -> 98.1 us  [pack(): jnp.concatenate([main.astype(BF), ranks.astype(BF), high, low, filler], a...]
    all_to_all x0 -> x5, waiting for transfers between devices: none -> 90.1 us  [exchange(): return lax.all_to_all(chunks, 'dp', 0, 0, axis_index_groups=groups)]
    dot_general x0 -> x8, local copies, waits for them, and re-layouts: none -> 28.8 us  [dot(): lax.dot_general(left, right, (dims, ((), ())), preferred_element_type=F32)]
    select_n x22 -> x2, other arithmetic: 24.3 us -> 1.06 us  [the longest x1 0.94 us: on_device(): current = jnp.where(section == 0, tokens, jnp.zeros_like(tokens))]
    reduce_sum x10 -> x55, other arithmetic: 2.05 us -> 25.2 us  [the longest x7 17.2 us: select_rank(): return jnp.sum(shaped * member[:, None, :], axis=0)]
    all_to_all x0 -> x5, starting transfers between devices: none -> 20.3 us  [exchange(): return lax.all_to_all(chunks, 'dp', 0, 0, axis_index_groups=groups)]
  transfers between devices with their start and end apart: 17 -> 19, of which waited for: 8 -> 15; matrix products, arithmetic and copies ran while one was open for 5% -> 3% of each run, Pallas kernels for 0% -> 0%
where the time goes in v1:
time: 645 us; the launch traced here: 634 us
  blocking collectives  177 us (27%)
  local copies, waits for them, and re-layouts  154 us (24%)
  waiting for transfers between devices  130 us (20%)
  matrix products  78.7 us (12%)
  other arithmetic  54.6 us (8%)
  starting transfers between devices  36.8 us (6%)
    all_to_all x11, blocking collectives, exchange(): return lax.all_to_all(chunks, 'dp', 0, 0, axis_index_groups=groups)  177 us
    concatenate x54, local copies, waits for them, and re-layouts, pack(): jnp.concatenate([main.astype(BF), ranks.astype(BF), high, low, filler], a...  98.1 us
    all_to_all x5, waiting for transfers between devices, exchange(): return lax.all_to_all(chunks, 'dp', 0, 0, axis_index_groups=groups)  90.1 us
    dot_general x31, matrix products, dot(): lax.dot_general(left, right, (dims, ((), ())), preferred_element_type=F32)  78.7 us
    dot_general x8, local copies, waits for them, and re-layouts, dot(): lax.dot_general(left, right, (dims, ((), ())), preferred_element_type=F32)  28.8 us
    ppermute x3, waiting for transfers between devices, on_device(): received = lax.ppermute(grad_in, 'section', [(i + 1, i) for i in range(3)])  20.7 us
    all_to_all x5, starting transfers between devices, exchange(): return lax.all_to_all(chunks, 'dp', 0, 0, axis_index_groups=groups)  20.3 us
    reduce_sum x7, other arithmetic, select_rank(): return jnp.sum(shaped * member[:, None, :], axis=0)  17.2 us
  transfers between devices with their start and end apart: 19, of which 15 were waited for; matrix products, arithmetic and copies ran while one was open for 3% of the time, Pallas kernels for 0%

profile of v1, /device:TPU:0, one launch (start us, length us, event | category | flops | bytes accessed | tf_op | source)
XLA Modules:
  0.0 633.6 jit_solution(9794639907196384204)
XLA Ops:
  12.9 18.2 %all_to_all.80 = bf16[4,304,384]{2,1,0:T(8,128)(2,1)S(1)} all-to-all(bf16[4,304,384]{2,1,0:T(8,128)(2,1)S(1)} %broadcast_in_dim.26), channel_id=1, replica_groups={{0,2,4,6},{1,3,5,7},{8,10,12,14},{9,11,13,15},{16,18,20,22},{17,19,21,2..., dimensions={0} | all-to-all | bytes 1867776 | tf_op jit(solution)/shard_map/all_to_all | solution.py:24
  31.1 4.9 all-to-all-start
  39.7 44.2 %all-to-all-done = bf16[4,2048,256]{2,1,0:T(8,128)(2,1)} async-done(((bf16[4,2048,256]{2,1,0:T(8,128)(2,1)}), bf16[4,2048,256]{2,1,0:T(8,128)(2,1)}, u32[]{:S(2)}, u32[]{:S(2)}) %all-to-all-start) | async-done | bytes 4194336 | tf_op jit(solution)/shard_map/all_to_all | solution.py:24
  96.4 11.5 %all-to-all-done.2 = bf16[4,304,384]{2,1,0:T(8,128)(2,1)S(1)} async-done(((bf16[4,304,384]{2,1,0:T(8,128)(2,1)}), bf16[4,304,384]{2,1,0:T(8,128)(2,1)S(1)}, u32[]{:S(2)}, u32[]{:S(2)}) %all-to-all-start.2) | async-done | bytes 933920 | tf_op jit(solution)/shard_map/all_to_all | solution.py:24
  131.9 12.9 %all_to_all.81 = bf16[4,304,384]{2,1,0:T(8,128)(2,1)S(1)} all-to-all(bf16[4,304,384]{2,1,0:T(8,128)(2,1)S(1)} %broadcast_in_dim.27), channel_id=1, replica_groups={{0,2,4,6},{1,3,5,7},{8,10,12,14},{9,11,13,15},{16,18,20,22},{17,19,21,2..., dimensions={0} | all-to-all | bytes 1867776 | tf_op jit(solution)/shard_map/all_to_all | solution.py:24
  153.5 4.1 concatenate.149
  162.1 17.2 %all_to_all.82 = bf16[4,304,384]{2,1,0:T(8,128)(2,1)S(1)} all-to-all(bf16[4,304,384]{2,1,0:T(8,128)(2,1)S(1)} %pad_maximum_fusion.1), channel_id=1, replica_groups={{0,8,16,24},{1,9,17,25},{2,10,18,26},{3,11,19,27},{4,12,20,28},{5,13,21..., dimensions={0} | all-to-all | bytes 1867776 | tf_op jit(solution)/shard_map/all_to_all | solution.py:24
  201.1 15.5 %all_to_all.83 = bf16[4,304,384]{2,1,0:T(8,128)(2,1)S(1)} all-to-all(bf16[4,304,384]{2,1,0:T(8,128)(2,1)S(1)} %broadcast_in_dim.28), channel_id=1, replica_groups={{0,2,4,6},{1,3,5,7},{8,10,12,14},{9,11,13,15},{16,18,20,22},{17,19,21,2..., dimensions={0} | all-to-all | bytes 1867776 | tf_op jit(solution)/shard_map/all_to_all | solution.py:24
  230.5 17.2 %all_to_all.84 = bf16[4,304,384]{2,1,0:T(8,128)(2,1)S(1)} all-to-all(bf16[4,304,384]{2,1,0:T(8,128)(2,1)S(1)} %pad_maximum_fusion.2), channel_id=1, replica_groups={{0,8,16,24},{1,9,17,25},{2,10,18,26},{3,11,19,27},{4,12,20,28},{5,13,21..., dimensions={0} | all-to-all | bytes 1867776 | tf_op jit(solution)/shard_map/all_to_all | solution.py:24
  251.6 4.6 collective-permute-start.5
  270.0 15.5 %all_to_all.85 = bf16[4,304,384]{2,1,0:T(8,128)(2,1)S(1)} all-to-all(bf16[4,304,384]{2,1,0:T(8,128)(2,1)S(1)} %broadcast_in_dim.29), channel_id=1, replica_groups={{0,2,4,6},{1,3,5,7},{8,10,12,14},{9,11,13,15},{16,18,20,22},{17,19,21,2..., dimensions={0} | all-to-all | bytes 1867776 | tf_op jit(solution)/shard_map/all_to_all | solution.py:24
  299.8 13.9 %all-to-all-done.8 = bf16[4,304,384]{2,1,0:T(8,128)(2,1)S(1)} async-done(((bf16[4,304,384]{2,1,0:T(8,128)(2,1)}), bf16[4,304,384]{2,1,0:T(8,128)(2,1)S(1)}, u32[]{:S(2)}, u32[]{:S(2)}) %all-to-all-start.8) | async-done | bytes 933920 | tf_op jit(solution)/shard_map/all_to_all | solution.py:24
  319.3 16.4 %all_to_all.86 = bf16[4,304,384]{2,1,0:T(8,128)(2,1)S(1)} all-to-all(bf16[4,304,384]{2,1,0:T(8,128)(2,1)S(1)} %broadcast_in_dim.31), channel_id=1, replica_groups={{0,8,16,24},{1,9,17,25},{2,10,18,26},{3,11,19,27},{4,12,20,28},{5,13,21..., dimensions={0} | all-to-all | bytes 1867776 | tf_op jit(solution)/shard_map/all_to_all | solution.py:24
  374.4 4.2 all-to-all-start.10
  379.6 13.5 %all-to-all-done.10 = bf16[4,304,384]{2,1,0:T(8,128)(2,1)} async-done(((bf16[4,304,384]{2,1,0:T(8,128)(2,1)}), bf16[4,304,384]{2,1,0:T(8,128)(2,1)}, u32[]{:S(2)}, u32[]{:S(2)}) %all-to-all-start.10) | async-done | bytes 933920 | tf_op jit(solution)/shard_map/all_to_all | solution.py:24
  403.3 7.2 %collective-permute-done.8 = bf16[256,384]{0,1:T(8,128)(2,1)S(1)} collective-permute-done((bf16[256,384]{0,1:T(8,128)(2,1)S(1)}, bf16[256,384]{0,1:T(8,128)(2,1)S(1)}, u32[]{:S(2)}, u32[]{:S(2)}) %collective-permute-start.8) | collective-permute-done | bytes 196640 | tf_op jit(solution)/shard_map/ppermute | solution.py:164
  423.0 15.4 %all_to_all.87 = bf16[4,304,384]{2,1,0:T(8,128)(2,1)S(1)} all-to-all(bf16[4,304,384]{2,1,0:T(8,128)(2,1)S(1)} %broadcast_in_dim.32), channel_id=1, replica_groups={{0,8,16,24},{1,9,17,25},{2,10,18,26},{3,11,19,27},{4,12,20,28},{5,13,21..., dimensions={0} | all-to-all | bytes 1867776 | tf_op jit(solution)/shard_map/all_to_all | solution.py:24
  481.2 16.8 %all_to_all.88 = bf16[4,304,384]{2,1,0:T(8,128)(2,1)S(1)} all-to-all(bf16[4,304,384]{2,1,0:T(8,128)(2,1)S(1)} %pad_maximum_fusion.7), channel_id=1, replica_groups={{0,2,4,6},{1,3,5,7},{8,10,12,14},{9,11,13,15},{16,18,20,22},{17,19,21,2..., dimensions={0} | all-to-all | bytes 1867776 | tf_op jit(solution)/shard_map/all_to_all | solution.py:24
  505.9 6.7 %collective-permute-done.10 = bf16[256,384]{0,1:T(8,128)(2,1)S(1)} collective-permute-done((bf16[256,384]{0,1:T(8,128)(2,1)S(1)}, bf16[256,384]{0,1:T(8,128)(2,1)S(1)}, u32[]{:S(2)}, u32[]{:S(2)}) %collective-permute-start.10) | collective-permute-done | bytes 196640 | tf_op jit(solution)/shard_map/ppermute | solution.py:164
  525.6 15.1 %all_to_all.89 = bf16[4,304,384]{2,1,0:T(8,128)(2,1)S(1)} all-to-all(bf16[4,304,384]{2,1,0:T(8,128)(2,1)S(1)} %broadcast_in_dim.33), channel_id=1, replica_groups={{0,8,16,24},{1,9,17,25},{2,10,18,26},{3,11,19,27},{4,12,20,28},{5,13,21..., dimensions={0} | all-to-all | bytes 1867776 | tf_op jit(solution)/shard_map/all_to_all | solution.py:24
  574.1 16.8 %all_to_all.90 = bf16[4,304,384]{2,1,0:T(8,128)(2,1)S(1)} all-to-all(bf16[4,304,384]{2,1,0:T(8,128)(2,1)S(1)} %pad_maximum_fusion.9), channel_id=1, replica_groups={{0,2,4,6},{1,3,5,7},{8,10,12,14},{9,11,13,15},{16,18,20,22},{17,19,21,2..., dimensions={0} | all-to-all | bytes 1867776 | tf_op jit(solution)/shard_map/all_to_all | solution.py:24
  597.6 6.7 %collective-permute-done.12 = bf16[256,384]{0,1:T(8,128)(2,1)S(1)} collective-permute-done((bf16[256,384]{0,1:T(8,128)(2,1)S(1)}, bf16[256,384]{0,1:T(8,128)(2,1)S(1)}, u32[]{:S(2)}, u32[]{:S(2)}) %collective-permute-start.12) | collective-permute-done | bytes 196640 | tf_op jit(solution)/shard_map/ppermute | solution.py:164
  615.4 4.2 all-to-all-start.15
  622.9 7.1 %all-to-all-done.15 = bf16[16,32,384]{2,1,0:T(8,128)(2,1)} async-done(((bf16[16,32,384]{2,1,0:T(8,128)(2,1)}), bf16[16,32,384]{2,1,0:T(8,128)(2,1)}, u32[]{:S(2)}, u32[]{:S(2)}) %all-to-all-start.15) | async-done | bytes 393248 | tf_op jit(solution)/shard_map/all_to_all | solution.py:24
  (374 shorter events, 321.4 us)
Async XLA Ops:
  0.6 109.1 %copy-start = (bf16[1,64,32,256]{3,2,1,0:T(8,128)(2,1)S(1)}, bf16[1,64,32,256]{3,2,1,0:T(8,128)(2,1)}, u32[]{:S(2)}) copy-start(bf16[1,64,32,256]{3,2,1,0:T(8,128)(2,1)} %param.13) | copy-start | bytes 3145732
  1.4 258.8 %copy-start.22 = (f32[1,256]{1,0:T(1,128)}, f32[1,256]{1,0:T(1,128)S(1)}, u32[]{:S(2)}) copy-start(f32[1,256]{1,0:T(1,128)S(1)} %convert_element_type.1480) | copy-start | bytes 3076
  31.1 52.8 %all-to-all-start = ((bf16[4,2048,256]{2,1,0:T(8,128)(2,1)}), bf16[4,2048,256]{2,1,0:T(8,128)(2,1)}, u32[]{:S(2)}, u32[]{:S(2)}) async-start(bf16[4,2048,256]{2,1,0:T(8,128)(2,1)} %bitcast.482), calls=%async_computation | async-start | bytes 8388608 | tf_op jit(solution)/shard_map/all_to_all | solution.py:24
  36.0 2.7 collective-permute-start
  92.3 15.5 %all-to-all-start.2 = ((bf16[4,304,384]{2,1,0:T(8,128)(2,1)}), bf16[4,304,384]{2,1,0:T(8,128)(2,1)S(1)}, u32[]{:S(2)}, u32[]{:S(2)}) async-start(bf16[4,304,384]{2,1,0:T(8,128)(2,1)} %pad_maximum_fusion), calls=%async_computation.2 | async-start | bytes 1867776 | tf_op jit(solution)/shard_map/all_to_all | solution.py:24
  111.8 8.9 %collective-permute-start.1 = (bf16[256,384]{0,1:T(8,128)(2,1)S(1)}, bf16[256,384]{0,1:T(8,128)(2,1)S(1)}, u32[]{:S(2)}, u32[]{:S(2)}) collective-permute-start(bf16[256,384]{0,1:T(8,128)(2,1)S(1)} %fusion.69), channel_id=1, source_target_pairs={{0,32},{32,64},{64,96},{1,33},{33,65},{65,97},{2,34},{34,66},{66,9... | collective-permute-start | bytes 589832 | tf_op jit(solution)/shard_map/ppermute | solution.py:158
  144.8 3.4 collective-permute-start.2
  184.0 7.9 %collective-permute-start.3 = (bf16[256,384]{0,1:T(8,128)(2,1)S(1)}, bf16[256,384]{0,1:T(8,128)(2,1)S(1)}, u32[]{:S(2)}, u32[]{:S(2)}) collective-permute-start(bf16[256,384]{0,1:T(8,128)(2,1)S(1)} %fusion.103), channel_id=1, source_target_pairs={{0,32},{32,64},{64,96},{1,33},{33,65},{65,97},{2,34},{34,66},{66,9... | collective-permute-start | bytes 589832 | tf_op jit(solution)/shard_map/ppermute | solution.py:158
  216.7 2.9 collective-permute-start.4
  251.6 8.4 %collective-permute-start.5 = (bf16[256,384]{0,1:T(8,128)(2,1)S(1)}, bf16[256,384]{0,1:T(8,128)(2,1)S(1)}, u32[]{:S(2)}, u32[]{:S(2)}) collective-permute-start(bf16[256,384]{0,1:T(8,128)(2,1)S(1)} %fusion.107), channel_id=1, source_target_pairs={{0,32},{32,64},{64,96},{1,33},{33,65},{65,97},{2,34},{34,66},{66,9... | collective-permute-start | bytes 589832 | tf_op jit(solution)/shard_map/ppermute | solution.py:158
  285.5 2.9 collective-permute-start.6
  295.4 18.3 %all-to-all-start.8 = ((bf16[4,304,384]{2,1,0:T(8,128)(2,1)}), bf16[4,304,384]{2,1,0:T(8,128)(2,1)S(1)}, u32[]{:S(2)}, u32[]{:S(2)}) async-start(bf16[4,304,384]{2,1,0:T(8,128)(2,1)} %pad_maximum_fusion.3), calls=%async_computation.8 | async-start | bytes 1867776 | tf_op jit(solution)/shard_map/all_to_all | solution.py:24
  353.4 2.6 collective-permute-start.7
  374.4 18.7 %all-to-all-start.10 = ((bf16[4,304,384]{2,1,0:T(8,128)(2,1)}), bf16[4,304,384]{2,1,0:T(8,128)(2,1)}, u32[]{:S(2)}, u32[]{:S(2)}) async-start(bf16[4,304,384]{2,1,0:T(8,128)(2,1)} %pad_maximum_fusion.5), calls=%async_computation.10 | async-start | bytes 1867776 | tf_op jit(solution)/shard_map/all_to_all | solution.py:24
  379.6 20.0 %copy-start.13 = (f32[32,384]{1,0:T(8,128)}, f32[32,384]{1,0:T(8,128)S(1)}, u32[]{:S(2)}) copy-start(f32[32,384]{1,0:T(8,128)S(1)} %slice_reduce_fusion.6) | copy-start | bytes 147460
  401.8 8.8 %collective-permute-start.8 = (bf16[256,384]{0,1:T(8,128)(2,1)S(1)}, bf16[256,384]{0,1:T(8,128)(2,1)S(1)}, u32[]{:S(2)}, u32[]{:S(2)}) collective-permute-start(bf16[256,384]{0,1:T(8,128)(2,1)S(1)} %fusion.97), channel_id=1, source_target_pairs={{32,0},{64,32},{96,64},{33,1},{65,33},{97,65},{34,2},{66,34},{98,6... | collective-permute-start | bytes 589832 | tf_op jit(solution)/shard_map/ppermute | solution.py:164
  458.7 2.6 collective-permute-start.9
  479.8 18.3 %copy-start.14 = (f32[32,384]{1,0:T(8,128)S(1)}, f32[32,384]{1,0:T(8,128)}, u32[]{:S(2)}) copy-start(f32[32,384]{1,0:T(8,128)} %copy-done.13) | copy-start | bytes 147460
  504.6 8.0 %collective-permute-start.10 = (bf16[256,384]{0,1:T(8,128)(2,1)S(1)}, bf16[256,384]{0,1:T(8,128)(2,1)S(1)}, u32[]{:S(2)}, u32[]{:S(2)}) collective-permute-start(bf16[256,384]{0,1:T(8,128)(2,1)S(1)} %fusion.67), channel_id=1, source_target_pairs={{32,0},{64,32},{96,64},{33,1},{65,33},{97,65},{34,2},{66,34},{98,6... | collective-permute-start | bytes 589832 | tf_op jit(solution)/shard_map/ppermute | solution.py:164
  555.7 2.8 collective-permute-start.11
  572.9 18.1 %copy-start.15 = (f32[32,384]{1,0:T(8,128)S(1)}, f32[32,384]{1,0:T(8,128)}, u32[]{:S(2)}) copy-start(f32[32,384]{1,0:T(8,128)} %copy-done.13) | copy-start | bytes 147460
  596.3 8.0 %collective-permute-start.12 = (bf16[256,384]{0,1:T(8,128)(2,1)S(1)}, bf16[256,384]{0,1:T(8,128)(2,1)S(1)}, u32[]{:S(2)}, u32[]{:S(2)}) collective-permute-start(bf16[256,384]{0,1:T(8,128)(2,1)S(1)} %fusion.68), channel_id=1, source_target_pairs={{32,0},{64,32},{96,64},{33,1},{65,33},{97,65},{34,2},{66,34},{98,6... | collective-permute-start | bytes 589832 | tf_op jit(solution)/shard_map/ppermute | solution.py:164
  613.3 1.3 collective-permute-start.13
  615.4 14.6 %all-to-all-start.15 = ((bf16[16,32,384]{2,1,0:T(8,128)(2,1)}), bf16[16,32,384]{2,1,0:T(8,128)(2,1)}, u32[]{:S(2)}, u32[]{:S(2)}) async-start(bf16[16,32,384]{2,1,0:T(8,128)(2,1)} %broadcast_in_dim.34), calls=%async_computation.15 | async-start | bytes 786432 | tf_op jit(solution)/shard_map/all_to_all | solution.py:24
  (22 other events, 84.5 us)

commit v2 on v1

v2 whole, which is shorter than its diff:
```python
import functools

import jax
import jax.numpy as jnp
from jax import lax
from jax.experimental import pallas as pl
from jax.experimental.pallas import tpu as pltpu
from jax.sharding import PartitionSpec as P

EPSILON = 1e-06
SCALING = 2.0
XS, YS, CS = 4, 4, 2
BF = jnp.bfloat16
F32 = jnp.float32
VM = pl.BlockSpec(memory_space=pltpu.VMEM)
SM = pl.BlockSpec(memory_space=pltpu.SMEM)
PARAMS = pltpu.CompilerParams(vmem_limit_bytes=48 << 20)


def place(x, y, c):
    return (x * YS + y) * CS + c


ALONG_X = [[place(x, y, c) for x in range(XS)] for y in range(YS) for c in range(CS)]
ALONG_Y = [[place(x, y, c) for y in range(YS)] for x in range(XS) for c in range(CS)]
ALONG_XY = [[place(x, y, c) for x in range(XS) for y in range(YS)] for c in range(CS)]
SIBLING = [(i, i ^ 1) for i in range(XS * YS * CS)]


def exchange(chunks, groups):
    return lax.all_to_all(chunks, "dp", 0, 0, axis_index_groups=groups)


def swap_cores(block):
    return lax.ppermute(block, "dp", SIBLING)


def tables_of(seg_ids, live_counts, adapters):
    micro, rows = seg_ids.shape
    labels = jnp.arange(adapters, dtype=jnp.int32)
    member = (seg_ids[:, None, :] == labels[None, :, None]).astype(jnp.int32)
    counts = jnp.sum(member, axis=2)
    before = (labels[:, None] < labels[None, :]).astype(jnp.int32)
    starts = jnp.sum(counts[:, :, None] * before[None], axis=1)
    row_start = jnp.sum(member * starts[:, :, None], axis=1)
    row_limit = jnp.sum(member * jnp.minimum(live_counts, counts)[:, :, None], axis=1)
    live = jnp.arange(rows, dtype=jnp.int32)[None] - row_start < row_limit
    whole = member.astype(F32).transpose(1, 0, 2).reshape(adapters, micro * rows)
    return whole, live.reshape(micro * rows)


def dot(left, right, dims=((1,), (0,))):
    return lax.dot_general(left, right, (dims, ((), ())), preferred_element_type=F32)


def tail_of(ranks, row):
    high = row.astype(BF).astype(F32)
    low = row - high
    index = lax.broadcasted_iota(jnp.int32, (16, row.shape[1]), 0)
    tail = jnp.where(index == 0, high, jnp.where(index == 1, low, jnp.zeros_like(high)))
    return jnp.concatenate([ranks, tail], axis=0).astype(BF)


def extras(chunks, cols, rank):
    ranks, row = None, None
    for j in range(chunks.shape[0]):
        part = chunks[j, cols : cols + rank].astype(F32)
        tail = chunks[j, cols + rank :].astype(F32)
        one = tail[0:1] + tail[1:2]
        ranks = part if ranks is None else ranks + part
        row = one if row is None else row + one
    return ranks, row


def select_rank(parts, member_ref, rank):
    total = None
    for a in range(member_ref.shape[0]):
        part = parts[a * rank : (a + 1) * rank] * member_ref[a : a + 1, :]
        total = part if total is None else total + part
    return total


def spread_rank(values, member_ref, store):
    rank = values.shape[0]
    for a in range(member_ref.shape[0]):
        store[a * rank : (a + 1) * rank] = (values * member_ref[a : a + 1, :]).astype(BF)


def pre_forward(flag, received, older, gain, a_flat, member, current, sent):
    cols, rank = received.shape[0], a_flat.shape[0] // member.shape[0]
    fresh = jnp.where(flag[0] > 0, received[...].astype(F32), older[...].astype(F32))
    current[...] = fresh.astype(BF)
    scaled = (fresh * gain[...]).astype(BF)
    ranks = select_rank(dot(a_flat[...], scaled), member, rank)
    tail = tail_of(ranks, jnp.sum(fresh * fresh, axis=0, keepdims=True))
    for j in range(sent.shape[0]):
        sent[j, :cols] = scaled
        sent[j, cols:] = tail


def mid_forward(core, got, other, weight, sent, joined):
    cols, rank = weight.shape[1], got.shape[1] - weight.shape[1] - 16

    @pl.when(pl.program_id(0) == 0)
    def _():
        for y in range(YS):
            mine = pl.multiple_of((y * CS + core[0]) * cols, cols)
            theirs = pl.multiple_of((y * CS + 1 - core[0]) * cols, cols)
            joined[pl.ds(mine, cols)] = got[y, :cols]
            joined[pl.ds(theirs, cols)] = other[y, :cols]

    sent[0, :cols] = dot(weight[0], joined[...]).astype(BF)
    ranks, row = extras(got, cols, rank)
    ranks_o, row_o = extras(other, cols, rank)
    sent[0, cols:] = tail_of(ranks + ranks_o, row + row_o)


def post_forward(
    width, got, current, b_turned, member, result, frozen, down_raw, inverse, down, store
):
    cols, rank = current.shape[0], down.shape[0]
    total = got[0, :cols].astype(F32)
    for j in range(1, XS):
        total = total + got[j, :cols].astype(F32)
    ranks, row = extras(got, cols, rank)
    scale = lax.rsqrt(row / width + EPSILON)
    kept = (ranks * scale).astype(BF)
    spread_rank(kept.astype(F32), member, store)
    adapter = dot(b_turned[...], store[...])
    result[...] = (current[...].astype(F32) + total * scale + SCALING * adapter).astype(BF)
    frozen[...] = total
    down_raw[...] = ranks
    inverse[...] = scale
    down[...] = kept


def pre_backward(flag, received, older, frozen, b_flat, member, grad, sent):
    cols, rank = received.shape[0], b_flat.shape[0] // member.shape[0]
    fresh = jnp.where(flag[0] > 0, received[...].astype(F32), older[...].astype(F32))
    kept = fresh.astype(BF)
    grad[...] = kept
    ranks = select_rank(dot(b_flat[...], kept), member, rank)
    tail = tail_of(ranks, jnp.sum(fresh * frozen[...], axis=0, keepdims=True))
    for j in range(sent.shape[0]):
        sent[j, :cols] = kept
        sent[j, cols:] = tail


def mid_backward(core, got, weight, *rest):
    sent = rest[-1]
    cols, rank = weight.shape[-1], got.shape[1] - weight.shape[-1] - 16
    total = dot(weight[0, 0, 0], got[0, :cols])
    for j in range(1, XS):
        total = total + dot(weight[j, 0, 0], got[j, :cols])
    ranks, row = extras(got, cols, rank)
    if len(rest) > 1:
        other = rest[0]
        total = total + other[0, :cols].astype(F32)
        ranks_o, row_o = extras(other, cols, rank)
        ranks, row = ranks + ranks_o, row + row_o
    sent[0, :cols] = total.astype(BF)
    sent[0, cols:] = tail_of(ranks, row)


def post_backward(
    width, got, grad, current, a_turned, member, down_raw, inverse, gain, grad_in, store
):
    cols, rank = current.shape[0], down_raw.shape[0]
    total = got[0, :cols].astype(F32)
    for j in range(1, YS):
        total = total + got[j, :cols].astype(F32)
    ranks, row = extras(got, cols, rank)
    grad_down = (SCALING * ranks).astype(BF).astype(F32)
    spread_rank(grad_down, member, store)
    normed_grad = total + dot(a_turned[...], store[...])
    stat = (row + jnp.sum(grad_down * down_raw[...], axis=0, keepdims=True)) / width
    scale = inverse[...]
    grad_in[...] = (
        grad[...].astype(F32)
        + scale * gain[...] * normed_grad
        - current[...].astype(F32) * (scale * scale * scale * stat)
    ).astype(BF)


def outer_up(down, grad, member, grad_b, store):
    spread_rank(SCALING * down[...].astype(F32), member, store)
    grad_b[...] = dot(store[...], grad[...], ((1,), (1,)))


def outer_down(got, current, inverse, gain, member, grad_a, store):
    ranks = got[0].astype(F32)
    for j in range(1, got.shape[0]):
        ranks = ranks + got[j].astype(F32)
    grad_down = (SCALING * ranks).astype(BF).astype(F32)
    spread_rank(grad_down, member, store)
    normed = (current[...].astype(F32) * inverse[...] * gain[...]).astype(BF)
    grad_a[...] = dot(store[...], normed, ((1,), (1,)))


def whole_call(body, name, outs, ins, scratch=(), scalars=0):
    return pl.pallas_call(
        body,
        out_shape=[jax.ShapeDtypeStruct(s, d) for s, d in outs],
        in_specs=[SM] * scalars + [VM] * (len(ins) - scalars),
        out_specs=[VM] * len(outs),
        scratch_shapes=list(scratch),
        compiler_params=PARAMS,
        name=name,
    )(*ins)


def on_device(
    tokens_in, cotangent, base_weight, norm_gain, adapter_a, adapter_b, seg_ids, live_counts
):
    section = lax.axis_index("section")
    core = (lax.axis_index("dp") % CS).astype(jnp.int32).reshape(1)
    micro, rows, cols = tokens_in.shape
    total = micro * rows
    adapters, rank = adapter_a.shape[1:3]
    width = base_weight.shape[1]
    tall = cols + rank + 16
    gain = norm_gain[0].astype(F32)[:, None]
    a_flat = adapter_a[0].reshape(adapters * rank, cols)
    b_flat = adapter_b[0].reshape(adapters * rank, cols)
    a_turned, b_turned = a_flat.T, b_flat.T
    member, live = tables_of(seg_ids, live_counts, adapters)
    block = exchange(base_weight[0].reshape(XS, width // XS, cols), ALONG_X)
    turned = block.transpose(0, 2, 1)
    block = block.reshape(XS, YS, CS, cols, cols)
    tokens = tokens_in.reshape(total, cols).T
    target = jnp.where(live[None, :], cotangent.reshape(total, cols).T, jnp.zeros((), BF))
    store = pltpu.VMEM((adapters * rank, total), BF)
    payload = ((XS, tall, total), BF)
    main = ((cols, total), BF)

    def flag_of(at):
        return (section == at).astype(jnp.int32).reshape(1)

    def mid_call(name, got, other=None):
        chosen = (lambda c: c[0]) if other is not None else (lambda c: 1 - c[0])
        specs = [
            pl.BlockSpec((XS, tall, total), lambda i, c: (0, 0, 0)),
            pl.BlockSpec((XS, 1, 1, cols, cols), lambda i, c: (0, i, chosen(c), 0, 0)),
        ]
        ins = [got, block]
        if other is not None:
            specs.append(pl.BlockSpec((1, tall, total), lambda i, c: (i, 0, 0)))
            ins.append(other)
        return pl.pallas_call(
            mid_backward,
            grid_spec=pltpu.PrefetchScalarGridSpec(
                num_scalar_prefetch=1,
                grid=(YS,),
                in_specs=specs,
                out_specs=pl.BlockSpec((1, tall, total), lambda i, c: (i, 0, 0)),
            ),
            out_shape=jax.ShapeDtypeStruct(*payload),
            compiler_params=PARAMS,
            name=name,
        )(core, *ins)

    def forward(flag, received, older):
        current, sent = whole_call(
            pre_forward,
            "pre_forward",
            [main, payload],
            [flag, received, older, gain, a_flat, member],
            scalars=1,
        )
        got = exchange(sent, ALONG_Y)
        other = swap_cores(got)
        sent = pl.pallas_call(
            mid_forward,
            grid_spec=pltpu.PrefetchScalarGridSpec(
                num_scalar_prefetch=1,
                grid=(XS,),
                in_specs=[
                    pl.BlockSpec((YS, tall, total), lambda i, c: (0, 0, 0)),
                    pl.BlockSpec((YS, tall, total), lambda i, c: (0, 0, 0)),
                    pl.BlockSpec((1, cols, width // XS), lambda i, c: (i, 0, 0)),
                ],
                out_specs=pl.BlockSpec((1, tall, total), lambda i, c: (i, 0, 0)),
                scratch_shapes=[pltpu.VMEM((width // XS, total), BF)],
            ),
            out_shape=jax.ShapeDtypeStruct(*payload),
            compiler_params=PARAMS,
            name="mid_forward",
        )(core, got, other, turned)
        got = exchange(sent, ALONG_X)
        outs = whole_call(
            functools.partial(post_forward, width),
            "post_forward",
            [
                main,
                ((cols, total), F32),
                ((rank, total), F32),
                ((1, total), F32),
                ((rank, total), BF),
            ],
            [got, current, b_turned, member],
            scratch=[store],
        )
        return current, outs

    def backward(flag, received, older, frozen, current, down_raw, inverse):
        grad, sent = whole_call(
            pre_backward,
            "pre_backward",
            [main, payload],
            [flag, received, older, frozen, b_flat, member],
            scalars=1,
        )
        got = exchange(sent, ALONG_X)
        other = swap_cores(mid_call("mid_backward_other", got))
        got = exchange(mid_call("mid_backward_own", got, other), ALONG_Y)
        (grad_in,) = whole_call(
            functools.partial(post_backward, width),
            "post_backward",
            [main],
            [got, grad, current, a_turned, member, down_raw, inverse, gain],
            scratch=[store],
        )
        return grad, grad_in

    received, current = tokens, jnp.zeros_like(tokens)
    for moment in range(4):
        current, outs = forward(flag_of(moment), received, current)
        if moment < 3:
            received = lax.ppermute(outs[0], "section", [(i, i + 1) for i in range(3)])
    result, frozen, down_raw, inverse, down = outs
    received, grad = target, jnp.zeros_like(target)
    for moment in range(3):
        grad, grad_in = backward(
            flag_of(3 - moment), received, grad, frozen, current, down_raw, inverse
        )
        received = lax.ppermute(grad_in, "section", [(i + 1, i) for i in range(3)])
    grad, sent = whole_call(
        pre_backward,
        "pre_last",
        [main, ((1, tall, total), BF)],
        [flag_of(0), received, grad, frozen, b_flat, member],
        scalars=1,
    )
    ranks = sent[0, cols : cols + rank].astype(F32)
    ranks = (ranks + lax.ppermute(ranks, "dp", SIBLING)).astype(BF)
    ranks = exchange(jnp.broadcast_to(ranks[None], (XS * YS,) + ranks.shape), ALONG_XY)
    (grad_b,) = whole_call(
        outer_up,
        "outer_up",
        [((adapters * rank, cols), F32)],
        [down, grad, member],
        scratch=[store],
    )
    (grad_a,) = whole_call(
        outer_down,
        "outer_down",
        [((adapters * rank, cols), F32)],
        [ranks, current, inverse, gain, member],
        scratch=[store],
    )
    section_out = result.T.reshape(1, micro, rows, cols)
    shape = (1, adapters, rank, cols)
    return section_out, grad_a.reshape(shape), grad_b.reshape(shape)


def solution(mesh):
    in_specs = (
        P(None, None, "dp"),
        P(None, None, "dp"),
        P("section", None, "dp"),
        P("section", "dp"),
        P("section", None, None, "dp"),
        P("section", None, None, "dp"),
        P(),
        P(),
    )
    out_specs = (
        P("section", None, None, "dp"),
        P("section", None, None, "dp"),
        P("section", None, None, "dp"),
    )
    return jax.shard_map(
        on_device, mesh=mesh, in_specs=in_specs, out_specs=out_specs, check_vma=False
    )
```

time: 645 us -> 449 us (0.70); the launches traced: 634 us -> 447 us
  local copies, waits for them, and re-layouts: 154 us -> 39 us
  matrix products: 78.7 us -> 0 us
  Pallas kernels: 0 us -> 62.5 us
  other arithmetic: 54.6 us -> 2.69 us
  blocking collectives: 177 us -> 141 us
  waiting for transfers between devices: 130 us -> 152 us
  starting transfers between devices: 36.8 us -> 48.5 us
    concatenate x54 -> x0, local copies, waits for them, and re-layouts: 98.1 us -> none  [pack(): jnp.concatenate([main.astype(BF), ranks.astype(BF), high, low, filler], a...]
    dot_general x31 -> x0, matrix products: 78.7 us -> none  [dot(): lax.dot_general(left, right, (dims, ((), ())), preferred_element_type=F32)]
    pallas_call x0 -> x27, Pallas kernels: none -> 62.5 us  [the longest x17 25.9 us: whole_call(): pl.pallas_call(body, out_shape=[jax.ShapeDtypeStruct(s, d) for s, d in ou...]
    all_to_all x11 -> x9, blocking collectives: 177 us -> 141 us  [exchange(): return lax.all_to_all(chunks, 'dp', 0, 0, axis_index_groups=groups)]
    dot_general x8 -> x0, local copies, waits for them, and re-layouts: 28.8 us -> none  [dot(): lax.dot_general(left, right, (dims, ((), ())), preferred_element_type=F32)]
    reduce_sum x52 -> x0, other arithmetic: 24.8 us -> none  [the longest x7 17.2 us: select_rank(): return jnp.sum(shaped * member[:, None, :], axis=0)]
    unnamed x54 -> x68, local copies, waits for them, and re-layouts: 2.97 us -> 19.7 us
    convert_element_type x59 -> x2, other arithmetic: 14 us -> 0.01 us  [the longest x1 0.01 us: on_device(): ranks = (ranks + lax.ppermute(ranks, 'dp', SIBLING)).astype(BF)]
  transfers between devices with their start and end apart: 19 -> 21, of which waited for: 15 -> 21; matrix products, arithmetic and copies ran while one was open for 3% -> 4% of each run, Pallas kernels for 0% -> 0%
where the time goes in v2:
time: 449 us; the launch traced here: 447 us
  waiting for transfers between devices  152 us (34%)
  blocking collectives  141 us (31%)
  Pallas kernels  62.5 us (14%)
  starting transfers between devices  48.5 us (11%)
  local copies, waits for them, and re-layouts  39 us (9%)
    all_to_all x9, blocking collectives, exchange(): return lax.all_to_all(chunks, 'dp', 0, 0, axis_index_groups=groups)  141 us
    all_to_all x7, waiting for transfers between devices, exchange(): return lax.all_to_all(chunks, 'dp', 0, 0, axis_index_groups=groups)  104 us
    all_to_all x7, starting transfers between devices, exchange(): return lax.all_to_all(chunks, 'dp', 0, 0, axis_index_groups=groups)  29.3 us
    pallas_call x17, Pallas kernels, whole_call(): pl.pallas_call(body, out_shape=[jax.ShapeDtypeStruct(s, d) for s, d in ou...  25.9 us
    ppermute x3, waiting for transfers between devices, on_device(): received = lax.ppermute(grad_in, 'section', [(i + 1, i) for i in range(3)])  20.7 us
    pallas_call x4, Pallas kernels, forward(): pl.pallas_call(mid_forward, grid_spec=pltpu.PrefetchScalarGridSpec(num_sc...  20.2 us
    unnamed x68, local copies, waits for them, and re-layouts  19.7 us
    ppermute x7, waiting for transfers between devices, swap_cores(): return lax.ppermute(block, 'dp', SIBLING)  17.3 us
  transfers between devices with their start and end apart: 21, of which 21 were waited for; matrix products, arithmetic and copies ran while one was open for 4% of the time, Pallas kernels for 0%

profile of v2, /device:TPU:0, one launch (start us, length us, event | category | flops | bytes accessed | tf_op | source)
XLA Modules:
  0.0 447.0 jit_solution(5447165577458298024)
XLA Ops:
  10.9 6.3 %copy.44 = bf16[4,2048,256]{1,2,0:T(8,128)(2,1)} copy(bf16[4,2048,256]{2,1,0:T(8,128)(2,1)} %bitcast.51) | data formatting | bytes 8388608 | tf_op jit(solution)/shard_map/reshape;squeeze | solution.py:227
  17.2 7.6 %all-to-all-done.got = bf16[4,304,384]{2,1,0:T(8,128)(2,1)S(1)} async-done(((bf16[4,304,384]{2,1,0:T(8,128)(2,1)}), bf16[4,304,384]{2,1,0:T(8,128)(2,1)S(1)}, u32[]{:S(2)}, u32[]{:S(2)}) %all-to-all-start) | async-done | bytes 933920 | tf_op jit(solution)/shard_map/all_to_all | solution.py:31
  32.2 45.4 %all-to-all-done.1 = bf16[4,2048,256]{1,2,0:T(8,128)(2,1)} async-done(((bf16[4,2048,256]{1,2,0:T(8,128)(2,1)}), bf16[4,2048,256]{1,2,0:T(8,128)(2,1)}, u32[]{:S(2)}, u32[]{:S(2)}) %all-to-all-start.1) | async-done | bytes 4194336 | tf_op jit(solution)/shard_map/all_to_all | solution.py:31
  77.6 5.7 %mid_forward.4 = bf16[4,304,384]{2,1,0:T(8,128)(2,1)} custom-call(s32[1]{0:T(128)} %bitcast.core, bf16[4,304,384]{2,1,0:T(8,128)(2,1)S(1)} %all-to-all-done.got, bf16[4,304,384]{2,1,0:T(8,128)(2,1)S(1)} %collective-permute-done.other, bf16[4,256,2048]{2,1,0:T(8,128)(2,1)} %bitcast.10.weight), custom_call_target="tpu_custom_call" | custom-call | tf_op jit(solution)/shard_map/mid_forward/pallas_call | solution.py:272
  88.3 11.4 %all-to-all-done.2.got = bf16[4,304,384]{2,1,0:T(8,128)(2,1)} async-done(((bf16[4,304,384]{2,1,0:T(8,128)(2,1)}), bf16[4,304,384]{2,1,0:T(8,128)(2,1)}, u32[]{:S(2)}, u32[]{:S(2)}) %all-to-all-start.2) | async-done | bytes 933920 | tf_op jit(solution)/shard_map/all_to_all | solution.py:31
  113.5 12.7 %all_to_all.80.got = bf16[4,304,384]{2,1,0:T(8,128)(2,1)S(1)} all-to-all(bf16[4,304,384]{2,1,0:T(8,128)(2,1)S(1)} %get-tuple-element.30), channel_id=1, replica_groups={{0,2,4,6},{1,3,5,7},{8,10,12,14},{9,11,13,15},{16,18,20,22},{17,19,21,2..., dimensions={0} | all-to-all | bytes 1867776 | tf_op jit(solution)/shard_map/all_to_all | solution.py:31
  133.5 16.8 %all_to_all.81.got = bf16[4,304,384]{2,1,0:T(8,128)(2,1)S(1)} all-to-all(bf16[4,304,384]{2,1,0:T(8,128)(2,1)S(1)} %mid_forward.5), channel_id=1, replica_groups={{0,8,16,24},{1,9,17,25},{2,10,18,26},{3,11,19,27},{4,12,20,28},{5,13,21..., dimensions={0} | all-to-all | bytes 1867776 | tf_op jit(solution)/shard_map/all_to_all | solution.py:31
  152.0 5.1 %collective-permute-start.3 = (bf16[256,384]{1,0:T(8,128)(2,1)}, bf16[256,384]{1,0:T(8,128)(2,1)}, u32[]{:S(2)}, u32[]{:S(2)}) collective-permute-start(bf16[256,384]{1,0:T(8,128)(2,1)} %get-tuple-element.32), channel_id=1, source_target_pairs={{0,32},{32,64},{64,96},{1,33},{33,65},{65,97},{2,34},{34,66},{66,9... | collective-permute-start | bytes 589832 | tf_op jit(solution)/shard_map/ppermute | solution.py:329
  163.0 15.1 %all_to_all.82.got = bf16[4,304,384]{2,1,0:T(8,128)(2,1)S(1)} all-to-all(bf16[4,304,384]{2,1,0:T(8,128)(2,1)S(1)} %get-tuple-element.33), channel_id=1, replica_groups={{0,2,4,6},{1,3,5,7},{8,10,12,14},{9,11,13,15},{16,18,20,22},{17,19,21,2..., dimensions={0} | all-to-all | bytes 1867776 | tf_op jit(solution)/shard_map/all_to_all | solution.py:31
  185.4 16.8 %all_to_all.83.got = bf16[4,304,384]{2,1,0:T(8,128)(2,1)S(1)} all-to-all(bf16[4,304,384]{2,1,0:T(8,128)(2,1)S(1)} %mid_forward.6), channel_id=1, replica_groups={{0,8,16,24},{1,9,17,25},{2,10,18,26},{3,11,19,27},{4,12,20,28},{5,13,21..., dimensions={0} | all-to-all | bytes 1867776 | tf_op jit(solution)/shard_map/all_to_all | solution.py:31
  203.9 5.0 %collective-permute-start.5 = (bf16[256,384]{1,0:T(8,128)(2,1)}, bf16[256,384]{1,0:T(8,128)(2,1)}, u32[]{:S(2)}, u32[]{:S(2)}) collective-permute-start(bf16[256,384]{1,0:T(8,128)(2,1)} %get-tuple-element.35), channel_id=1, source_target_pairs={{0,32},{32,64},{64,96},{1,33},{33,65},{65,97},{2,34},{34,66},{66,9... | collective-permute-start | bytes 589832 | tf_op jit(solution)/shard_map/ppermute | solution.py:329
  215.5 15.1 %all_to_all.84.got = bf16[4,304,384]{2,1,0:T(8,128)(2,1)S(1)} all-to-all(bf16[4,304,384]{2,1,0:T(8,128)(2,1)S(1)} %get-tuple-element.36), channel_id=1, replica_groups={{0,2,4,6},{1,3,5,7},{8,10,12,14},{9,11,13,15},{16,18,20,22},{17,19,21,2..., dimensions={0} | all-to-all | bytes 1867776 | tf_op jit(solution)/shard_map/all_to_all | solution.py:31
  246.9 10.8 %all-to-all-done.8.got = bf16[4,304,384]{2,1,0:T(8,128)(2,1)} async-done(((bf16[4,304,384]{2,1,0:T(8,128)(2,1)}), bf16[4,304,384]{2,1,0:T(8,128)(2,1)}, u32[]{:S(2)}, u32[]{:S(2)}) %all-to-all-start.8) | async-done | bytes 933920 | tf_op jit(solution)/shard_map/all_to_all | solution.py:31
  269.7 6.3 %copy.54 = bf16[4,2048,256]{2,1,0:T(8,128)(2,1)} copy(bf16[4,2048,256]{1,2,0:T(8,128)(2,1)} %all-to-all-done.1) | data formatting | bytes 8388608 | tf_op jit(solution)/shard_map/all_to_all | solution.py:31
  276.0 7.3 %all-to-all-done.9.got = bf16[4,304,384]{2,1,0:T(8,128)(2,1)S(1)} async-done(((bf16[4,304,384]{2,1,0:T(8,128)(2,1)}), bf16[4,304,384]{2,1,0:T(8,128)(2,1)S(1)}, u32[]{:S(2)}, u32[]{:S(2)}) %all-to-all-start.9) | async-done | bytes 933920 | tf_op jit(solution)/shard_map/all_to_all | solution.py:31
  299.4 13.9 %all-to-all-done.10.got = bf16[4,304,384]{2,1,0:T(8,128)(2,1)} async-done(((bf16[4,304,384]{2,1,0:T(8,128)(2,1)}), bf16[4,304,384]{2,1,0:T(8,128)(2,1)}, u32[]{:S(2)}, u32[]{:S(2)}) %all-to-all-start.10) | async-done | bytes 933920 | tf_op jit(solution)/shard_map/all_to_all | solution.py:31
  318.8 7.5 %collective-permute-done.8.received = bf16[256,384]{1,0:T(8,128)(2,1)S(1)} collective-permute-done((bf16[256,384]{1,0:T(8,128)(2,1)S(1)}, bf16[256,384]{1,0:T(8,128)(2,1)S(1)}, u32[]{:S(2)}, u32[]{:S(2)}) %collective-permute-start.8) | collective-permute-done | bytes 196640 | tf_op jit(solution)/shard_map/ppermute | solution.py:336
  329.0 15.4 %all_to_all.85.got = bf16[4,304,384]{2,1,0:T(8,128)(2,1)S(1)} all-to-all(bf16[4,304,384]{2,1,0:T(8,128)(2,1)S(1)} %get-tuple-element.44), channel_id=1, replica_groups={{0,8,16,24},{1,9,17,25},{2,10,18,26},{3,11,19,27},{4,12,20,28},{5,13,21..., dimensions={0} | all-to-all | bytes 1867776 | tf_op jit(solution)/shard_map/all_to_all | solution.py:31
  352.4 17.1 %all_to_all.86.got = bf16[4,304,384]{2,1,0:T(8,128)(2,1)S(1)} all-to-all(bf16[4,304,384]{2,1,0:T(8,128)(2,1)S(1)} %mid_backward_own.4), channel_id=1, replica_groups={{0,2,4,6},{1,3,5,7},{8,10,12,14},{9,11,13,15},{16,18,20,22},{17,19,21,2..., dimensions={0} | all-to-all | bytes 1867776 | tf_op jit(solution)/shard_map/all_to_all | solution.py:31
  371.7 6.7 %collective-permute-done.10.received = bf16[256,384]{1,0:T(8,128)(2,1)S(1)} collective-permute-done((bf16[256,384]{1,0:T(8,128)(2,1)S(1)}, bf16[256,384]{1,0:T(8,128)(2,1)S(1)}, u32[]{:S(2)}, u32[]{:S(2)}) %collective-permute-start.10) | collective-permute-done | bytes 196640 | tf_op jit(solution)/shard_map/ppermute | solution.py:336
  379.1 15.1 %all_to_all.87.got = bf16[4,304,384]{2,1,0:T(8,128)(2,1)S(1)} all-to-all(bf16[4,304,384]{2,1,0:T(8,128)(2,1)S(1)} %get-tuple-element.46), channel_id=1, replica_groups={{0,8,16,24},{1,9,17,25},{2,10,18,26},{3,11,19,27},{4,12,20,28},{5,13,21..., dimensions={0} | all-to-all | bytes 1867776 | tf_op jit(solution)/shard_map/all_to_all | solution.py:31
  402.3 17.0 %all_to_all.88.got = bf16[4,304,384]{2,1,0:T(8,128)(2,1)S(1)} all-to-all(bf16[4,304,384]{2,1,0:T(8,128)(2,1)S(1)} %mid_backward_own.5), channel_id=1, replica_groups={{0,2,4,6},{1,3,5,7},{8,10,12,14},{9,11,13,15},{16,18,20,22},{17,19,21,2..., dimensions={0} | all-to-all | bytes 1867776 | tf_op jit(solution)/shard_map/all_to_all | solution.py:31
  421.6 6.5 %collective-permute-done.12.received = bf16[256,384]{1,0:T(8,128)(2,1)S(1)} collective-permute-done((bf16[256,384]{1,0:T(8,128)(2,1)S(1)}, bf16[256,384]{1,0:T(8,128)(2,1)S(1)}, u32[]{:S(2)}, u32[]{:S(2)}) %collective-permute-start.12) | collective-permute-done | bytes 196640 | tf_op jit(solution)/shard_map/ppermute | solution.py:336
  437.4 7.5 %all-to-all-done.15.got = bf16[16,32,384]{2,1,0:T(8,128)(2,1)S(1)} async-done(((bf16[16,32,384]{2,1,0:T(8,128)(2,1)}), bf16[16,32,384]{2,1,0:T(8,128)(2,1)S(1)}, u32[]{:S(2)}, u32[]{:S(2)}) %all-to-all-start.15) | async-done | bytes 393248 | tf_op jit(solution)/shard_map/all_to_all | solution.py:31
  (145 shorter events, 152.1 us)
Async XLA Ops:
  6.3 18.4 %all-to-all-start = ((bf16[4,304,384]{2,1,0:T(8,128)(2,1)}), bf16[4,304,384]{2,1,0:T(8,128)(2,1)S(1)}, u32[]{:S(2)}, u32[]{:S(2)}) async-start(bf16[4,304,384]{2,1,0:T(8,128)(2,1)} %get-tuple-element.27), calls=%async_computation | async-start | bytes 1867776 | tf_op jit(solution)/shard_map/all_to_all | solution.py:31
  24.8 52.9 %all-to-all-start.1 = ((bf16[4,2048,256]{1,2,0:T(8,128)(2,1)}), bf16[4,2048,256]{1,2,0:T(8,128)(2,1)}, u32[]{:S(2)}, u32[]{:S(2)}) async-start(bf16[4,2048,256]{1,2,0:T(8,128)(2,1)} %copy.44), calls=%async_computation.1 | async-start | bytes 8388608 | tf_op jit(solution)/shard_map/all_to_all | solution.py:31
  29.7 2.6 collective-permute-start
  83.3 16.4 %all-to-all-start.2 = ((bf16[4,304,384]{2,1,0:T(8,128)(2,1)}), bf16[4,304,384]{2,1,0:T(8,128)(2,1)}, u32[]{:S(2)}, u32[]{:S(2)}) async-start(bf16[4,304,384]{2,1,0:T(8,128)(2,1)} %mid_forward.4), calls=%async_computation.2 | async-start | bytes 1867776 | tf_op jit(solution)/shard_map/all_to_all | solution.py:31
  103.5 7.3 %collective-permute-start.1 = (bf16[256,384]{1,0:T(8,128)(2,1)}, bf16[256,384]{1,0:T(8,128)(2,1)}, u32[]{:S(2)}, u32[]{:S(2)}) collective-permute-start(bf16[256,384]{1,0:T(8,128)(2,1)} %get-tuple-element.29), channel_id=1, source_target_pairs={{0,32},{32,64},{64,96},{1,33},{33,65},{65,97},{2,34},{34,66},{66,9... | collective-permute-start | bytes 589832 | tf_op jit(solution)/shard_map/ppermute | solution.py:329
  126.2 2.5 collective-permute-start.2
  152.0 8.3 %collective-permute-start.3 = (bf16[256,384]{1,0:T(8,128)(2,1)}, bf16[256,384]{1,0:T(8,128)(2,1)}, u32[]{:S(2)}, u32[]{:S(2)}) collective-permute-start(bf16[256,384]{1,0:T(8,128)(2,1)} %get-tuple-element.32), channel_id=1, source_target_pairs={{0,32},{32,64},{64,96},{1,33},{33,65},{65,97},{2,34},{34,66},{66,9... | collective-permute-start | bytes 589832 | tf_op jit(solution)/shard_map/ppermute | solution.py:329
  163.0 39.3 %copy-start.25 = (bf16[256,384]{1,0:T(8,128)(2,1)}, bf16[256,384]{1,0:T(8,128)(2,1)S(1)}, u32[]{:S(2)}) copy-start(bf16[256,384]{1,0:T(8,128)(2,1)S(1)} %get-tuple-element.34.current.older) | copy-start | bytes 589828
  178.1 2.5 collective-permute-start.4
  185.4 45.2 %copy-start.32 = (s32[2,192]{1,0:T(2,128)S(1)}, s32[2,192]{1,0:T(2,128)}, u32[]{:S(2)}) copy-start(s32[2,192]{1,0:T(2,128)} %param.14) | copy-start | bytes 4612
  203.9 8.3 %collective-permute-start.5 = (bf16[256,384]{1,0:T(8,128)(2,1)}, bf16[256,384]{1,0:T(8,128)(2,1)}, u32[]{:S(2)}, u32[]{:S(2)}) collective-permute-start(bf16[256,384]{1,0:T(8,128)(2,1)} %get-tuple-element.35), channel_id=1, source_target_pairs={{0,32},{32,64},{64,96},{1,33},{33,65},{65,97},{2,34},{34,66},{66,9... | collective-permute-start | bytes 589832 | tf_op jit(solution)/shard_map/ppermute | solution.py:329
  230.6 2.5 collective-permute-start.6
  238.9 18.7 %all-to-all-start.8 = ((bf16[4,304,384]{2,1,0:T(8,128)(2,1)}), bf16[4,304,384]{2,1,0:T(8,128)(2,1)}, u32[]{:S(2)}, u32[]{:S(2)}) async-start(bf16[4,304,384]{2,1,0:T(8,128)(2,1)} %copy-done.14), calls=%async_computation.8 | async-start | bytes 1867776 | tf_op jit(solution)/shard_map/all_to_all | solution.py:31
  266.2 17.1 %all-to-all-start.9 = ((bf16[4,304,384]{2,1,0:T(8,128)(2,1)}), bf16[4,304,384]{2,1,0:T(8,128)(2,1)S(1)}, u32[]{:S(2)}, u32[]{:S(2)}) async-start(bf16[4,304,384]{2,1,0:T(8,128)(2,1)} %copy-done.18), calls=%async_computation.9 | async-start | bytes 1867776 | tf_op jit(solution)/shard_map/all_to_all | solution.py:31
  287.5 2.6 collective-permute-start.7
  294.5 18.8 %all-to-all-start.10 = ((bf16[4,304,384]{2,1,0:T(8,128)(2,1)}), bf16[4,304,384]{2,1,0:T(8,128)(2,1)}, u32[]{:S(2)}, u32[]{:S(2)}) async-start(bf16[4,304,384]{2,1,0:T(8,128)(2,1)} %copy-done.15), calls=%async_computation.10 | async-start | bytes 1867776 | tf_op jit(solution)/shard_map/all_to_all | solution.py:31
  317.5 8.8 %collective-permute-start.8 = (bf16[256,384]{1,0:T(8,128)(2,1)S(1)}, bf16[256,384]{1,0:T(8,128)(2,1)S(1)}, u32[]{:S(2)}, u32[]{:S(2)}) collective-permute-start(bf16[256,384]{1,0:T(8,128)(2,1)S(1)} %post_backward.3), channel_id=1, source_target_pairs={{32,0},{64,32},{96,64},{33,1},{65,33},{97,65},{34,2},{66,34},{98,6... | collective-permute-start | bytes 589832 | tf_op jit(solution)/shard_map/ppermute | solution.py:336
  346.3 2.6 collective-permute-start.9
  352.4 41.8 %copy-start.2 = (bf16[4,2048,256]{2,1,0:T(8,128)(2,1)S(1)}, bf16[4,2048,256]{2,1,0:T(8,128)(2,1)}, u32[]{:S(2)}) copy-start(bf16[4,2048,256]{2,1,0:T(8,128)(2,1)} %copy.54) | copy-start | bytes 12582916
  370.4 8.0 %collective-permute-start.10 = (bf16[256,384]{1,0:T(8,128)(2,1)S(1)}, bf16[256,384]{1,0:T(8,128)(2,1)S(1)}, u32[]{:S(2)}, u32[]{:S(2)}) collective-permute-start(bf16[256,384]{1,0:T(8,128)(2,1)S(1)} %post_backward.4), channel_id=1, source_target_pairs={{32,0},{64,32},{96,64},{33,1},{65,33},{97,65},{34,2},{66,34},{98,6... | collective-permute-start | bytes 589832 | tf_op jit(solution)/shard_map/ppermute | solution.py:336
  396.2 2.6 collective-permute-start.11
  420.1 8.0 %collective-permute-start.12 = (bf16[256,384]{1,0:T(8,128)(2,1)S(1)}, bf16[256,384]{1,0:T(8,128)(2,1)S(1)}, u32[]{:S(2)}, u32[]{:S(2)}) collective-permute-start(bf16[256,384]{1,0:T(8,128)(2,1)S(1)} %post_backward.5), channel_id=1, source_target_pairs={{32,0},{64,32},{96,64},{33,1},{65,33},{97,65},{34,2},{66,34},{98,6... | collective-permute-start | bytes 589832 | tf_op jit(solution)/shard_map/ppermute | solution.py:336
  428.9 1.3 collective-permute-start.13
  431.0 13.9 %all-to-all-start.15 = ((bf16[16,32,384]{2,1,0:T(8,128)(2,1)}), bf16[16,32,384]{2,1,0:T(8,128)(2,1)S(1)}, u32[]{:S(2)}, u32[]{:S(2)}) async-start(bf16[16,32,384]{2,1,0:T(8,128)(2,1)} %broadcast_in_dim.9), calls=%async_computation.15 | async-start | bytes 786432 | tf_op jit(solution)/shard_map/all_to_all | solution.py:31
  (31 other events, 263.4 us)

commit v3 on v2

--- a/solution.py
+++ b/solution.py
@@ -86,33 +86,62 @@
         store[a * rank : (a + 1) * rank] = (values * member_ref[a : a + 1, :]).astype(BF)
 
 
-def pre_forward(flag, received, older, gain, a_flat, member, current, sent):
-    cols, rank = received.shape[0], a_flat.shape[0] // member.shape[0]
-    fresh = jnp.where(flag[0] > 0, received[...].astype(F32), older[...].astype(F32))
+def fill(flags, sent, main, tail, alt):
+    cols = main.shape[0]
+
+    def write():
+        for j in range(sent.shape[0]):
+            sent[j, :cols] = main
+            sent[j, cols:] = tail
+
+    if alt is None:
+        write()
+        return
+    pl.when(flags[1] == 0)(write)
+
+    @pl.when(flags[1] > 0)
+    def _():
+        sent[...] = alt[...]
+
+
+def pre_forward(flags, received, older, gain, a_flat, member, *rest):
+    alt, current, sent = rest if len(rest) == 3 else (None,) + rest
+    rank = a_flat.shape[0] // member.shape[0]
+    fresh = jnp.where(flags[0] > 0, received[...].astype(F32), older[...].astype(F32))
     current[...] = fresh.astype(BF)
     scaled = (fresh * gain[...]).astype(BF)
     ranks = select_rank(dot(a_flat[...], scaled), member, rank)
     tail = tail_of(ranks, jnp.sum(fresh * fresh, axis=0, keepdims=True))
-    for j in range(sent.shape[0]):
-        sent[j, :cols] = scaled
-        sent[j, cols:] = tail
-
-
-def mid_forward(core, got, other, weight, sent, joined):
+    fill(flags, sent, scaled, tail, alt)
+
+
+def mid_forward(info, got, other, weight, *rest):
+    alt, sent, joined = rest if len(rest) == 3 else (None,) + rest
     cols, rank = weight.shape[1], got.shape[1] - weight.shape[1] - 16
+    core = info[0]
 
     @pl.when(pl.program_id(0) == 0)
     def _():
         for y in range(YS):
-            mine = pl.multiple_of((y * CS + core[0]) * cols, cols)
-            theirs = pl.multiple_of((y * CS + 1 - core[0]) * cols, cols)
+            mine = pl.multiple_of((y * CS + core) * cols, cols)
+            theirs = pl.multiple_of((y * CS + 1 - core) * cols, cols)
             joined[pl.ds(mine, cols)] = got[y, :cols]
             joined[pl.ds(theirs, cols)] = other[y, :cols]
 
-    sent[0, :cols] = dot(weight[0], joined[...]).astype(BF)
-    ranks, row = extras(got, cols, rank)
-    ranks_o, row_o = extras(other, cols, rank)
-    sent[0, cols:] = tail_of(ranks + ranks_o, row + row_o)
+    def write():
+        sent[0, :cols] = dot(weight[0], joined[...]).astype(BF)
+        ranks, row = extras(got, cols, rank)
+        ranks_o, row_o = extras(other, cols, rank)
+        sent[0, cols:] = tail_of(ranks + ranks_o, row + row_o)
+
+    if alt is None:
+        write()
+        return
+    pl.when(info[1] == 0)(write)
+
+    @pl.when(info[1] > 0)
+    def _():
+        sent[...] = alt[...]
 
 
 def post_forward(
@@ -134,45 +163,112 @@
     down[...] = kept
 
 
-def pre_backward(flag, received, older, frozen, b_flat, member, grad, sent):
-    cols, rank = received.shape[0], b_flat.shape[0] // member.shape[0]
-    fresh = jnp.where(flag[0] > 0, received[...].astype(F32), older[...].astype(F32))
+def post_forward_turn(
+    width, got, current, b_turned, member, ahead, result, frozen, down_raw, inverse, down, small, store
+):
+    post_forward(
+        width, got, current, b_turned, member, result, frozen, down_raw, inverse, down, store
+    )
+    values = result[...].astype(F32)
+    squares = jnp.sum(values * values, axis=0, keepdims=True)
+    stat = jnp.sum(values * ahead[...], axis=0, keepdims=True)
+    index = lax.broadcasted_iota(jnp.int32, (16, values.shape[1]), 0)
+    tail = jnp.zeros((16, values.shape[1]), F32)
+    for at, row in ((0, squares), (2, stat)):
+        high = row.astype(BF).astype(F32)
+        tail = jnp.where(index == at, high, jnp.where(index == at + 1, row - high, tail))
+    tail = tail.astype(BF)
+    for j in range(small.shape[0]):
+        small[j] = tail
+
+
+def turn(width, flags, small, result, target, ahead, frozen, b_flat, member, grad, sent):
+    rank = b_flat.shape[0] // member.shape[0]
+    rows = jnp.sum(small[...].astype(F32), axis=0)
+    scale = lax.rsqrt((rows[0:1] + rows[1:2]) / width + EPSILON)
+    stat = (rows[2:3] + rows[3:4]) / width
+    first = target[...].astype(F32)
+    fresh = (
+        first + scale * ahead[...] - result[...].astype(F32) * (scale * scale * scale * stat)
+    )
+    kept = jnp.where(flags[0] > 0, fresh, first).astype(BF)
+    grad[...] = kept
+    ranks = select_rank(dot(b_flat[...], kept), member, rank)
+    row = jnp.sum(kept.astype(F32) * frozen[...], axis=0, keepdims=True)
+    fill(flags, sent, kept, tail_of(ranks, row), None)
+
+
+def pre_backward(flags, received, older, frozen, b_flat, member, *rest):
+    alt, grad, sent = rest if len(rest) == 3 else (None,) + rest
+    rank = b_flat.shape[0] // member.shape[0]
+    fresh = jnp.where(flags[0] > 0, received[...].astype(F32), older[...].astype(F32))
     kept = fresh.astype(BF)
     grad[...] = kept
     ranks = select_rank(dot(b_flat[...], kept), member, rank)
     tail = tail_of(ranks, jnp.sum(fresh * frozen[...], axis=0, keepdims=True))
-    for j in range(sent.shape[0]):
-        sent[j, :cols] = kept
-        sent[j, cols:] = tail
-
-
-def mid_backward(core, got, weight, *rest):
-    sent = rest[-1]
+    fill(flags, sent, kept, tail, alt)
+
+
+def pre_target(target, b_flat, member, sent):
+    rank = b_flat.shape[0] // member.shape[0]
+    kept = target[...]
+    ranks = select_rank(dot(b_flat[...], kept), member, rank)
+    tail = tail_of(ranks, jnp.zeros((1, kept.shape[1]), F32))
+    fill(None, sent, kept, tail, None)
+
+
+def mid_backward_other(info, got, weight, sent):
     cols, rank = weight.shape[-1], got.shape[1] - weight.shape[-1] - 16
     total = dot(weight[0, 0, 0], got[0, :cols])
     for j in range(1, XS):
         total = total + dot(weight[j, 0, 0], got[j, :cols])
-    ranks, row = extras(got, cols, rank)
-    if len(rest) > 1:
-        other = rest[0]
-        total = total + other[0, :cols].astype(F32)
+    sent[0, :cols] = total.astype(BF)
+    sent[0, cols:] = tail_of(*extras(got, cols, rank))
+
+
+def mid_backward_own(info, got, weight, other, *rest):
+    alt, sent = rest if len(rest) == 2 else (None,) + rest
+    cols, rank = weight.shape[-1], got.shape[1] - weight.shape[-1] - 16
+
+    def write():
+        total = other[0, :cols].astype(F32)
+        for j in range(XS):
+            total = total + dot(weight[j, 0, 0], got[j, :cols])
+        sent[0, :cols] = total.astype(BF)
+        ranks, row = extras(got, cols, rank)
         ranks_o, row_o = extras(other, cols, rank)
-        ranks, row = ranks + ranks_o, row + row_o
-    sent[0, :cols] = total.astype(BF)
-    sent[0, cols:] = tail_of(ranks, row)
-
-
-def post_backward(
-    width, got, grad, current, a_turned, member, down_raw, inverse, gain, grad_in, store
-):
-    cols, rank = current.shape[0], down_raw.shape[0]
+        sent[0, cols:] = tail_of(ranks + ranks_o, row + row_o)
+
+    if alt is None:
+        write()
+        return
+    pl.when(info[1] == 0)(write)
+
+    @pl.when(info[1] > 0)
+    def _():
+        sent[...] = alt[...]
+
+
+def collect(got, a_turned, member, rank, store):
+    cols = a_turned.shape[0]
     total = got[0, :cols].astype(F32)
     for j in range(1, YS):
         total = total + got[j, :cols].astype(F32)
     ranks, row = extras(got, cols, rank)
     grad_down = (SCALING * ranks).astype(BF).astype(F32)
     spread_rank(grad_down, member, store)
-    normed_grad = total + dot(a_turned[...], store[...])
+    return total + dot(a_turned[...], store[...]), grad_down, row
+
+
+def post_target(rank, got, a_turned, member, gain, ahead, store):
+    normed_grad, _, _ = collect(got, a_turned, member, rank, store)
+    ahead[...] = gain[...] * normed_grad
+
+
+def post_backward(
+    width, got, grad, current, a_turned, member, down_raw, inverse, gain, grad_in, store
+):
+    normed_grad, grad_down, row = collect(got, a_turned, member, down_raw.shape[0], store)
     stat = (row + jnp.sum(grad_down * down_raw[...], axis=0, keepdims=True)) / width
     scale = inverse[...]
     grad_in[...] = (
@@ -213,7 +309,7 @@
     tokens_in, cotangent, base_weight, norm_gain, adapter_a, adapter_b, seg_ids, live_counts
 ):
     section = lax.axis_index("section")
-    core = (lax.axis_index("dp") % CS).astype(jnp.int32).reshape(1)
+    core = (lax.axis_index("dp") % CS).astype(jnp.int32)
     micro, rows, cols = tokens_in.shape
     total = micro * rows
     adapters, rank = adapter_a.shape[1:3]
@@ -231,119 +327,175 @@
     target = jnp.where(live[None, :], cotangent.reshape(total, cols).T, jnp.zeros((), BF))
     store = pltpu.VMEM((adapters * rank, total), BF)
     payload = ((XS, tall, total), BF)
+    single = ((1, tall, total), BF)
     main = ((cols, total), BF)
-
-    def flag_of(at):
-        return (section == at).astype(jnp.int32).reshape(1)
-
-    def mid_call(name, got, other=None):
-        chosen = (lambda c: c[0]) if other is not None else (lambda c: 1 - c[0])
-        specs = [
-            pl.BlockSpec((XS, tall, total), lambda i, c: (0, 0, 0)),
-            pl.BlockSpec((XS, 1, 1, cols, cols), lambda i, c: (0, i, chosen(c), 0, 0)),
-        ]
-        ins = [got, block]
-        if other is not None:
-            specs.append(pl.BlockSpec((1, tall, total), lambda i, c: (i, 0, 0)))
-            ins.append(other)
+    wide = ((cols, total), F32)
+
+    def is_at(at):
+        return (section == at).astype(jnp.int32)
+
+    never = jnp.zeros((), jnp.int32)
+    last = is_at(3)
+
+    def mid_call(body, name, weight, weight_spec, got, other, alt, scratch=()):
+        block_of = pl.BlockSpec((1, tall, total), lambda i, c: (i, 0, 0))
+        full = pl.BlockSpec((XS, tall, total), lambda i, c: (0, 0, 0))
+        ins, specs = [got], [full]
+        if body is mid_forward:
+            ins, specs = ins + [other, weight], specs + [full, weight_spec]
+        else:
+            ins, specs = ins + [weight], specs + [weight_spec]
+            if other is not None:
+                ins, specs = ins + [other], specs + [block_of]
+        if alt is not None:
+            ins.append(alt)
+            specs.append(pl.BlockSpec((1, tall, total), lambda i, c: (0, 0, 0)))
+        flag = never if alt is None else last
         return pl.pallas_call(
-            mid_backward,
+            body,
             grid_spec=pltpu.PrefetchScalarGridSpec(
                 num_scalar_prefetch=1,
-                grid=(YS,),
+                grid=(4,),
                 in_specs=specs,
-                out_specs=pl.BlockSpec((1, tall, total), lambda i, c: (i, 0, 0)),
+                out_specs=block_of,
+                scratch_shapes=list(scratch),
             ),
             out_shape=jax.ShapeDtypeStruct(*payload),
             compiler_params=PARAMS,
             name=name,
-        )(core, *ins)
-
-    def forward(flag, received, older):
-        current, sent = whole_call(
+        )(jnp.stack([core, flag]), *ins)
+
+    def start_forward(at, received, older, alt=None, out=payload):
+        flags = jnp.stack([is_at(at), never if alt is None else last])
+        extra = [] if alt is None else [alt]
+        return whole_call(
             pre_forward,
             "pre_forward",
-            [main, payload],
-            [flag, received, older, gain, a_flat, member],
+            [main, out],
+            [flags, received, older, gain, a_flat, member] + extra,
             scalars=1,
         )
-        got = exchange(sent, ALONG_Y)
-        other = swap_cores(got)
-        sent = pl.pallas_call(
+
+    def product_forward(got, alt=None):
+        return mid_call(
             mid_forward,
-            grid_spec=pltpu.PrefetchScalarGridSpec(
-                num_scalar_prefetch=1,
-                grid=(XS,),
-                in_specs=[
-                    pl.BlockSpec((YS, tall, total), lambda i, c: (0, 0, 0)),
-                    pl.BlockSpec((YS, tall, total), lambda i, c: (0, 0, 0)),
-                    pl.BlockSpec((1, cols, width // XS), lambda i, c: (i, 0, 0)),
-                ],
-                out_specs=pl.BlockSpec((1, tall, total), lambda i, c: (i, 0, 0)),
-                scratch_shapes=[pltpu.VMEM((width // XS, total), BF)],
-            ),
-            out_shape=jax.ShapeDtypeStruct(*payload),
-            compiler_params=PARAMS,
-            name="mid_forward",
-        )(core, got, other, turned)
-        got = exchange(sent, ALONG_X)
-        outs = whole_call(
-            functools.partial(post_forward, width),
-            "post_forward",
-            [
-                main,
-                ((cols, total), F32),
-                ((rank, total), F32),
-                ((1, total), F32),
-                ((rank, total), BF),
-            ],
-            [got, current, b_turned, member],
-            scratch=[store],
+            "mid_forward",
+            turned,
+            pl.BlockSpec((1, cols, width // XS), lambda i, c: (i, 0, 0)),
+            got,
+            swap_cores(got),
+            alt,
+            [pltpu.VMEM((width // XS, total), BF)],
         )
-        return current, outs
-
-    def backward(flag, received, older, frozen, current, down_raw, inverse):
-        grad, sent = whole_call(
-            pre_backward,
-            "pre_backward",
-            [main, payload],
-            [flag, received, older, frozen, b_flat, member],
-            scalars=1,
+
+    kept_outs = [main, wide, ((rank, total), F32), ((1, total), F32), ((rank, total), BF)]
+
+    def end_forward(got, current, ahead=None):
+        body, outs, ins = post_forward, kept_outs, [got, current, b_turned, member]
+        if ahead is not None:
+            body = post_forward_turn
+            outs, ins = outs + [((XS * YS * CS, 16, total), BF)], ins + [ahead]
+        return whole_call(
+            functools.partial(body, width), "post_forward", outs, ins, scratch=[store]
         )
-        got = exchange(sent, ALONG_X)
-        other = swap_cores(mid_call("mid_backward_other", got))
-        got = exchange(mid_call("mid_backward_own", got, other), ALONG_Y)
-        (grad_in,) = whole_call(
+
+    def product_backward(got, alt=None):
+        shape = (XS, 1, 1, cols, cols)
+        other = mid_call(
+            mid_backward_other,
+            "mid_backward_other",
+            block,
+            pl.BlockSpec(shape, lambda i, c: (0, i, 1 - c[0], 0, 0)),
+            got,
+            None,
+            None,
+        )
+        return mid_call(
+            mid_backward_own,
+            "mid_backward_own",
+            block,
+            pl.BlockSpec(shape, lambda i, c: (0, i, c[0], 0, 0)),
+            got,
+            swap_cores(other),
+            alt,
+        )
+
+    def end_backward(got, grad, current, down_raw, inverse):
+        return whole_call(
             functools.partial(post_backward, width),
             "post_backward",
             [main],
             [got, grad, current, a_turned, member, down_raw, inverse, gain],
             scratch=[store],
+        )[0]
+
+    def start_backward(at, received, older, frozen, alt=None, out=payload):
+        flags = jnp.stack([is_at(at), never if alt is None else last])
+        extra = [] if alt is None else [alt]
+        return whole_call(
+            pre_backward,
+            "pre_backward",
+            [main, out],
+            [flags, received, older, frozen, b_flat, member] + extra,
+            scalars=1,
         )
-        return grad, grad_in
-
-    received, current = tokens, jnp.zeros_like(tokens)
-    for moment in range(4):
-        current, outs = forward(flag_of(moment), received, current)
-        if moment < 3:
-            received = lax.ppermute(outs[0], "section", [(i, i + 1) for i in range(3)])
-    result, frozen, down_raw, inverse, down = outs
-    received, grad = target, jnp.zeros_like(target)
-    for moment in range(3):
-        grad, grad_in = backward(
-            flag_of(3 - moment), received, grad, frozen, current, down_raw, inverse
-        )
-        received = lax.ppermute(grad_in, "section", [(i + 1, i) for i in range(3)])
+
+    def onward(value):
+        return lax.ppermute(value, "section", [(i, i + 1) for i in range(3)])
+
+    def back(value):
+        return lax.ppermute(value, "section", [(i + 1, i) for i in range(3)])
+
+    current, sent = start_forward(0, tokens, jnp.zeros_like(tokens))
+    got = exchange(sent, ALONG_Y)
+    (alt,) = whole_call(pre_target, "pre_target", [single], [target, b_flat, member])
+    got = exchange(product_forward(got, alt), ALONG_X)
+    outs = end_forward(got, current)
+    received = onward(outs[0])
+    last_sums = product_backward(got)
+    current, sent = start_forward(1, received, current)
+    got = exchange(sent, ALONG_Y)
+    got = exchange(product_forward(got), ALONG_X)
+    outs = end_forward(got, current)
+    received = onward(outs[0])
+    current, sent = start_forward(2, received, current, last_sums)
+    got = exchange(sent, ALONG_Y)
+    (ahead,) = whole_call(
+        functools.partial(post_target, rank),
+        "post_target",
+        [wide],
+        [got, a_turned, member, gain],
+        scratch=[store],
+    )
+    ahead = back(ahead)
+    got = exchange(product_forward(got), ALONG_X)
+    result, frozen, down_raw, inverse, down, small = end_forward(got, current, ahead)
+    received = onward(result)
+    small = lax.all_to_all(small, "dp", 0, 0)
     grad, sent = whole_call(
-        pre_backward,
-        "pre_last",
-        [main, ((1, tall, total), BF)],
-        [flag_of(0), received, grad, frozen, b_flat, member],
+        functools.partial(turn, width),
+        "turn",
+        [main, payload],
+        [is_at(2).reshape(1), small, result, target, ahead, frozen, b_flat, member],
         scalars=1,
     )
+    got = exchange(sent, ALONG_X)
+    current, alt = start_forward(3, received, current, out=single)
+    got = exchange(product_backward(got, alt), ALONG_Y)
+    received = back(end_backward(got, grad, current, down_raw, inverse))
+    last_product = product_forward(got)
+    grad, sent = start_backward(1, received, grad, frozen, last_product)
+    got = exchange(sent, ALONG_X)
+    outs = end_forward(got, current)
+    got = exchange(product_backward(got), ALONG_Y)
+    received = back(end_backward(got, grad, current, down_raw, inverse))
+    grad, sent = start_backward(0, received, grad, frozen, out=single)
     ranks = sent[0, cols : cols + rank].astype(F32)
     ranks = (ranks + lax.ppermute(ranks, "dp", SIBLING)).astype(BF)
     ranks = exchange(jnp.broadcast_to(ranks[None], (XS * YS,) + ranks.shape), ALONG_XY)
+    result = jnp.where(last > 0, outs[0], result)
+    inverse = jnp.where(last > 0, outs[3], inverse)
+    down = jnp.where(last > 0, outs[4], down)
     (grad_b,) = whole_call(
         outer_up,
         "outer_up",

time: 449 us -> 384 us (0.86)
  waiting for transfers between devices: 152 us -> 103 us
  blocking collectives: 141 us -> 128 us
  Pallas kernels: 62.5 us -> 72.1 us
  starting transfers between devices: 48.5 us -> 39.3 us
    all_to_all x7 -> x5, waiting for transfers between devices: 104 us -> 72.6 us  [exchange(): return lax.all_to_all(chunks, 'dp', 0, 0, axis_index_groups=groups)]
    all_to_all x9 -> x7, blocking collectives: 141 us -> 113 us  [exchange(): return lax.all_to_all(chunks, 'dp', 0, 0, axis_index_groups=groups)]
    all_to_all x0 -> x1, blocking collectives: none -> 15.2 us  [on_device(): small = lax.all_to_all(small, 'dp', 0, 0)]
    ppermute x7, waiting for transfers between devices: 17.3 us -> 5.53 us  [swap_cores(): return lax.ppermute(block, 'dp', SIBLING)]
    pallas_call x10, Pallas kernels: 36.5 us -> 45.5 us  [mid_call(): pl.pallas_call(body, grid_spec=pltpu.PrefetchScalarGridSpec(num_scalar_pr...]
    all_to_all x7 -> x5, starting transfers between devices: 29.3 us -> 21.6 us  [exchange(): return lax.all_to_all(chunks, 'dp', 0, 0, axis_index_groups=groups)]
    ppermute x6, waiting for transfers between devices: 30 us -> 24.7 us  [the longest x3 17.3 us: back(): return lax.ppermute(value, 'section', [(i + 1, i) for i in range(3)])]
    unnamed x68 -> x82, local copies, waits for them, and re-layouts: 19.7 us -> 17.8 us
  transfers between devices with their start and end apart: 21 -> 19, of which waited for: 21 -> 14; matrix products, arithmetic and copies ran while one was open for 4% -> 4% of each run, Pallas kernels for 0% -> 8%
where the time goes in v3:
time: 384 us; the launch traced here: 382 us
  blocking collectives  128 us (33%)
  waiting for transfers between devices  103 us (27%)
  Pallas kernels  72.1 us (19%)
  starting transfers between devices  39.3 us (10%)
  local copies, waits for them, and re-layouts  36.2 us (9%)
    all_to_all x7, blocking collectives, exchange(): return lax.all_to_all(chunks, 'dp', 0, 0, axis_index_groups=groups)  113 us
    all_to_all x5, waiting for transfers between devices, exchange(): return lax.all_to_all(chunks, 'dp', 0, 0, axis_index_groups=groups)  72.6 us
    pallas_call x10, Pallas kernels, mid_call(): pl.pallas_call(body, grid_spec=pltpu.PrefetchScalarGridSpec(num_scalar_pr...  45.5 us
    pallas_call x17, Pallas kernels, whole_call(): pl.pallas_call(body, out_shape=[jax.ShapeDtypeStruct(s, d) for s, d in ou...  26.7 us
    all_to_all x5, starting transfers between devices, exchange(): return lax.all_to_all(chunks, 'dp', 0, 0, axis_index_groups=groups)  21.6 us
    unnamed x82, local copies, waits for them, and re-layouts  17.8 us
    ppermute x3, waiting for transfers between devices, back(): return lax.ppermute(value, 'section', [(i + 1, i) for i in range(3)])  17.3 us
    all_to_all x1, blocking collectives, on_device(): small = lax.all_to_all(small, 'dp', 0, 0)  15.2 us
  transfers between devices with their start and end apart: 19, of which 14 were waited for; matrix products, arithmetic and copies ran while one was open for 4% of the time, Pallas kernels for 8%

profile of v3, /device:TPU:0, one launch (start us, length us, event | category | flops | bytes accessed | tf_op | source)
XLA Modules:
  0.0 382.2 jit_solution(13249451817959737335)
XLA Ops:
  7.6 4.5 %all-to-all-start = ((bf16[4,304,384]{2,1,0:T(8,128)(2,1)}), bf16[4,304,384]{2,1,0:T(8,128)(2,1)S(1)}, u32[]{:S(2)}, u32[]{:S(2)}) async-start(bf16[4,304,384]{2,1,0:T(8,128)(2,1)} %get-tuple-element.28), calls=%async_computation | async-start | bytes 1867776 | tf_op jit(solution)/shard_map/all_to_all | solution.py:31
  12.2 6.3 %copy.44 = bf16[4,2048,256]{1,2,0:T(8,128)(2,1)} copy(bf16[4,2048,256]{2,1,0:T(8,128)(2,1)} %bitcast.51) | data formatting | bytes 8388608 | tf_op jit(solution)/shard_map/reshape;squeeze | solution.py:323
  18.5 7.6 %all-to-all-done.got = bf16[4,304,384]{2,1,0:T(8,128)(2,1)S(1)} async-done(((bf16[4,304,384]{2,1,0:T(8,128)(2,1)}), bf16[4,304,384]{2,1,0:T(8,128)(2,1)S(1)}, u32[]{:S(2)}, u32[]{:S(2)}) %all-to-all-start) | async-done | bytes 933920 | tf_op jit(solution)/shard_map/all_to_all | solution.py:31
  26.0 4.9 %all-to-all-start.1 = ((bf16[4,2048,256]{1,2,0:T(8,128)(2,1)}), bf16[4,2048,256]{1,2,0:T(8,128)(2,1)}, u32[]{:S(2)}, u32[]{:S(2)}) async-start(bf16[4,2048,256]{1,2,0:T(8,128)(2,1)} %copy.44), calls=%async_computation.1 | async-start | bytes 8388608 | tf_op jit(solution)/shard_map/all_to_all | solution.py:31
  33.5 45.4 %all-to-all-done.1 = bf16[4,2048,256]{1,2,0:T(8,128)(2,1)} async-done(((bf16[4,2048,256]{1,2,0:T(8,128)(2,1)}), bf16[4,2048,256]{1,2,0:T(8,128)(2,1)}, u32[]{:S(2)}, u32[]{:S(2)}) %all-to-all-start.1) | async-done | bytes 4194336 | tf_op jit(solution)/shard_map/all_to_all | solution.py:31
  78.9 6.2 %mid_forward.4 = bf16[4,304,384]{2,1,0:T(8,128)(2,1)} custom-call(s32[2]{0:T(128)S(1)} %pad_add_fusion.5.info, bf16[4,304,384]{2,1,0:T(8,128)(2,1)S(1)} %all-to-all-done.got, bf16[4,304,384]{2,1,0:T(8,128)(2,1)S(1)} %collective-permute-done.other, bf16[4,256,2048]{2,1,0:T(8,128)(2,1)} %bitcast.10.weight, bf16[1,304,384]{2,1,0:T(8,128)(2,1)S(1)} %pre_target.1.rest_0_), custom_call_target="tpu_custom_call" | custom-call | tf_op jit(solution)/shard_map/mid_forward/pallas_call | solution.py:354
  90.1 11.4 %all-to-all-done.2.got = bf16[4,304,384]{2,1,0:T(8,128)(2,1)} async-done(((bf16[4,304,384]{2,1,0:T(8,128)(2,1)}), bf16[4,304,384]{2,1,0:T(8,128)(2,1)}, u32[]{:S(2)}, u32[]{:S(2)}) %all-to-all-start.2) | async-done | bytes 933920 | tf_op jit(solution)/shard_map/all_to_all | solution.py:31
  115.3 13.4 %all_to_all.65.got = bf16[4,304,384]{2,1,0:T(8,128)(2,1)} all-to-all(bf16[4,304,384]{2,1,0:T(8,128)(2,1)S(1)} %get-tuple-element.31), channel_id=1, replica_groups={{0,2,4,6},{1,3,5,7},{8,10,12,14},{9,11,13,15},{16,18,20,22},{17,19,21,2..., dimensions={0} | all-to-all | bytes 1867776 | tf_op jit(solution)/shard_map/all_to_all | solution.py:31
  128.8 6.3 %copy.49 = bf16[4,2048,256]{2,1,0:T(8,128)(2,1)} copy(bf16[4,2048,256]{1,2,0:T(8,128)(2,1)} %all-to-all-done.1) | data formatting | bytes 8388608 | tf_op jit(solution)/shard_map/all_to_all | solution.py:31
  137.2 4.5 %mid_backward_other.3 = bf16[4,304,384]{2,1,0:T(8,128)(2,1)} custom-call(s32[2]{0:T(128)S(1)} %pad_add_fusion.2.info, bf16[4,304,384]{2,1,0:T(8,128)(2,1)} %all-to-all-done.2.got, bf16[4,4,2,256,256]{4,3,2,1,0:T(8,128)(2,1)S(1)} %bitcast.34), custom_call_target="tpu_custom_call" | custom-call | tf_op jit(solution)/shard_map/mid_backward_other/pallas_call | solution.py:354
  142.2 6.0 %mid_forward.5 = bf16[4,304,384]{2,1,0:T(8,128)(2,1)S(1)} custom-call(s32[2]{0:T(128)S(1)} %pad_add_fusion.2.info, bf16[4,304,384]{2,1,0:T(8,128)(2,1)} %all_to_all.65.got, bf16[4,304,384]{2,1,0:T(8,128)(2,1)} %collective-permute-done.2.other, bf16[4,256,2048]{2,1,0:T(8,128)(2,1)} %bitcast.10.weight), custom_call_target="tpu_custom_call" | custom-call | tf_op jit(solution)/shard_map/mid_forward/pallas_call | solution.py:354
  148.2 16.7 %all_to_all.66.got = bf16[4,304,384]{2,1,0:T(8,128)(2,1)S(1)} all-to-all(bf16[4,304,384]{2,1,0:T(8,128)(2,1)S(1)} %mid_forward.5), channel_id=1, replica_groups={{0,8,16,24},{1,9,17,25},{2,10,18,26},{3,11,19,27},{4,12,20,28},{5,13,21..., dimensions={0} | all-to-all | bytes 1867776 | tf_op jit(solution)/shard_map/all_to_all | solution.py:31
  166.5 5.1 %collective-permute-start.3 = (bf16[256,384]{1,0:T(8,128)(2,1)}, bf16[256,384]{1,0:T(8,128)(2,1)}, u32[]{:S(2)}, u32[]{:S(2)}) collective-permute-start(bf16[256,384]{1,0:T(8,128)(2,1)} %get-tuple-element.33), channel_id=1, source_target_pairs={{0,32},{32,64},{64,96},{1,33},{33,65},{65,97},{2,34},{34,66},{66,9... | collective-permute-start | bytes 589832 | tf_op jit(solution)/shard_map/ppermute | solution.py:444
  178.0 15.6 %all_to_all.67.got = bf16[4,304,384]{2,1,0:T(8,128)(2,1)S(1)} all-to-all(bf16[4,304,384]{2,1,0:T(8,128)(2,1)S(1)} %get-tuple-element.34), channel_id=1, replica_groups={{0,2,4,6},{1,3,5,7},{8,10,12,14},{9,11,13,15},{16,18,20,22},{17,19,21,2..., dimensions={0} | all-to-all | bytes 1867776 | tf_op jit(solution)/shard_map/all_to_all | solution.py:31
  196.1 5.4 %mid_forward.6 = bf16[4,304,384]{2,1,0:T(8,128)(2,1)S(1)} custom-call(s32[2]{0:T(128)S(1)} %pad_add_fusion.2.info, bf16[4,304,384]{2,1,0:T(8,128)(2,1)S(1)} %all_to_all.67.got, bf16[4,304,384]{2,1,0:T(8,128)(2,1)S(1)} %collective-permute-done.5.other, bf16[4,256,2048]{2,1,0:T(8,128)(2,1)} %bitcast.10.weight), custom_call_target="tpu_custom_call" | custom-call | tf_op jit(solution)/shard_map/mid_forward/pallas_call | solution.py:354
  213.5 11.8 %collective-permute-done.6.ahead = f32[256,384]{1,0:T(8,128)S(1)} collective-permute-done((f32[256,384]{1,0:T(8,128)S(1)}, f32[256,384]{1,0:T(8,128)S(1)}, u32[]{:S(2)}, u32[]{:S(2)}) %collective-permute-start.6) | collective-permute-done | bytes 393248 | tf_op jit(solution)/shard_map/ppermute | solution.py:447
  230.4 15.2 %all_to_all.68.small = bf16[32,16,384]{2,1,0:T(8,128)(2,1)S(1)} all-to-all(bf16[32,16,384]{2,1,0:T(8,128)(2,1)S(1)} %get-tuple-element.36), channel_id=1, replica_groups=mesh['section'=4,'dp'=32] {'dp'}, dimensions={0} | all-to-all | bytes 786432 | tf_op jit(solution)/shard_map/all_to_all | solution.py:474
  247.5 17.5 %all_to_all.69.got = bf16[4,304,384]{2,1,0:T(8,128)(2,1)S(1)} all-to-all(bf16[4,304,384]{2,1,0:T(8,128)(2,1)S(1)} %get-tuple-element.39), channel_id=1, replica_groups={{0,8,16,24},{1,9,17,25},{2,10,18,26},{3,11,19,27},{4,12,20,28},{5,13,21..., dimensions={0} | all-to-all | bytes 1867776 | tf_op jit(solution)/shard_map/all_to_all | solution.py:31
  270.8 4.7 %collective-permute-done.8.received = bf16[256,384]{1,0:T(8,128)(2,1)S(1)} collective-permute-done((bf16[256,384]{1,0:T(8,128)(2,1)S(1)}, bf16[256,384]{1,0:T(8,128)(2,1)S(1)}, u32[]{:S(2)}, u32[]{:S(2)}) %collective-permute-start.8) | collective-permute-done | bytes 196640 | tf_op jit(solution)/shard_map/ppermute | solution.py:444
  280.9 16.4 %all_to_all.70.got = bf16[4,304,384]{2,1,0:T(8,128)(2,1)S(1)} all-to-all(bf16[4,304,384]{2,1,0:T(8,128)(2,1)S(1)} %mid_backward_own.4), channel_id=1, replica_groups={{0,2,4,6},{1,3,5,7},{8,10,12,14},{9,11,13,15},{16,18,20,22},{17,19,21,2..., dimensions={0} | all-to-all | bytes 1867776 | tf_op jit(solution)/shard_map/all_to_all | solution.py:31
  299.8 5.8 %mid_forward.7.rest_0_ = bf16[4,304,384]{2,1,0:T(8,128)(2,1)S(1)} custom-call(s32[2]{0:T(128)S(1)} %pad_add_fusion.2.info, bf16[4,304,384]{2,1,0:T(8,128)(2,1)S(1)} %all_to_all.70.got, bf16[4,304,384]{2,1,0:T(8,128)(2,1)S(1)} %collective-permute-done.10.other, bf16[4,256,2048]{2,1,0:T(8,128)(2,1)} %bitcast.10.weight), custom_call_target="tpu_custom_call" | custom-call | tf_op jit(solution)/shard_map/mid_forward/pallas_call | solution.py:354
  309.5 16.6 %all_to_all.71.got = bf16[4,304,384]{2,1,0:T(8,128)(2,1)S(1)} all-to-all(bf16[4,304,384]{2,1,0:T(8,128)(2,1)S(1)} %get-tuple-element.45), channel_id=1, replica_groups={{0,8,16,24},{1,9,17,25},{2,10,18,26},{3,11,19,27},{4,12,20,28},{5,13,21..., dimensions={0} | all-to-all | bytes 1867776 | tf_op jit(solution)/shard_map/all_to_all | solution.py:31
  335.3 17.0 %all_to_all.72.got = bf16[4,304,384]{2,1,0:T(8,128)(2,1)S(1)} all-to-all(bf16[4,304,384]{2,1,0:T(8,128)(2,1)S(1)} %mid_backward_own.5), channel_id=1, replica_groups={{0,2,4,6},{1,3,5,7},{8,10,12,14},{9,11,13,15},{16,18,20,22},{17,19,21,2..., dimensions={0} | all-to-all | bytes 1867776 | tf_op jit(solution)/shard_map/all_to_all | solution.py:31
  371.8 8.3 %all-to-all-done.12.got = bf16[16,32,384]{2,1,0:T(8,128)(2,1)S(1)} async-done(((bf16[16,32,384]{2,1,0:T(8,128)(2,1)}), bf16[16,32,384]{2,1,0:T(8,128)(2,1)S(1)}, u32[]{:S(2)}, u32[]{:S(2)}) %all-to-all-start.12) | async-done | bytes 393248 | tf_op jit(solution)/shard_map/all_to_all | solution.py:31
  (164 shorter events, 108.7 us)
Async XLA Ops:
  7.6 18.4 %all-to-all-start = ((bf16[4,304,384]{2,1,0:T(8,128)(2,1)}), bf16[4,304,384]{2,1,0:T(8,128)(2,1)S(1)}, u32[]{:S(2)}, u32[]{:S(2)}) async-start(bf16[4,304,384]{2,1,0:T(8,128)(2,1)} %get-tuple-element.28), calls=%async_computation | async-start | bytes 1867776 | tf_op jit(solution)/shard_map/all_to_all | solution.py:31
  26.0 52.8 %all-to-all-start.1 = ((bf16[4,2048,256]{1,2,0:T(8,128)(2,1)}), bf16[4,2048,256]{1,2,0:T(8,128)(2,1)}, u32[]{:S(2)}, u32[]{:S(2)}) async-start(bf16[4,2048,256]{1,2,0:T(8,128)(2,1)} %copy.44), calls=%async_computation.1 | async-start | bytes 8388608 | tf_op jit(solution)/shard_map/all_to_all | solution.py:31
  30.9 2.6 collective-permute-start
  85.1 16.5 %all-to-all-start.2 = ((bf16[4,304,384]{2,1,0:T(8,128)(2,1)}), bf16[4,304,384]{2,1,0:T(8,128)(2,1)}, u32[]{:S(2)}, u32[]{:S(2)}) async-start(bf16[4,304,384]{2,1,0:T(8,128)(2,1)} %mid_forward.4), calls=%async_computation.2 | async-start | bytes 1867776 | tf_op jit(solution)/shard_map/all_to_all | solution.py:31
  105.2 7.3 %collective-permute-start.1 = (bf16[256,384]{1,0:T(8,128)(2,1)}, bf16[256,384]{1,0:T(8,128)(2,1)}, u32[]{:S(2)}, u32[]{:S(2)}) collective-permute-start(bf16[256,384]{1,0:T(8,128)(2,1)} %get-tuple-element.30), channel_id=1, source_target_pairs={{0,32},{32,64},{64,96},{1,33},{33,65},{65,97},{2,34},{34,66},{66,9... | collective-permute-start | bytes 589832 | tf_op jit(solution)/shard_map/ppermute | solution.py:444
  128.7 13.6 %collective-permute-start.2 = (bf16[4,304,384]{2,1,0:T(8,128)(2,1)}, bf16[4,304,384]{2,1,0:T(8,128)(2,1)}, u32[]{:S(2)}, u32[]{:S(2)}) collective-permute-start(bf16[4,304,384]{2,1,0:T(8,128)(2,1)} %all_to_all.65.got), channel_id=1, source_target_pairs={{0,1},{1,0},{2,3},{3,2},{4,5},{5,4},{6,7},{7,6},{8,9},{9,8},{10,11... | collective-permute-start | bytes 2801672 | tf_op jit(solution)/shard_map/ppermute | solution.py:35
  141.7 29.9 %collective-permute-start.4 = (bf16[4,304,384]{2,1,0:T(8,128)(2,1)}, bf16[4,304,384]{2,1,0:T(8,128)(2,1)}, u32[]{:S(2)}, u32[]{:S(2)}) collective-permute-start(bf16[4,304,384]{2,1,0:T(8,128)(2,1)} %mid_backward_other.3), channel_id=1, source_target_pairs={{0,1},{1,0},{2,3},{3,2},{4,5},{5,4},{6,7},{7,6},{8,9},{9,8},{10,11... | collective-permute-start | bytes 2801672 | tf_op jit(solution)/shard_map/ppermute | solution.py:35
  166.5 9.7 %collective-permute-start.3 = (bf16[256,384]{1,0:T(8,128)(2,1)}, bf16[256,384]{1,0:T(8,128)(2,1)}, u32[]{:S(2)}, u32[]{:S(2)}) collective-permute-start(bf16[256,384]{1,0:T(8,128)(2,1)} %get-tuple-element.33), channel_id=1, source_target_pairs={{0,32},{32,64},{64,96},{1,33},{33,65},{65,97},{2,34},{34,66},{66,9... | collective-permute-start | bytes 589832 | tf_op jit(solution)/shard_map/ppermute | solution.py:444
  193.6 2.5 collective-permute-start.5
  203.4 22.7 %all-to-all-start.6 = ((bf16[4,304,384]{2,1,0:T(8,128)(2,1)}), bf16[4,304,384]{2,1,0:T(8,128)(2,1)}, u32[]{:S(2)}, u32[]{:S(2)}) async-start(bf16[4,304,384]{2,1,0:T(8,128)(2,1)} %copy-done.12), calls=%async_computation.6 | async-start | bytes 1867776 | tf_op jit(solution)/shard_map/all_to_all | solution.py:31
  212.2 13.1 %collective-permute-start.6 = (f32[256,384]{1,0:T(8,128)S(1)}, f32[256,384]{1,0:T(8,128)S(1)}, u32[]{:S(2)}, u32[]{:S(2)}) collective-permute-start(f32[256,384]{1,0:T(8,128)S(1)} %post_target.1), channel_id=1, source_target_pairs={{32,0},{64,32},{96,64},{33,1},{65,33},{97,65},{34,2},{66,34},{98,6... | collective-permute-start | bytes 1179656 | tf_op jit(solution)/shard_map/ppermute | solution.py:447
  226.0 38.9 %copy-start.1 = (bf16[4,2048,256]{2,1,0:T(8,128)(2,1)S(1)}, bf16[4,2048,256]{2,1,0:T(8,128)(2,1)}, u32[]{:S(2)}) copy-start(bf16[4,2048,256]{2,1,0:T(8,128)(2,1)} %copy.49) | copy-start | bytes 12582916
  230.4 37.1 %copy-start.28 = (bf16[256,384]{1,0:T(8,128)(2,1)}, bf16[256,384]{1,0:T(8,128)(2,1)S(1)}, u32[]{:S(2)}) copy-start(bf16[256,384]{1,0:T(8,128)(2,1)S(1)} %get-tuple-element.37.result) | copy-start | bytes 589828
  230.4 77.7 %copy-start.13 = (f32[256,384]{1,0:T(8,128)}, f32[256,384]{1,0:T(8,128)S(1)}, u32[]{:S(2)}) copy-start(f32[256,384]{1,0:T(8,128)S(1)} %get-tuple-element.38.frozen) | copy-start | bytes 1179652
  230.4 121.9 %copy-start.33 = (f32[1,384]{1,0:T(1,128)}, f32[1,384]{1,0:T(1,128)S(1)}, u32[]{:S(2)}) copy-start(f32[1,384]{1,0:T(1,128)S(1)} %get-tuple-element.44.inverse) | copy-start | bytes 4612
  267.4 9.4 %collective-permute-start.7 = (bf16[4,304,384]{2,1,0:T(8,128)(2,1)S(1)}, bf16[4,304,384]{2,1,0:T(8,128)(2,1)S(1)}, u32[]{:S(2)}, u32[]{:S(2)}) collective-permute-start(bf16[4,304,384]{2,1,0:T(8,128)(2,1)S(1)} %mid_backward_other.4), channel_id=1, source_target_pairs={{0,1},{1,0},{2,3},{3,2},{4,5},{5,4},{6,7},{7,6},{8,9},{9,8},{10,11... | collective-permute-start | bytes 2801672 | tf_op jit(solution)/shard_map/ppermute | solution.py:35
  267.5 8.0 %collective-permute-start.8 = (bf16[256,384]{1,0:T(8,128)(2,1)S(1)}, bf16[256,384]{1,0:T(8,128)(2,1)S(1)}, u32[]{:S(2)}, u32[]{:S(2)}) collective-permute-start(bf16[256,384]{1,0:T(8,128)(2,1)S(1)} %get-tuple-element.37.result), channel_id=1, source_target_pairs={{0,32},{32,64},{64,96},{1,33},{33,65},{65,97},{2,34},{34,66},{66,9... | collective-permute-start | bytes 589832 | tf_op jit(solution)/shard_map/ppermute | solution.py:444
  276.8 75.5 %copy-start.15 = (bf16[256,384]{1,0:T(8,128)(2,1)}, bf16[256,384]{1,0:T(8,128)(2,1)S(1)}, u32[]{:S(2)}) copy-start(bf16[256,384]{1,0:T(8,128)(2,1)S(1)} %get-tuple-element.42.current) | copy-start | bytes 589828
  297.3 2.5 collective-permute-start.10
  298.2 10.0 %collective-permute-start.9 = (bf16[256,384]{1,0:T(8,128)(2,1)S(1)}, bf16[256,384]{1,0:T(8,128)(2,1)S(1)}, u32[]{:S(2)}, u32[]{:S(2)}) collective-permute-start(bf16[256,384]{1,0:T(8,128)(2,1)S(1)} %post_backward.2), channel_id=1, source_target_pairs={{32,0},{64,32},{96,64},{33,1},{65,33},{97,65},{34,2},{66,34},{98,6... | collective-permute-start | bytes 589832 | tf_op jit(solution)/shard_map/ppermute | solution.py:447
  328.7 2.6 collective-permute-start.11
  353.8 8.2 %collective-permute-start.12 = (bf16[256,384]{1,0:T(8,128)(2,1)}, bf16[256,384]{1,0:T(8,128)(2,1)S(1)}, u32[]{:S(2)}, u32[]{:S(2)}) collective-permute-start(bf16[256,384]{1,0:T(8,128)(2,1)} %post_backward.3), channel_id=1, source_target_pairs={{32,0},{64,32},{96,64},{33,1},{65,33},{97,65},{34,2},{66,34},{98,6... | collective-permute-start | bytes 589832 | tf_op jit(solution)/shard_map/ppermute | solution.py:447
  364.0 1.3 collective-permute-start.13
  366.1 13.9 %all-to-all-start.12 = ((bf16[16,32,384]{2,1,0:T(8,128)(2,1)}), bf16[16,32,384]{2,1,0:T(8,128)(2,1)S(1)}, u32[]{:S(2)}, u32[]{:S(2)}) async-start(bf16[16,32,384]{2,1,0:T(8,128)(2,1)} %broadcast_in_dim.19), calls=%async_computation.12 | async-start | bytes 786432 | tf_op jit(solution)/shard_map/all_to_all | solution.py:31
  (36 other events, 335.1 us)

commit v4 on v2

v4 whole, which is shorter than its diff:
```python
import functools

import jax
import jax.numpy as jnp
from jax import lax
from jax.experimental import pallas as pl
from jax.experimental.pallas import tpu as pltpu
from jax.sharding import PartitionSpec as P

EPSILON = 1e-06
SCALING = 2.0
XS, YS, CS = 4, 4, 2
BF = jnp.bfloat16
F32 = jnp.float32
VM = pl.BlockSpec(memory_space=pltpu.VMEM)
SM = pl.BlockSpec(memory_space=pltpu.SMEM)
PARAMS = pltpu.CompilerParams(vmem_limit_bytes=48 << 20)


def place(x, y, c):
    return (x * YS + y) * CS + c


def partner(x, y, c, k):
    other = lambda v: (v ^ 1) if c == 0 else ((v + 1) % 4 if v % 2 else (v - 1) % 4)
    return (other(x) if k & 2 else x), (other(y) if k & 1 else y)


APART = [
    [place(x + 2 * i, y + 2 * j, c) for i in range(2) for j in range(2)]
    for x in range(2)
    for y in range(2)
    for c in range(CS)
]
BLOCKS = [
    [place(*partner(x, y, c, k), c) for k in range(4)]
    for x in range(0, XS, 2)
    for y in range(0, YS, 2)
    for c in range(CS)
]
ALONG_XY = [[place(x, y, c) for x in range(XS) for y in range(YS)] for c in range(CS)]
SIBLING = [(i, i ^ 1) for i in range(XS * YS * CS)]


def exchange(chunks, groups):
    return lax.all_to_all(chunks, "dp", 0, 0, axis_index_groups=groups)


def swap_cores(block):
    return lax.ppermute(block, "dp", SIBLING)


def tables_of(seg_ids, live_counts, adapters):
    micro, rows = seg_ids.shape
    labels = jnp.arange(adapters, dtype=jnp.int32)
    member = (seg_ids[:, None, :] == labels[None, :, None]).astype(jnp.int32)
    counts = jnp.sum(member, axis=2)
    before = (labels[:, None] < labels[None, :]).astype(jnp.int32)
    starts = jnp.sum(counts[:, :, None] * before[None], axis=1)
    row_start = jnp.sum(member * starts[:, :, None], axis=1)
    row_limit = jnp.sum(member * jnp.minimum(live_counts, counts)[:, :, None], axis=1)
    live = jnp.arange(rows, dtype=jnp.int32)[None] - row_start < row_limit
    whole = member.astype(F32).transpose(1, 0, 2).reshape(adapters, micro * rows)
    return whole, live.reshape(micro * rows)


def dot(left, right, dims=((1,), (0,))):
    return lax.dot_general(left, right, (dims, ((), ())), preferred_element_type=F32)


def tail_of(ranks, rows):
    high = rows.astype(BF).astype(F32)
    return jnp.concatenate([ranks, high, rows - high], axis=0).astype(BF)


def eight(*rows):
    index = lax.broadcasted_iota(jnp.int32, (8, rows[0].shape[1]), 0)
    total = jnp.zeros(index.shape, F32)
    for at, row in enumerate(rows):
        total = jnp.where(index == at, row, total)
    return total


def extras(chunks, cols, rank):
    total = chunks[0, cols:].astype(F32)
    for j in range(1, chunks.shape[0]):
        total = total + chunks[j, cols:].astype(F32)
    return total[:rank], total[rank : rank + 8] + total[rank + 8 :]


def mains(chunks, cols):
    total = chunks[0, :cols].astype(F32)
    for j in range(1, chunks.shape[0]):
        total = total + chunks[j, :cols].astype(F32)
    return total


def select_rank(parts, member, rank):
    total = None
    for a in range(member.shape[0]):
        part = parts[a * rank : (a + 1) * rank] * member[a : a + 1, :]
        total = part if total is None else total + part
    return total


def spread_rank(values, member, store):
    rank = values.shape[0]
    for a in range(member.shape[0]):
        store[a * rank : (a + 1) * rank] = (values * member[a : a + 1, :]).astype(BF)


def fill(sent, main, tail):
    cols = main.shape[0]
    for j in range(sent.shape[0]):
        sent[j, :cols] = main
        sent[j, cols:] = tail


def column_sum(left, right):
    return jnp.sum(left * right, axis=0, keepdims=True)


def pre_forward(current, gain, a_flat, member, sent):
    rank = a_flat.shape[0] // member.shape[0]
    values = current[...].astype(F32)
    scaled = (values * gain[...]).astype(BF)
    ranks = select_rank(dot(a_flat[...], scaled), member, rank)
    fill(sent, scaled, tail_of(ranks, eight(column_sum(values, values))))


def mid_forward(info, got, other, weight, sent, joined):
    cols, rank = weight.shape[2], got.shape[1] - weight.shape[2] - 16
    core = info[0]

    @pl.when(pl.program_id(0) == 0)
    def _():
        for y in range(YS):
            mine = pl.multiple_of((y * CS + core) * cols, cols)
            theirs = pl.multiple_of((y * CS + 1 - core) * cols, cols)
            joined[pl.ds(mine, cols)] = got[y, :cols]
            joined[pl.ds(theirs, cols)] = other[y, :cols]

    sent[0, :cols] = dot(weight[0].T, joined[...]).astype(BF)
    ranks, rows = extras(got, cols, rank)
    ranks_o, rows_o = extras(other, cols, rank)
    sent[0, cols:] = tail_of(ranks + ranks_o, rows + rows_o)


def finish(width, got, current, b_turned, member, result, frozen, down_raw, inverse, down, store):
    cols, rank = current.shape[0], down.shape[0]
    total = mains(got, cols)
    ranks, rows = extras(got, cols, rank)
    scale = lax.rsqrt(rows[0:1] / width + EPSILON)
    kept = (ranks * scale).astype(BF)
    spread_rank(kept.astype(F32), member, store)
    adapter = dot(b_turned[...], store[...])
    value = (current[...].astype(F32) + total * scale + SCALING * adapter).astype(BF)
    result[...] = value
    frozen[...] = total
    down_raw[...] = ranks
    inverse[...] = scale
    down[...] = kept
    return value, total


def post_forward(width, *refs):
    finish(width, *refs)


def post_forward_turn(width, target, ahead, b_flat, *refs):
    sent = refs[-2]
    member, rank = refs[3], refs[-3].shape[0]
    value, frozen = finish(width, *refs[:-2], refs[-1])
    ranks = select_rank(dot(b_flat[...], value), member, rank)
    values = value.astype(F32)
    early, late = target[...].astype(F32), ahead[...].astype(F32)
    rows = eight(
        column_sum(values, values),
        column_sum(values, late),
        column_sum(early, frozen),
        column_sum(late, frozen),
        column_sum(values, frozen),
    )
    fill(sent, value, tail_of(ranks, rows))


def pre_backward(grad, frozen, b_flat, member, sent):
    rank = b_flat.shape[0] // member.shape[0]
    kept = grad[...]
    ranks = select_rank(dot(b_flat[...], kept), member, rank)
    row = column_sum(kept.astype(F32), frozen[...])
    fill(sent, kept, tail_of(ranks, eight(row)))


def pre_plain(grad, b_flat, member, sent):
    rank = b_flat.shape[0] // member.shape[0]
    kept = grad[...]
    ranks = select_rank(dot(b_flat[...], kept), member, rank)
    fill(sent, kept, tail_of(ranks, jnp.zeros((8, kept.shape[1]), F32)))


def row_product(got, weight, cols):
    total = dot(weight[0, 0, 0], got[0, :cols])
    for j in range(1, XS):
        total = total + dot(weight[j, 0, 0], got[j, :cols])
    return total


def mid_backward_other(info, got, weight, sent):
    cols = weight.shape[-1]
    sent[0, :cols] = row_product(got, weight, cols).astype(BF)
    sent[0, cols:] = tail_of(*extras(got, cols, got.shape[1] - cols - 16))


def mid_backward_own(info, got, weight, other, sent):
    cols = weight.shape[-1]
    rank = got.shape[1] - cols - 16
    total = row_product(got, weight, cols) + other[0, :cols].astype(F32)
    sent[0, :cols] = total.astype(BF)
    ranks, rows = extras(got, cols, rank)
    ranks_o, rows_o = extras(other, cols, rank)
    sent[0, cols:] = tail_of(ranks + ranks_o, rows + rows_o)


def add_up(got, total, ranks):
    cols, rank = total.shape[0], ranks.shape[0]
    total[...] = mains(got, cols)
    ranks[...] = extras(got, cols, rank)[0]


def post_target(rank, got, a_turned, member, gain, ahead, store):
    cols = ahead.shape[0]
    ranks, _ = extras(got, cols, rank)
    spread_rank((SCALING * ranks).astype(BF).astype(F32), member, store)
    normed_grad = mains(got, cols) + dot(a_turned[...], store[...])
    ahead[...] = (gain[...] * normed_grad).astype(BF)


def step_back(
    width, grad, back, ranks, row, current, a_turned, member, down_raw, inverse, gain, store
):
    grad_down = (SCALING * ranks).astype(BF).astype(F32)
    spread_rank(grad_down, member, store)
    normed_grad = back + dot(a_turned[...], store[...])
    stat = (row + column_sum(grad_down, down_raw[...])) / width
    scale = inverse[...]
    return (
        grad
        + scale * gain[...] * normed_grad
        - current[...].astype(F32) * (scale * scale * scale * stat)
    ).astype(BF)


def post_backward(
    width, got, grad, current, a_turned, member, down_raw, inverse, gain, grad_in, store
):
    cols, rank = current.shape[0], down_raw.shape[0]
    ranks, rows = extras(got, cols, rank)
    grad_in[...] = step_back(
        width, grad[...].astype(F32), mains(got, cols), ranks, rows[0:1],
        current, a_turned, member, down_raw, inverse, gain, store,
    )


def post_turn(
    width, got, back_first, ranks_first, back_late, ranks_late, target, ahead, result,
    current, a_turned, member, down_raw, inverse, gain, grad, grad_in, store,
):
    cols, rank = current.shape[0], down_raw.shape[0]
    ranks, rows = extras(got, cols, rank)
    scale = lax.rsqrt(rows[0:1] / width + EPSILON)
    least = scale * scale * scale * (rows[1:2] / width)
    fresh = (
        target[...].astype(F32)
        + scale * ahead[...].astype(F32)
        - least * result[...].astype(F32)
    )
    kept = fresh.astype(BF)
    grad[...] = kept
    grad_in[...] = step_back(
        width,
        kept.astype(F32),
        back_first[...] + scale * back_late[...] - least * mains(got, cols),
        ranks_first[...] + scale * ranks_late[...] - least * ranks,
        rows[2:3] + scale * rows[3:4] - least * rows[4:5],
        current, a_turned, member, down_raw, inverse, gain, store,
    )


def ranks_of(grad, b_flat, member, ranks):
    ranks[...] = select_rank(dot(b_flat[...], grad[...]), member, ranks.shape[0])


def outer_up(down, grad, member, grad_b, store):
    spread_rank(SCALING * down[...].astype(F32), member, store)
    grad_b[...] = dot(store[...], grad[...], ((1,), (1,)))


def outer_down(got, current, inverse, gain, member, grad_a, store):
    ranks = got[0].astype(F32)
    for j in range(1, got.shape[0]):
        ranks = ranks + got[j].astype(F32)
    spread_rank((SCALING * ranks).astype(BF).astype(F32), member, store)
    normed = (current[...].astype(F32) * inverse[...] * gain[...]).astype(BF)
    grad_a[...] = dot(store[...], normed, ((1,), (1,)))


def cost(flops, arrays):
    return pl.CostEstimate(
        flops=int(flops),
        bytes_accessed=sum(x.size * x.dtype.itemsize for x in arrays),
        transcendentals=0,
    )


def whole_call(body, name, outs, ins, scratch=(), flops=4e8):
    return pl.pallas_call(
        body,
        out_shape=[jax.ShapeDtypeStruct(s, d) for s, d in outs],
        in_specs=[VM] * len(ins),
        out_specs=[VM] * len(outs),
        scratch_shapes=list(scratch),
        compiler_params=PARAMS,
        cost_estimate=cost(flops, ins),
        name=name,
    )(*ins)


def on_device(
    tokens_in, cotangent, base_weight, norm_gain, adapter_a, adapter_b, seg_ids, live_counts
):
    section = lax.axis_index("section")
    at = lax.axis_index("dp")
    at_x, at_y, core = at // (YS * CS), (at // CS) % YS, at % CS
    micro, rows, cols = tokens_in.shape
    total = micro * rows
    adapters, rank = adapter_a.shape[1:3]
    width = base_weight.shape[1]
    tall = cols + rank + 16
    gain = norm_gain[0].astype(F32)[:, None]
    a_flat = adapter_a[0].reshape(adapters * rank, cols)
    b_flat = adapter_b[0].reshape(adapters * rank, cols)
    a_turned, b_turned = a_flat.T, b_flat.T
    member, live = tables_of(seg_ids, live_counts, adapters)
    info = core.astype(jnp.int32).reshape(1)
    store = pltpu.VMEM((adapters * rank, total), BF)
    payload = ((XS, tall, total), BF)
    main = ((cols, total), BF)
    wide = ((cols, total), F32)
    thin = ((rank, total), F32)
    kept_outs = [main, wide, thin, ((1, total), F32), ((rank, total), BF)]

    block = base_weight[0].reshape(2, 2, 2, 2, CS * cols, cols).transpose(1, 3, 0, 2, 4, 5)
    block = exchange(block.reshape(XS, width // XS, cols), BLOCKS)
    halves = block.reshape(XS, YS, CS, cols, cols)
    tokens = tokens_in.reshape(total, cols).T
    target = jnp.where(live[None, :], cotangent.reshape(total, cols).T, jnp.zeros((), BF))

    def mid_call(body, name, weight, weight_spec, ins, whole, scratch=(), flops=8e8):
        block_of = pl.BlockSpec((1, tall, total), lambda i, c: (i, 0, 0))
        full = pl.BlockSpec((XS, tall, total), lambda i, c: (0, 0, 0))
        specs = [full] * whole + [weight_spec] + [block_of] * (len(ins) - whole)
        ins = ins[:whole] + [weight] + ins[whole:]
        return pl.pallas_call(
            body,
            grid_spec=pltpu.PrefetchScalarGridSpec(
                num_scalar_prefetch=1,
                grid=(4,),
                in_specs=specs,
                out_specs=block_of,
                scratch_shapes=list(scratch),
            ),
            out_shape=jax.ShapeDtypeStruct(*payload),
            compiler_params=PARAMS,
            cost_estimate=cost(flops, ins),
            name=name,
        )(info, *ins)

    def start_forward(current, out=payload):
        (sent,) = whole_call(pre_forward, "pre_forward", [out], [current, gain, a_flat, member])
        return sent

    def product_forward(got, other):
        return mid_call(
            mid_forward,
            "mid_forward",
            block,
            pl.BlockSpec((1, width // XS, cols), lambda i, c: (i, 0, 0)),
            [got, other],
            2,
            [pltpu.VMEM((width // XS, total), BF)],
            flops=16e8,
        )

    def end_forward(got, current):
        return whole_call(
            functools.partial(post_forward, width),
            "post_forward",
            kept_outs,
            [got, current, b_turned, member],
            scratch=[store],
        )

    def forward(current):
        got = exchange(start_forward(current), APART)
        return exchange(product_forward(got, swap_cores(got)), BLOCKS)

    def product_backward(got):
        shape = (XS, 1, 1, cols, cols)
        other = mid_call(
            mid_backward_other,
            "mid_backward_other",
            halves,
            pl.BlockSpec(shape, lambda i, c: (0, i, 1 - c[0], 0, 0)),
            [got],
            1,
        )
        return mid_call(
            mid_backward_own,
            "mid_backward_own",
            halves,
            pl.BlockSpec(shape, lambda i, c: (0, i, c[0], 0, 0)),
            [got, swap_cores(other)],
            1,
        )

    def backward(got):
        return exchange(product_backward(got), APART)

    def plain(vector, out=payload):
        return whole_call(pre_plain, "pre_plain", [out], [vector, b_flat, member])[0]

    def sums_of(got):
        return whole_call(add_up, "add_up", [wide, thin], [backward(got)])

    def zeros(*kinds):
        return [jnp.zeros(*kind) for kind in kinds]

    def hop(value, pairs):
        return lax.ppermute(value, "section", pairs)

    def switch(cases, outs):
        nothing = lambda: tuple(zeros(*outs))
        return lax.switch(
            section, [(lambda f=cases.get(s): tuple(f())) if s in cases else nothing for s in range(4)]
        )

    single = ((1, tall, total), BF)
    gather = section < 2
    first = jnp.where(gather, start_forward(tokens, single), plain(target, single))
    turns = [first]
    for k in range(1, 4):
        pairs = []
        for i in range(4 * XS * YS * CS):
            s, x, y, c = i // (XS * YS * CS), i // (YS * CS) % XS, i // CS % YS, i % CS
            to = (x ^ (k & 2), y ^ (k & 1) * 2) if s < 2 else partner(x, y, c, k)
            pairs.append((i, s * XS * YS * CS + place(*to, c)))
        turns.append(lax.ppermute(first, ("section", "dp"), pairs))
    turns = jnp.concatenate(turns)
    own = jnp.where(gather, at_x // 2 * 2 + at_y // 2, at_x % 2 * 2 + at_y % 2)
    got = jnp.stack([lax.dynamic_index_in_dim(turns, own ^ j, 0, False) for j in range(4)])
    other = swap_cores(got)

    def run_first():
        outs = end_forward(exchange(product_forward(got, other), BLOCKS), tokens)
        return [outs[0], outs[3], outs[4]] + zeros(wide, thin)

    def run_target():
        (ahead,) = whole_call(
            functools.partial(post_target, rank),
            "post_target",
            [main],
            [backward(got), a_turned, member, gain],
            scratch=[store],
        )
        return [ahead] + zeros(kept_outs[3], kept_outs[4], wide, thin)

    def run_ready():
        return zeros(main, kept_outs[3], kept_outs[4]) + list(sums_of(got))

    vector, inverse_0, down_0, back_first, ranks_first = switch(
        {0: run_first, 3: run_target, 2: run_ready}, [main, kept_outs[3], kept_outs[4], wide, thin]
    )
    received = hop(vector, [(0, 1), (3, 2)])

    def run_second():
        return list(end_forward(forward(received), received)) + zeros(wide, thin)

    def run_late():
        return zeros(*kept_outs) + list(sums_of(exchange(plain(received), BLOCKS)))

    result_1, frozen_1, raw_1, inverse_1, down_1, back_late, ranks_late = switch(
        {1: run_second, 2: run_late}, kept_outs + [wide, thin]
    )
    second = hop(result_1, [(1, 2)])

    def run_turn():
        result, _, raw, inverse, down, sent = whole_call(
            functools.partial(post_forward_turn, width),
            "post_forward_turn",
            kept_outs + [payload],
            [target, received, b_flat, forward(second), second, b_turned, member],
            scratch=[store],
        )
        grad, grad_in = whole_call(
            functools.partial(post_turn, width),
            "post_turn",
            [main, main],
            [backward(exchange(sent, BLOCKS)), back_first, ranks_first, back_late, ranks_late, target, received]
            + [result, second, a_turned, member, raw, inverse, gain],
            scratch=[store],
        )
        return result, inverse, down, grad, grad_in

    result_2, inverse_2, down_2, grad_2, grad_in = switch(
        {2: run_turn}, [main, kept_outs[3], kept_outs[4], main, main]
    )
    third = hop(result_2, [(2, 3)])
    grad_1 = hop(grad_in, [(2, 1)])

    def run_back():
        (sent,) = whole_call(
            pre_backward, "pre_backward", [payload], [grad_1, frozen_1, b_flat, member]
        )
        (grad_in,) = whole_call(
            functools.partial(post_backward, width),
            "post_backward",
            [main],
            [backward(exchange(sent, BLOCKS)), grad_1, received, a_turned, member, raw_1, inverse_1, gain],
            scratch=[store],
        )
        return [grad_in] + zeros(kept_outs[3], kept_outs[4])

    def run_last():
        outs = end_forward(forward(third), third)
        return outs[0], outs[3], outs[4]

    vector_3, inverse_3, down_3 = switch({1: run_back, 3: run_last}, [main] + kept_outs[3:])
    grad_0 = hop(vector_3, [(1, 0)])

    def choose(*values):
        return lax.select_n(section.astype(jnp.int32), *values)

    grad = choose(grad_0, grad_1, grad_2, target)
    (ranks,) = whole_call(ranks_of, "ranks_of", [thin], [grad, b_flat, member])
    ranks = (ranks + swap_cores(ranks)).astype(BF)
    ranks = exchange(jnp.broadcast_to(ranks[None], (XS * YS,) + ranks.shape), ALONG_XY)
    current = choose(tokens, received, second, third)
    result = choose(vector, result_1, result_2, vector_3)
    inverse = choose(inverse_0, inverse_1, inverse_2, inverse_3)
    down = choose(down_0, down_1, down_2, down_3)
    (grad_b,) = whole_call(
        outer_up,
        "outer_up",
        [((adapters * rank, cols), F32)],
        [down, grad, member],
        scratch=[store],
    )
    (grad_a,) = whole_call(
        outer_down,
        "outer_down",
        [((adapters * rank, cols), F32)],
        [ranks, current, inverse, gain, member],
        scratch=[store],
    )
    section_out = result.T.reshape(1, micro, rows, cols)
    shape = (1, adapters, rank, cols)
    return section_out, grad_a.reshape(shape), grad_b.reshape(shape)


def solution(mesh):
    in_specs = (
        P(None, None, "dp"),
        P(None, None, "dp"),
        P("section", None, "dp"),
        P("section", "dp"),
        P("section", None, None, "dp"),
        P("section", None, None, "dp"),
        P(),
        P(),
    )
    out_specs = (
        P("section", None, None, "dp"),
        P("section", None, None, "dp"),
        P("section", None, None, "dp"),
    )
    return jax.shard_map(
        on_device, mesh=mesh, in_specs=in_specs, out_specs=out_specs, check_vma=False
    )
```

time: 449 us -> 316 us (0.70)
  blocking collectives: 141 us -> 0 us
  waiting for transfers between devices: 152 us -> 252 us
  Pallas kernels: 62.5 us -> 13.9 us
  local copies, waits for them, and re-layouts: 39 us -> 13.8 us
  starting transfers between devices: 48.5 us -> 26.9 us
    ppermute x7 -> x8, waiting for transfers between devices: 31.2 us -> 236 us  [the longest x5 207 us: hop(): return lax.ppermute(value, 'section', pairs)]
    all_to_all x9 -> x0, blocking collectives: 141 us -> none  [exchange(): return lax.all_to_all(chunks, 'dp', 0, 0, axis_index_groups=groups)]
    all_to_all x7 -> x3, waiting for transfers between devices: 104 us -> 13.7 us  [exchange(): return lax.all_to_all(chunks, 'dp', 0, 0, axis_index_groups=groups)]
    pallas_call x10 -> x1, Pallas kernels: 36.5 us -> 5.99 us  [mid_call(): pl.pallas_call(body, grid_spec=pltpu.PrefetchScalarGridSpec(num_scalar_pr...]
    unnamed x68 -> x58, local copies, waits for them, and re-layouts: 19.7 us -> 0.78 us
    pallas_call x17 -> x6, Pallas kernels: 25.9 us -> 7.93 us  [whole_call(): pl.pallas_call(body, out_shape=[jax.ShapeDtypeStruct(s, d) for s, d in ou...]
    all_to_all x7 -> x3, starting transfers between devices: 29.3 us -> 14.1 us  [exchange(): return lax.all_to_all(chunks, 'dp', 0, 0, axis_index_groups=groups)]
    ppermute x7 -> x2, waiting for transfers between devices: 17.3 us -> 3.02 us  [swap_cores(): return lax.ppermute(block, 'dp', SIBLING)]
  transfers between devices with their start and end apart: 21 -> 13, of which waited for: 21 -> 7; matrix products, arithmetic and copies ran while one was open for 4% -> 2% of each run, Pallas kernels for 0% -> 1%
where the time goes in v4:
time: 316 us; the launch traced here: 315 us
  waiting for transfers between devices  252 us (80%)
  starting transfers between devices  26.9 us (9%)
  Pallas kernels  13.9 us (4%)
  local copies, waits for them, and re-layouts  13.8 us (4%)
  other arithmetic  6.26 us (2%)
    ppermute x5, waiting for transfers between devices, hop(): return lax.ppermute(value, 'section', pairs)  207 us
    ppermute x3, waiting for transfers between devices, on_device(): turns.append(lax.ppermute(first, ('section', 'dp'), pairs))  28.2 us
    all_to_all x3, starting transfers between devices, exchange(): return lax.all_to_all(chunks, 'dp', 0, 0, axis_index_groups=groups)  14.1 us
    all_to_all x3, waiting for transfers between devices, exchange(): return lax.all_to_all(chunks, 'dp', 0, 0, axis_index_groups=groups)  13.7 us
    pallas_call x6, Pallas kernels, whole_call(): pl.pallas_call(body, out_shape=[jax.ShapeDtypeStruct(s, d) for s, d in ou...  7.93 us
    ppermute x3, starting transfers between devices, on_device(): turns.append(lax.ppermute(first, ('section', 'dp'), pairs))  6.58 us
  transfers between devices with their start and end apart: 13, of which 7 were waited for; matrix products, arithmetic and copies ran while one was open for 2% of the time, Pallas kernels for 1%

profile of v4, /device:TPU:0, one launch (start us, length us, event | category | flops | bytes accessed | tf_op | source)
XLA Modules:
  0.0 314.8 jit_solution(1442412682699855232)
XLA Ops:
  0.6 4.6 %copy.43 = bf16[2,2,2,2,512,256]{5,4,2,0,3,1:T(8,128)(2,1)} copy(bf16[2,2,2,2,512,256]{5,4,3,2,1,0:T(8,128)(2,1)} %bitcast.47) | data formatting | bytes 8388608 | tf_op jit(solution)/shard_map/reshape;squeeze | solution.py:353
  5.3 5.1 %all-to-all-start.15 = ((bf16[4,2048,256]{2,1,0:T(8,128)(2,1)}), bf16[4,2048,256]{2,1,0:T(8,128)(2,1)}, u32[]{:S(2)}, u32[]{:S(2)}) async-start(bf16[4,2048,256]{2,1,0:T(8,128)(2,1)} %bitcast.46), calls=%async_computation.15 | async-start | bytes 8388608 | tf_op jit(solution)/shard_map/all_to_all | solution.py:46
  13.2 5.8 %collective-permute-start.10 = (bf16[1,304,384]{2,1,0:T(8,128)(2,1)S(1)}, bf16[1,304,384]{2,1,0:T(8,128)(2,1)S(1)}, u32[]{:S(2)}, u32[]{:S(2)}) collective-permute-start(bf16[1,304,384]{2,1,0:T(8,128)(2,1)S(1)} %broadcast_select_fusion), channel_id=1, source_target_pairs={{0,20},{1,21},{2,22},{3,23},{4,16},{5,17},{6,18},{7,19},{8,28},{9,... | collective-permute-start | bytes 700424 | tf_op jit(solution)/shard_map/ppermute | solution.py:458
  19.8 28.2 %collective-permute-done.10 = bf16[1,304,384]{2,1,0:T(8,128)(2,1)S(1)} collective-permute-done((bf16[1,304,384]{2,1,0:T(8,128)(2,1)S(1)}, bf16[1,304,384]{2,1,0:T(8,128)(2,1)S(1)}, u32[]{:S(2)}, u32[]{:S(2)}) %collective-permute-start.10) | collective-permute-done | bytes 233504 | tf_op jit(solution)/shard_map/ppermute | solution.py:458
  48.0 1.1 pad_maximum_fusion
  49.5 2.6 collective-permute-done.11
  52.1 19.9 %conditional.4 = (bf16[256,384]{1,0:T(8,128)(2,1)S(1)}, f32[1,384]{1,0:T(1,128)S(1)}, bf16[32,384]{1,0:T(8,128)(2,1)S(1)}, f32[256,384]{1,0:T(8,128)S(1)}, f32[32,384]{1,0:T(8,128)S(1)}) conditional(s32[]{:T(128)} %clamp.2, (s32[1]{0:T(128)}, bf16[4,304,384]{2,1,0:T(8,128)(2,1)S(1)}, bf16[4,304,384]{2,1,0:T(8,128)(2,1)}, ...), branch_computations={%region_4.5_spmd, %region_5.6_spmd, %region_6.7_spmd, %region_7.8_... | conditional | flops 2000000000 | bytes 26571418 | solution.py:444
  52.1 6.0 %mid_forward.4 = bf16[4,304,384]{2,1,0:T(8,128)(2,1)} custom-call(s32[1]{0:T(128)} %get-tuple-element.124.info, bf16[4,304,384]{2,1,0:T(8,128)(2,1)S(1)} %get-tuple-element.125.got, bf16[4,304,384]{2,1,0:T(8,128)(2,1)} %get-tuple-element.126.other, bf16[4,2048,256]{2,1,0:T(8,128)(2,1)} %get-tuple-element.127.weight), custom_call_target="tpu_custom_call" | custom-call | flops 1600000000 | bytes 6062080 | tf_op jit(solution)/shard_map/cond/branch_0_fun/mid_forward/pallas_call | solution.py:364
  58.1 3.5 %all-to-all-start = ((bf16[4,304,384]{2,1,0:T(8,128)(2,1)}), bf16[4,304,384]{2,1,0:T(8,128)(2,1)S(1)}, u32[]{:S(2)}, u32[]{:S(2)}) async-start(bf16[4,304,384]{2,1,0:T(8,128)(2,1)} %mid_forward.4), calls=%async_computation | async-start | bytes 1867776 | tf_op jit(solution)/shard_map/cond/branch_0_fun/all_to_all | solution.py:46
  62.2 8.1 %all-to-all-done.refs_0_ = bf16[4,304,384]{2,1,0:T(8,128)(2,1)S(1)} async-done(((bf16[4,304,384]{2,1,0:T(8,128)(2,1)}), bf16[4,304,384]{2,1,0:T(8,128)(2,1)S(1)}, u32[]{:S(2)}, u32[]{:S(2)}) %all-to-all-start) | async-done | bytes 933920 | tf_op jit(solution)/shard_map/cond/branch_0_fun/all_to_all | solution.py:46
  70.4 1.5 post_forward.3
  72.0 1.3 collective-permute-start.12
  73.3 4.0 %collective-permute-done.12 = bf16[256,384]{1,0:T(8,128)(2,1)S(1)} collective-permute-done((bf16[256,384]{1,0:T(8,128)(2,1)S(1)}, bf16[256,384]{1,0:T(8,128)(2,1)S(1)}, u32[]{:S(2)}, u32[]{:S(2)}) %collective-permute-start.12) | collective-permute-done | bytes 196640 | tf_op jit(solution)/shard_map/ppermute | solution.py:440
  77.4 1.1 conditional.5
  78.5 1.3 collective-permute-start.13
  79.9 3.3 %conditional.6 = (bf16[256,384]{1,0:T(8,128)(2,1)}, f32[1,384]{1,0:T(1,128)}, bf16[32,384]{1,0:T(8,128)(2,1)}, bf16[256,384]{1,0:T(8,128)(2,1)}, bf16[256,384]{1,0:T(8,128)(2,1)}) conditional(s32[]{:T(128)} %clamp.2, () %tuple.80, () %tuple.81, (bf16[256,384]{1,0:T(8,128)(2,1)}, f32[256,1]{0,1:T(1,128)}, ...), branch_computations={%region_12.13_spmd, %region_13.14_spmd, %region_14.15_spmd, %regio... | conditional | flops 4400000000 | bytes 47912660 | solution.py:444
  83.9 1.3 collective-permute-start.14
  85.9 1.3 conditional.7
  87.2 1.4 collective-permute-start.16
  89.7 203.4 %collective-permute-done.16 = bf16[256,384]{1,0:T(8,128)(2,1)S(1)} collective-permute-done((bf16[256,384]{1,0:T(8,128)(2,1)}, bf16[256,384]{1,0:T(8,128)(2,1)S(1)}, u32[]{:S(2)}, u32[]{:S(2)}) %collective-permute-start.16) | collective-permute-done | bytes 196640 | tf_op jit(solution)/shard_map/ppermute | solution.py:440
  297.1 5.4 %all-to-all-start.16 = ((bf16[16,32,384]{2,1,0:T(8,128)(2,1)}), bf16[16,32,384]{2,1,0:T(8,128)(2,1)S(1)}, u32[]{:S(2)}, u32[]{:S(2)}) async-start(bf16[16,32,384]{2,1,0:T(8,128)(2,1)} %broadcast_in_dim.12), calls=%async_computation.16 | async-start | bytes 786432 | tf_op jit(solution)/shard_map/all_to_all | solution.py:46
  305.0 2.1 outer_up.1
  307.1 5.6 %all-to-all-done.16.got = bf16[16,32,384]{2,1,0:T(8,128)(2,1)S(1)} async-done(((bf16[16,32,384]{2,1,0:T(8,128)(2,1)}), bf16[16,32,384]{2,1,0:T(8,128)(2,1)S(1)}, u32[]{:S(2)}, u32[]{:S(2)}) %all-to-all-start.16) | async-done | bytes 393248 | tf_op jit(solution)/shard_map/all_to_all | solution.py:46
  312.6 2.1 outer_down.1
  (116 shorter events, 18.7 us)
Async XLA Ops:
  5.2 6.4 %copy-start = (bf16[1,64,32,256]{3,2,1,0:T(8,128)(2,1)S(1)}, bf16[1,64,32,256]{3,2,1,0:T(8,128)(2,1)}, u32[]{:S(2)}) copy-start(bf16[1,64,32,256]{3,2,1,0:T(8,128)(2,1)} %param.29) | copy-start | bytes 3145732
  5.2 7.1 %copy-start.1 = (bf16[1,64,32,256]{3,2,1,0:T(8,128)(2,1)S(1)}, bf16[1,64,32,256]{3,2,1,0:T(8,128)(2,1)}, u32[]{:S(2)}) copy-start(bf16[1,64,32,256]{3,2,1,0:T(8,128)(2,1)} %param.28) | copy-start | bytes 3145732
  5.3 44.2 %all-to-all-start.15 = ((bf16[4,2048,256]{2,1,0:T(8,128)(2,1)}), bf16[4,2048,256]{2,1,0:T(8,128)(2,1)}, u32[]{:S(2)}, u32[]{:S(2)}) async-start(bf16[4,2048,256]{2,1,0:T(8,128)(2,1)} %bitcast.46), calls=%async_computation.15 | async-start | bytes 8388608 | tf_op jit(solution)/shard_map/all_to_all | solution.py:46
  11.2 38.1 %copy-start.13 = (bf16[384,256]{0,1:T(8,128)(2,1)}, bf16[384,256]{0,1:T(8,128)(2,1)S(1)}, u32[]{:S(2)}) copy-start(bf16[384,256]{0,1:T(8,128)(2,1)S(1)} %copy.42) | copy-start | bytes 589828
  11.2 66.2 %copy-start.24 = (f32[256,1]{0,1:T(1,128)}, f32[256,1]{0,1:T(1,128)S(1)}, u32[]{:S(2)}) copy-start(f32[256,1]{0,1:T(1,128)S(1)} %bitcast_convert_fusion) | copy-start | bytes 3076
  11.5 40.6 %copy-start.7 = (bf16[384,256]{0,1:T(8,128)(2,1)}, bf16[384,256]{0,1:T(8,128)(2,1)S(1)}, u32[]{:S(2)}) copy-start(bf16[384,256]{0,1:T(8,128)(2,1)S(1)} %copy.40) | copy-start | bytes 589828
  13.2 34.8 %collective-permute-start.10 = (bf16[1,304,384]{2,1,0:T(8,128)(2,1)S(1)}, bf16[1,304,384]{2,1,0:T(8,128)(2,1)S(1)}, u32[]{:S(2)}, u32[]{:S(2)}) collective-permute-start(bf16[1,304,384]{2,1,0:T(8,128)(2,1)S(1)} %broadcast_select_fusion), channel_id=1, source_target_pairs={{0,20},{1,21},{2,22},{3,23},{4,16},{5,17},{6,18},{7,19},{8,28},{9,... | collective-permute-start | bytes 700424 | tf_op jit(solution)/shard_map/ppermute | solution.py:458
  19.0 29.0 %collective-permute-start.8 = (bf16[1,304,384]{2,1,0:T(8,128)(2,1)S(1)}, bf16[1,304,384]{2,1,0:T(8,128)(2,1)S(1)}, u32[]{:S(2)}, u32[]{:S(2)}) collective-permute-start(bf16[1,304,384]{2,1,0:T(8,128)(2,1)S(1)} %broadcast_select_fusion), channel_id=1, source_target_pairs={{0,4},{1,5},{2,6},{3,7},{4,0},{5,1},{6,2},{7,3},{8,12},{9,13},{10,... | collective-permute-start | bytes 700424 | tf_op jit(solution)/shard_map/ppermute | solution.py:458
  19.3 28.7 %collective-permute-start.9 = (bf16[1,304,384]{2,1,0:T(8,128)(2,1)S(1)}, bf16[1,304,384]{2,1,0:T(8,128)(2,1)}, u32[]{:S(2)}, u32[]{:S(2)}) collective-permute-start(bf16[1,304,384]{2,1,0:T(8,128)(2,1)S(1)} %broadcast_select_fusion), channel_id=1, source_target_pairs={{0,16},{1,17},{2,18},{3,19},{4,20},{5,21},{6,22},{7,23},{8,24},{9,... | collective-permute-start | bytes 700424 | tf_op jit(solution)/shard_map/ppermute | solution.py:458
  49.4 2.7 collective-permute-start.11
  58.1 12.3 %all-to-all-start = ((bf16[4,304,384]{2,1,0:T(8,128)(2,1)}), bf16[4,304,384]{2,1,0:T(8,128)(2,1)S(1)}, u32[]{:S(2)}, u32[]{:S(2)}) async-start(bf16[4,304,384]{2,1,0:T(8,128)(2,1)} %mid_forward.4), calls=%async_computation | async-start | bytes 1867776 | tf_op jit(solution)/shard_map/cond/branch_0_fun/all_to_all | solution.py:46
  72.0 5.3 %collective-permute-start.12 = (bf16[256,384]{1,0:T(8,128)(2,1)S(1)}, bf16[256,384]{1,0:T(8,128)(2,1)S(1)}, u32[]{:S(2)}, u32[]{:S(2)}) collective-permute-start(bf16[256,384]{1,0:T(8,128)(2,1)S(1)} %get-tuple-element.231), channel_id=1, source_target_pairs={{0,32},{96,64},{1,33},{97,65},{2,34},{98,66},{3,35},{99,67},{4,36}... | collective-permute-start | bytes 589832 | tf_op jit(solution)/shard_map/ppermute | solution.py:440
  78.5 1.3 collective-permute-start.13
  83.2 2.0 collective-permute-start.15
  83.9 1.3 collective-permute-start.14
  85.2 209.8 %copy-start.23 = (bf16[32,384]{1,0:T(8,128)(2,1)S(1)}, bf16[32,384]{1,0:T(8,128)(2,1)}, u32[]{:S(2)}) copy-start(bf16[32,384]{1,0:T(8,128)(2,1)} %copy-done.22) | copy-start | bytes 73732
  87.2 215.3 %copy-start.29 = (f32[1,384]{1,0:T(1,128)S(1)}, f32[1,384]{1,0:T(1,128)}, u32[]{:S(2)}) copy-start(f32[1,384]{1,0:T(1,128)} %copy-done.28) | copy-start | bytes 4612
  87.2 215.3 %copy-start.33 = (f32[1,384]{1,0:T(1,128)S(1)}, f32[1,384]{1,0:T(1,128)}, u32[]{:S(2)}) copy-start(f32[1,384]{1,0:T(1,128)} %copy-done.32) | copy-start | bytes 4612
  87.2 216.8 %copy-start.4 = (bf16[256,384]{1,0:T(8,128)(2,1)S(1)}, bf16[256,384]{1,0:T(8,128)(2,1)}, u32[]{:S(2)}) copy-start(bf16[256,384]{1,0:T(8,128)(2,1)} %copy-done.3) | copy-start | bytes 589828
  87.2 216.8 %copy-start.8 = (bf16[384,256]{0,1:T(8,128)(2,1)S(1)}, bf16[384,256]{0,1:T(8,128)(2,1)}, u32[]{:S(2)}) copy-start(bf16[384,256]{0,1:T(8,128)(2,1)} %copy-done.7) | copy-start | bytes 589828
  87.2 216.8 %copy-start.10 = (bf16[256,384]{1,0:T(8,128)(2,1)S(1)}, bf16[256,384]{1,0:T(8,128)(2,1)}, u32[]{:S(2)}) copy-start(bf16[256,384]{1,0:T(8,128)(2,1)} %copy-done.9) | copy-start | bytes 589828
  87.2 205.9 %collective-permute-start.16 = (bf16[256,384]{1,0:T(8,128)(2,1)}, bf16[256,384]{1,0:T(8,128)(2,1)S(1)}, u32[]{:S(2)}, u32[]{:S(2)}) collective-permute-start(bf16[256,384]{1,0:T(8,128)(2,1)} %get-tuple-element.242), channel_id=1, source_target_pairs={{32,0},{33,1},{34,2},{35,3},{36,4},{37,5},{38,6},{39,7},{40,8},{41... | collective-permute-start | bytes 589832 | tf_op jit(solution)/shard_map/ppermute | solution.py:440
  295.0 1.3 collective-permute-start.17
  297.1 15.6 %all-to-all-start.16 = ((bf16[16,32,384]{2,1,0:T(8,128)(2,1)}), bf16[16,32,384]{2,1,0:T(8,128)(2,1)S(1)}, u32[]{:S(2)}, u32[]{:S(2)}) async-start(bf16[16,32,384]{2,1,0:T(8,128)(2,1)} %broadcast_in_dim.12), calls=%async_computation.16 | async-start | bytes 786432 | tf_op jit(solution)/shard_map/all_to_all | solution.py:46
  (18 other events, 63.0 us)

commit v5 on v4

--- a/solution.py
+++ b/solution.py
@@ -14,7 +14,7 @@
 F32 = jnp.float32
 VM = pl.BlockSpec(memory_space=pltpu.VMEM)
 SM = pl.BlockSpec(memory_space=pltpu.SMEM)
-PARAMS = pltpu.CompilerParams(vmem_limit_bytes=48 << 20)
+PARAMS = pltpu.CompilerParams(vmem_limit_bytes=24 << 20)
 
 
 def place(x, y, c):
@@ -128,22 +128,30 @@
     fill(sent, scaled, tail_of(ranks, eight(column_sum(values, values))))
 
 
-def mid_forward(info, got, other, weight, sent, joined):
-    cols, rank = weight.shape[2], got.shape[1] - weight.shape[2] - 16
-    core = info[0]
-
+def turn_rows(got, cols, turned):
     @pl.when(pl.program_id(0) == 0)
     def _():
-        for y in range(YS):
-            mine = pl.multiple_of((y * CS + core) * cols, cols)
-            theirs = pl.multiple_of((y * CS + 1 - core) * cols, cols)
-            joined[pl.ds(mine, cols)] = got[y, :cols]
-            joined[pl.ds(theirs, cols)] = other[y, :cols]
-
-    sent[0, :cols] = dot(weight[0].T, joined[...]).astype(BF)
+        turned[...] = got[:, :cols].reshape(got.shape[0] * cols, got.shape[2]).T
+
+
+def mid_forward_own(info, got, weight, total, turned):
+    cols = weight.shape[-1]
+    turn_rows(got, cols, turned)
+    for i in range(total.shape[0]):
+        total[i] = dot(turned[...], weight[i].reshape(YS * cols, cols))
+
+
+def mid_forward(info, got, other, weight, total, sent, turned):
+    cols = weight.shape[-1]
+    rank = got.shape[1] - cols - 16
+    turn_rows(other, cols, turned)
     ranks, rows = extras(got, cols, rank)
     ranks_o, rows_o = extras(other, cols, rank)
-    sent[0, cols:] = tail_of(ranks + ranks_o, rows + rows_o)
+    tail = tail_of(ranks + ranks_o, rows + rows_o)
+    for i in range(sent.shape[0]):
+        both = total[i] + dot(turned[...], weight[i].reshape(YS * cols, cols))
+        sent[i, :cols] = both.astype(BF).T
+        sent[i, cols:] = tail
 
 
 def finish(width, got, current, b_turned, member, result, frozen, down_raw, inverse, down, store):
@@ -199,27 +207,37 @@
     fill(sent, kept, tail_of(ranks, jnp.zeros((8, kept.shape[1]), F32)))
 
 
-def row_product(got, weight, cols):
-    total = dot(weight[0, 0, 0], got[0, :cols])
-    for j in range(1, XS):
-        total = total + dot(weight[j, 0, 0], got[j, :cols])
-    return total
+def row_product(got, weight):
+    chips, cols = weight.shape[1], weight.shape[-1]
+    total = None
+    for j in range(XS):
+        part = dot(weight[j].reshape(chips * cols, cols), got[j, :cols])
+        total = part if total is None else total + part
+    return total.reshape(chips, cols, total.shape[1])
 
 
 def mid_backward_other(info, got, weight, sent):
     cols = weight.shape[-1]
-    sent[0, :cols] = row_product(got, weight, cols).astype(BF)
-    sent[0, cols:] = tail_of(*extras(got, cols, got.shape[1] - cols - 16))
-
-
-def mid_backward_own(info, got, weight, other, sent):
-    cols = weight.shape[-1]
+    main = row_product(got, weight).astype(BF)
+    tail = tail_of(*extras(got, cols, got.shape[1] - cols - 16))
+    for j in range(sent.shape[0]):
+        sent[j, :cols] = main[j]
+        sent[j, cols:] = tail
+
+
+def mid_backward_own(info, got, weight, total):
+    total[...] = row_product(got, weight)
+
+
+def mid_backward(got, total, other, sent):
+    cols = total.shape[1]
     rank = got.shape[1] - cols - 16
-    total = row_product(got, weight, cols) + other[0, :cols].astype(F32)
-    sent[0, :cols] = total.astype(BF)
     ranks, rows = extras(got, cols, rank)
-    ranks_o, rows_o = extras(other, cols, rank)
-    sent[0, cols:] = tail_of(ranks + ranks_o, rows + rows_o)
+    ranks_o, rows_o = extras(other[:1], cols, rank)
+    tail = tail_of(ranks + ranks_o, rows + rows_o)
+    for j in range(sent.shape[0]):
+        sent[j, :cols] = (total[j] + other[j, :cols].astype(F32)).astype(BF)
+        sent[j, cols:] = tail
 
 
 def add_up(got, total, ranks):
@@ -287,8 +305,10 @@
     )
 
 
-def ranks_of(grad, b_flat, member, ranks):
-    ranks[...] = select_rank(dot(b_flat[...], grad[...]), member, ranks.shape[0])
+def ranks_of(flag, received, others, b_flat, member, grad, ranks):
+    kept = jnp.where(flag[0] > 0, received[...].astype(F32), others[...].astype(F32)).astype(BF)
+    grad[...] = kept
+    ranks[...] = select_rank(dot(b_flat[...], kept), member, ranks.shape[0])
 
 
 def outer_up(down, grad, member, grad_b, store):
@@ -313,11 +333,11 @@
     )
 
 
-def whole_call(body, name, outs, ins, scratch=(), flops=4e8):
+def whole_call(body, name, outs, ins, scratch=(), flops=4e8, scalars=0):
     return pl.pallas_call(
         body,
         out_shape=[jax.ShapeDtypeStruct(s, d) for s, d in outs],
-        in_specs=[VM] * len(ins),
+        in_specs=[SM] * scalars + [VM] * (len(ins) - scalars),
         out_specs=[VM] * len(outs),
         scratch_shapes=list(scratch),
         compiler_params=PARAMS,
@@ -356,40 +376,57 @@
     tokens = tokens_in.reshape(total, cols).T
     target = jnp.where(live[None, :], cotangent.reshape(total, cols).T, jnp.zeros((), BF))
 
-    def mid_call(body, name, weight, weight_spec, ins, whole, scratch=(), flops=8e8):
-        block_of = pl.BlockSpec((1, tall, total), lambda i, c: (i, 0, 0))
-        full = pl.BlockSpec((XS, tall, total), lambda i, c: (0, 0, 0))
-        specs = [full] * whole + [weight_spec] + [block_of] * (len(ins) - whole)
-        ins = ins[:whole] + [weight] + ins[whole:]
+    def mid_call(body, name, steps, specs, ins, out, out_rows, flops, scratch=()):
         return pl.pallas_call(
             body,
             grid_spec=pltpu.PrefetchScalarGridSpec(
                 num_scalar_prefetch=1,
-                grid=(4,),
+                grid=(steps,),
                 in_specs=specs,
-                out_specs=block_of,
+                out_specs=pl.BlockSpec((XS // steps,) + out_rows, lambda i, c: (i, 0, 0)),
                 scratch_shapes=list(scratch),
             ),
-            out_shape=jax.ShapeDtypeStruct(*payload),
+            out_shape=jax.ShapeDtypeStruct((XS,) + out_rows, out),
             compiler_params=PARAMS,
             cost_estimate=cost(flops, ins),
             name=name,
         )(info, *ins)
 
+    tall_full = pl.BlockSpec((XS, tall, total), lambda i, c: (0, 0, 0))
+
     def start_forward(current, out=payload):
         (sent,) = whole_call(pre_forward, "pre_forward", [out], [current, gain, a_flat, member])
         return sent
 
-    def product_forward(got, other):
+    def product_forward(got):
+        shape = (2, YS, 1, cols, cols)
+        other = swap_cores(got)
+        own = mid_call(
+            mid_forward_own,
+            "mid_forward_own",
+            2,
+            [tall_full, pl.BlockSpec(shape, lambda i, c: (i, 0, c[0], 0, 0))],
+            [got, halves],
+            F32,
+            (total, cols),
+            8e8,
+            [pltpu.VMEM((total, YS * cols), BF)],
+        )
         return mid_call(
             mid_forward,
             "mid_forward",
-            block,
-            pl.BlockSpec((1, width // XS, cols), lambda i, c: (i, 0, 0)),
-            [got, other],
             2,
-            [pltpu.VMEM((width // XS, total), BF)],
-            flops=16e8,
+            [
+                tall_full,
+                tall_full,
+                pl.BlockSpec(shape, lambda i, c: (i, 0, 1 - c[0], 0, 0)),
+                pl.BlockSpec((2, total, cols), lambda i, c: (i, 0, 0)),
+            ],
+            [got, other, halves, own],
+            BF,
+            (tall, total),
+            8e8,
+            [pltpu.VMEM((total, YS * cols), BF)],
         )
 
     def end_forward(got, current):
@@ -403,26 +440,34 @@
 
     def forward(current):
         got = exchange(start_forward(current), APART)
-        return exchange(product_forward(got, swap_cores(got)), BLOCKS)
+        return exchange(product_forward(got), BLOCKS)
 
     def product_backward(got):
-        shape = (XS, 1, 1, cols, cols)
+        shape = (XS, 2, 1, cols, cols)
         other = mid_call(
             mid_backward_other,
             "mid_backward_other",
-            halves,
-            pl.BlockSpec(shape, lambda i, c: (0, i, 1 - c[0], 0, 0)),
-            [got],
-            1,
-        )
-        return mid_call(
+            2,
+            [tall_full, pl.BlockSpec(shape, lambda i, c: (0, i, 1 - c[0], 0, 0))],
+            [got, halves],
+            BF,
+            (tall, total),
+            8e8,
+        )
+        own = mid_call(
             mid_backward_own,
             "mid_backward_own",
-            halves,
-            pl.BlockSpec(shape, lambda i, c: (0, i, c[0], 0, 0)),
-            [got, swap_cores(other)],
-            1,
-        )
+            2,
+            [tall_full, pl.BlockSpec(shape, lambda i, c: (0, i, c[0], 0, 0))],
+            [got, halves],
+            F32,
+            (cols, total),
+            8e8,
+        )
+        (sent,) = whole_call(
+            mid_backward, "mid_backward", [payload], [got, own, swap_cores(other)], flops=1e6
+        )
+        return sent
 
     def backward(got):
         return exchange(product_backward(got), APART)
@@ -459,10 +504,9 @@
     turns = jnp.concatenate(turns)
     own = jnp.where(gather, at_x // 2 * 2 + at_y // 2, at_x % 2 * 2 + at_y % 2)
     got = jnp.stack([lax.dynamic_index_in_dim(turns, own ^ j, 0, False) for j in range(4)])
-    other = swap_cores(got)
 
     def run_first():
-        outs = end_forward(exchange(product_forward(got, other), BLOCKS), tokens)
+        outs = end_forward(exchange(product_forward(got), BLOCKS), tokens)
         return [outs[0], outs[3], outs[4]] + zeros(wide, thin)
 
     def run_target():
@@ -541,8 +585,14 @@
     def choose(*values):
         return lax.select_n(section.astype(jnp.int32), *values)
 
-    grad = choose(grad_0, grad_1, grad_2, target)
-    (ranks,) = whole_call(ranks_of, "ranks_of", [thin], [grad, b_flat, member])
+    others = choose(target, grad_1, grad_2, target)
+    grad, ranks = whole_call(
+        ranks_of,
+        "ranks_of",
+        [main, thin],
+        [(section == 0).astype(jnp.int32).reshape(1), grad_0, others, b_flat, member],
+        scalars=1,
+    )
     ranks = (ranks + swap_cores(ranks)).astype(BF)
     ranks = exchange(jnp.broadcast_to(ranks[None], (XS * YS,) + ranks.shape), ALONG_XY)
     current = choose(tokens, received, second, third)

time: 316 us -> 299 us (0.946)
  waiting for transfers between devices: 252 us -> 234 us
    ppermute x5, waiting for transfers between devices: 207 us -> 188 us  [hop(): return lax.ppermute(value, 'section', pairs)]
    transpose x0 -> x1, local copies, waits for them, and re-layouts: none -> 4.58 us  [on_device(): base_weight[0].reshape(2, 2, 2, 2, CS * cols, cols)]
    ppermute x3, waiting for transfers between devices: 28.2 us -> 31.7 us  [on_device(): turns.append(lax.ppermute(first, ('section', 'dp'), pairs))]
    another operation x19 -> x18, local copies, waits for them, and re-layouts: 10.7 us -> 8.73 us
  transfers between devices with their start and end apart: 13 -> 13, of which waited for: 7 -> 7; matrix products, arithmetic and copies ran while one was open for 2% -> 3% of each run, Pallas kernels for 1% -> 2%
where the time goes in v5:
time: 299 us; the launch traced here: 298 us
  waiting for transfers between devices  234 us (78%)
  starting transfers between devices  26.3 us (9%)
  local copies, waits for them, and re-layouts  16.5 us (6%)
  Pallas kernels  14.2 us (5%)
  other arithmetic  6.26 us (2%)
    ppermute x5, waiting for transfers between devices, hop(): return lax.ppermute(value, 'section', pairs)  188 us
    ppermute x3, waiting for transfers between devices, on_device(): turns.append(lax.ppermute(first, ('section', 'dp'), pairs))  31.7 us
    all_to_all x3, waiting for transfers between devices, exchange(): return lax.all_to_all(chunks, 'dp', 0, 0, axis_index_groups=groups)  13.7 us
    all_to_all x3, starting transfers between devices, exchange(): return lax.all_to_all(chunks, 'dp', 0, 0, axis_index_groups=groups)  13.6 us
    another operation x18, local copies, waits for them, and re-layouts  8.73 us
    pallas_call x6, Pallas kernels, whole_call(): pl.pallas_call(body, out_shape=[jax.ShapeDtypeStruct(s, d) for s, d in ou...  7.94 us
    ppermute x3, starting transfers between devices, on_device(): turns.append(lax.ppermute(first, ('section', 'dp'), pairs))  6.58 us
    pallas_call x2, Pallas kernels, mid_call(): pl.pallas_call(body, grid_spec=pltpu.PrefetchScalarGridSpec(num_scalar_pr...  6.3 us
  transfers between devices with their start and end apart: 13, of which 7 were waited for; matrix products, arithmetic and copies ran while one was open for 3% of the time, Pallas kernels for 2%

profile of v5, /device:TPU:0, one launch (start us, length us, event | category | flops | bytes accessed | tf_op | source)
XLA Modules:
  0.0 298.0 jit_solution(8384284988533292791)
XLA Ops:
  0.6 4.6 %copy.43 = bf16[2,2,2,2,512,256]{5,4,3,2,1,0:T(8,128)(2,1)} copy(bf16[2,2,2,2,512,256]{5,4,1,3,0,2:T(8,128)(2,1)} %bitcast.48) | data formatting | bytes 8388608 | tf_op jit(solution)/shard_map/transpose | solution.py:373
  5.2 5.0 %all-to-all-start.15 = ((bf16[4,2048,256]{2,1,0:T(8,128)(2,1)}), bf16[4,2048,256]{2,1,0:T(8,128)(2,1)}, u32[]{:S(2)}, u32[]{:S(2)}) async-start(bf16[4,2048,256]{2,1,0:T(8,128)(2,1)} %bitcast.47), calls=%async_computation.15 | async-start | bytes 8388608 | tf_op jit(solution)/shard_map/all_to_all | solution.py:46
  13.1 3.2 %collective-permute-start.10 = (bf16[1,304,384]{2,1,0:T(8,128)(2,1)S(1)}, bf16[1,304,384]{2,1,0:T(8,128)(2,1)S(1)}, u32[]{:S(2)}, u32[]{:S(2)}) collective-permute-start(bf16[1,304,384]{2,1,0:T(8,128)(2,1)S(1)} %broadcast_select_fusion), channel_id=1, source_target_pairs={{0,16},{1,17},{2,18},{3,19},{4,20},{5,21},{6,22},{7,23},{8,24},{9,... | collective-permute-start | bytes 700424 | tf_op jit(solution)/shard_map/ppermute | solution.py:503
  16.3 3.1 %collective-permute-start.11 = (bf16[1,304,384]{2,1,0:T(8,128)(2,1)S(1)}, bf16[1,304,384]{2,1,0:T(8,128)(2,1)S(1)}, u32[]{:S(2)}, u32[]{:S(2)}) collective-permute-start(bf16[1,304,384]{2,1,0:T(8,128)(2,1)S(1)} %broadcast_select_fusion), channel_id=1, source_target_pairs={{0,20},{1,21},{2,22},{3,23},{4,16},{5,17},{6,18},{7,19},{8,28},{9,... | collective-permute-start | bytes 700424 | tf_op jit(solution)/shard_map/ppermute | solution.py:503
  19.6 26.5 %collective-permute-done.10 = bf16[1,304,384]{2,1,0:T(8,128)(2,1)S(1)} collective-permute-done((bf16[1,304,384]{2,1,0:T(8,128)(2,1)S(1)}, bf16[1,304,384]{2,1,0:T(8,128)(2,1)S(1)}, u32[]{:S(2)}, u32[]{:S(2)}) %collective-permute-start.10) | collective-permute-done | bytes 233504 | tf_op jit(solution)/shard_map/ppermute | solution.py:503
  46.2 5.1 %collective-permute-done.11 = bf16[1,304,384]{2,1,0:T(8,128)(2,1)S(1)} collective-permute-done((bf16[1,304,384]{2,1,0:T(8,128)(2,1)S(1)}, bf16[1,304,384]{2,1,0:T(8,128)(2,1)S(1)}, u32[]{:S(2)}, u32[]{:S(2)}) %collective-permute-start.11) | collective-permute-done | bytes 233504 | tf_op jit(solution)/shard_map/ppermute | solution.py:503
  52.7 20.3 %conditional.4 = (bf16[256,384]{1,0:T(8,128)(2,1)S(1)}, f32[1,384]{1,0:T(1,128)S(1)}, bf16[32,384]{1,0:T(8,128)(2,1)S(1)}, f32[256,384]{1,0:T(8,128)S(1)}, f32[32,384]{1,0:T(8,128)S(1)}) conditional(s32[]{:T(128)} %clamp.2, (bf16[4,304,384]{2,1,0:T(8,128)(2,1)S(1)}, s32[1]{0:T(128)}, ...), branch_computations={%region_4.5_spmd, %region_5.6_spmd, %region_6.7_spmd, %region_7.8_... | conditional | flops 2000999936 | bytes 29078170 | solution.py:489
  52.8 2.7 mid_forward_own.4.total
  55.5 3.6 %mid_forward.4 = bf16[4,304,384]{2,1,0:T(8,128)(2,1)} custom-call(s32[1]{0:T(128)} %get-tuple-element.120.info, bf16[4,304,384]{2,1,0:T(8,128)(2,1)S(1)} %get-tuple-element.121.got, bf16[4,304,384]{2,1,0:T(8,128)(2,1)S(1)} %collective-permute-done.other, bf16[4,4,2,256,256]{4,3,2,1,0:T(8,128)(2,1)} %get-tuple-element.122.weight, ...), custom_call_target="tpu_custom_call" | custom-call | flops 800000000 | bytes 7634944 | tf_op jit(solution)/shard_map/cond/branch_0_fun/mid_forward/pallas_call | solution.py:380
  59.2 3.5 %all-to-all-start = ((bf16[4,304,384]{2,1,0:T(8,128)(2,1)}), bf16[4,304,384]{2,1,0:T(8,128)(2,1)S(1)}, u32[]{:S(2)}, u32[]{:S(2)}) async-start(bf16[4,304,384]{2,1,0:T(8,128)(2,1)} %mid_forward.4), calls=%async_computation | async-start | bytes 1867776 | tf_op jit(solution)/shard_map/cond/branch_0_fun/all_to_all | solution.py:46
  63.3 8.1 %all-to-all-done.refs_0_ = bf16[4,304,384]{2,1,0:T(8,128)(2,1)S(1)} async-done(((bf16[4,304,384]{2,1,0:T(8,128)(2,1)}), bf16[4,304,384]{2,1,0:T(8,128)(2,1)S(1)}, u32[]{:S(2)}, u32[]{:S(2)}) %all-to-all-start) | async-done | bytes 933920 | tf_op jit(solution)/shard_map/cond/branch_0_fun/all_to_all | solution.py:46
  71.5 1.5 post_forward.3
  73.1 1.3 collective-permute-start.12
  74.4 5.1 %collective-permute-done.12 = bf16[256,384]{1,0:T(8,128)(2,1)S(1)} collective-permute-done((bf16[256,384]{1,0:T(8,128)(2,1)S(1)}, bf16[256,384]{1,0:T(8,128)(2,1)S(1)}, u32[]{:S(2)}, u32[]{:S(2)}) %collective-permute-start.12) | collective-permute-done | bytes 196640 | tf_op jit(solution)/shard_map/ppermute | solution.py:485
  79.5 4.1 %conditional.5 = (bf16[256,384]{1,0:T(8,128)(2,1)}, f32[256,384]{1,0:T(8,128)}, f32[32,384]{1,0:T(8,128)}, f32[1,384]{1,0:T(1,128)}, bf16[32,384]{1,0:T(8,128)(2...) conditional(s32[]{:T(128)} %clamp.2, () %tuple.76, ...), branch_computations={%region_8.9_spmd, %region_9.10_spmd, %region_10.11_spmd, %region_1... | conditional | flops 2400999936 | bytes 27331720 | solution.py:489
  83.6 1.3 collective-permute-start.13
  85.0 3.3 %conditional.6 = (bf16[256,384]{1,0:T(8,128)(2,1)}, f32[1,384]{1,0:T(1,128)}, bf16[32,384]{1,0:T(8,128)(2,1)}, bf16[256,384]{1,0:T(8,128)(2,1)}, bf16[256,384]{1,0:T(8,128)(2,1)}) conditional(s32[]{:T(128)} %clamp.2, () %tuple.80, () %tuple.81, (bf16[256,384]{1,0:T(8,128)(2,1)}, f32[256,1]{0,1:T(1,128)}, ...), branch_computations={%region_12.13_spmd, %region_13.14_spmd, %region_14.15_spmd, %regio... | conditional | flops 4400999936 | bytes 57120468 | solution.py:489
  88.9 1.4 collective-permute-start.14
  91.7 1.3 collective-permute-start.16
  95.2 182.7 %collective-permute-done.16.received = bf16[256,384]{1,0:T(8,128)(2,1)S(1)} collective-permute-done((bf16[256,384]{1,0:T(8,128)(2,1)}, bf16[256,384]{1,0:T(8,128)(2,1)S(1)}, u32[]{:S(2)}, u32[]{:S(2)}) %collective-permute-start.16) | collective-permute-done | bytes 196640 | tf_op jit(solution)/shard_map/ppermute | solution.py:485
  280.7 5.1 %all-to-all-start.16 = ((bf16[16,32,384]{2,1,0:T(8,128)(2,1)}), bf16[16,32,384]{2,1,0:T(8,128)(2,1)S(1)}, u32[]{:S(2)}, u32[]{:S(2)}) async-start(bf16[16,32,384]{2,1,0:T(8,128)(2,1)} %broadcast_in_dim.12), calls=%async_computation.16 | async-start | bytes 786432 | tf_op jit(solution)/shard_map/all_to_all | solution.py:46
  288.3 2.1 outer_up.1
  290.3 5.6 %all-to-all-done.16.got = bf16[16,32,384]{2,1,0:T(8,128)(2,1)S(1)} async-done(((bf16[16,32,384]{2,1,0:T(8,128)(2,1)}), bf16[16,32,384]{2,1,0:T(8,128)(2,1)S(1)}, u32[]{:S(2)}, u32[]{:S(2)}) %all-to-all-start.16) | async-done | bytes 393248 | tf_op jit(solution)/shard_map/all_to_all | solution.py:46
  295.9 2.1 outer_down.1
  (107 shorter events, 22.6 us)
Async XLA Ops:
  5.2 47.5 %all-to-all-start.15 = ((bf16[4,2048,256]{2,1,0:T(8,128)(2,1)}), bf16[4,2048,256]{2,1,0:T(8,128)(2,1)}, u32[]{:S(2)}, u32[]{:S(2)}) async-start(bf16[4,2048,256]{2,1,0:T(8,128)(2,1)} %bitcast.47), calls=%async_computation.15 | async-start | bytes 8388608 | tf_op jit(solution)/shard_map/all_to_all | solution.py:46
  11.1 68.5 %copy-start.18 = (f32[256,1]{0,1:T(1,128)}, f32[256,1]{0,1:T(1,128)S(1)}, u32[]{:S(2)}) copy-start(f32[256,1]{0,1:T(1,128)S(1)} %bitcast_convert_fusion) | copy-start | bytes 3076
  11.4 41.3 %copy-start.7 = (bf16[384,256]{0,1:T(8,128)(2,1)}, bf16[384,256]{0,1:T(8,128)(2,1)S(1)}, u32[]{:S(2)}) copy-start(bf16[384,256]{0,1:T(8,128)(2,1)S(1)} %copy.40) | copy-start | bytes 589828
  13.1 33.1 %collective-permute-start.10 = (bf16[1,304,384]{2,1,0:T(8,128)(2,1)S(1)}, bf16[1,304,384]{2,1,0:T(8,128)(2,1)S(1)}, u32[]{:S(2)}, u32[]{:S(2)}) collective-permute-start(bf16[1,304,384]{2,1,0:T(8,128)(2,1)S(1)} %broadcast_select_fusion), channel_id=1, source_target_pairs={{0,16},{1,17},{2,18},{3,19},{4,20},{5,21},{6,22},{7,23},{8,24},{9,... | collective-permute-start | bytes 700424 | tf_op jit(solution)/shard_map/ppermute | solution.py:503
  16.3 35.1 %collective-permute-start.11 = (bf16[1,304,384]{2,1,0:T(8,128)(2,1)S(1)}, bf16[1,304,384]{2,1,0:T(8,128)(2,1)S(1)}, u32[]{:S(2)}, u32[]{:S(2)}) collective-permute-start(bf16[1,304,384]{2,1,0:T(8,128)(2,1)S(1)} %broadcast_select_fusion), channel_id=1, source_target_pairs={{0,20},{1,21},{2,22},{3,23},{4,16},{5,17},{6,18},{7,19},{8,28},{9,... | collective-permute-start | bytes 700424 | tf_op jit(solution)/shard_map/ppermute | solution.py:503
  19.4 31.9 %collective-permute-start.9 = (bf16[1,304,384]{2,1,0:T(8,128)(2,1)S(1)}, bf16[1,304,384]{2,1,0:T(8,128)(2,1)}, u32[]{:S(2)}, u32[]{:S(2)}) collective-permute-start(bf16[1,304,384]{2,1,0:T(8,128)(2,1)S(1)} %broadcast_select_fusion), channel_id=1, source_target_pairs={{0,4},{1,5},{2,6},{3,7},{4,0},{5,1},{6,2},{7,3},{8,12},{9,13},{10,... | collective-permute-start | bytes 700424 | tf_op jit(solution)/shard_map/ppermute | solution.py:503
  52.8 2.8 collective-permute-start
  59.2 12.3 %all-to-all-start = ((bf16[4,304,384]{2,1,0:T(8,128)(2,1)}), bf16[4,304,384]{2,1,0:T(8,128)(2,1)S(1)}, u32[]{:S(2)}, u32[]{:S(2)}) async-start(bf16[4,304,384]{2,1,0:T(8,128)(2,1)} %mid_forward.4), calls=%async_computation | async-start | bytes 1867776 | tf_op jit(solution)/shard_map/cond/branch_0_fun/all_to_all | solution.py:46
  73.0 6.5 %copy-start.20 = (bf16[32,384]{1,0:T(8,128)(2,1)}, bf16[32,384]{1,0:T(8,128)(2,1)S(1)}, u32[]{:S(2)}) copy-start(bf16[32,384]{1,0:T(8,128)(2,1)S(1)} %get-tuple-element.244) | copy-start | bytes 73732
  73.1 6.5 %copy-start.25 = (f32[1,384]{1,0:T(1,128)}, f32[1,384]{1,0:T(1,128)S(1)}, u32[]{:S(2)}) copy-start(f32[1,384]{1,0:T(1,128)S(1)} %get-tuple-element.241) | copy-start | bytes 4612
  73.1 6.5 %copy-start.14 = (f32[256,384]{1,0:T(8,128)}, f32[256,384]{1,0:T(8,128)S(1)}, u32[]{:S(2)}) copy-start(f32[256,384]{1,0:T(8,128)S(1)} %get-tuple-element.229) | copy-start | bytes 1179652
  73.1 6.5 %copy-start.17 = (bf16[256,384]{1,0:T(8,128)(2,1)}, bf16[256,384]{1,0:T(8,128)(2,1)S(1)}, u32[]{:S(2)}) copy-start(bf16[256,384]{1,0:T(8,128)(2,1)S(1)} %get-tuple-element.227) | copy-start | bytes 589828
  73.1 6.4 %collective-permute-start.12 = (bf16[256,384]{1,0:T(8,128)(2,1)S(1)}, bf16[256,384]{1,0:T(8,128)(2,1)S(1)}, u32[]{:S(2)}, u32[]{:S(2)}) collective-permute-start(bf16[256,384]{1,0:T(8,128)(2,1)S(1)} %get-tuple-element.227), channel_id=1, source_target_pairs={{0,32},{96,64},{1,33},{97,65},{2,34},{98,66},{3,35},{99,67},{4,36}... | collective-permute-start | bytes 589832 | tf_op jit(solution)/shard_map/ppermute | solution.py:485
  83.6 1.3 collective-permute-start.13
  88.3 2.0 collective-permute-start.15
  88.9 1.4 collective-permute-start.14
  91.7 187.0 %copy-start.21 = (bf16[32,384]{1,0:T(8,128)(2,1)S(1)}, bf16[32,384]{1,0:T(8,128)(2,1)}, u32[]{:S(2)}) copy-start(bf16[32,384]{1,0:T(8,128)(2,1)} %copy-done.20) | copy-start | bytes 73732
  91.7 186.2 %collective-permute-start.16 = (bf16[256,384]{1,0:T(8,128)(2,1)}, bf16[256,384]{1,0:T(8,128)(2,1)S(1)}, u32[]{:S(2)}, u32[]{:S(2)}) collective-permute-start(bf16[256,384]{1,0:T(8,128)(2,1)} %get-tuple-element.238), channel_id=1, source_target_pairs={{32,0},{33,1},{34,2},{35,3},{36,4},{37,5},{38,6},{39,7},{40,8},{41... | collective-permute-start | bytes 589832 | tf_op jit(solution)/shard_map/ppermute | solution.py:485
  95.2 190.6 %copy-start.26 = (f32[1,384]{1,0:T(1,128)S(1)}, f32[1,384]{1,0:T(1,128)}, u32[]{:S(2)}) copy-start(f32[1,384]{1,0:T(1,128)} %copy-done.25) | copy-start | bytes 4612
  277.8 9.4 %copy-start.4 = (bf16[256,384]{1,0:T(8,128)(2,1)S(1)}, bf16[256,384]{1,0:T(8,128)(2,1)}, u32[]{:S(2)}) copy-start(bf16[256,384]{1,0:T(8,128)(2,1)} %copy-done.3) | copy-start | bytes 589828
  277.9 9.4 %copy-start.8 = (bf16[384,256]{0,1:T(8,128)(2,1)S(1)}, bf16[384,256]{0,1:T(8,128)(2,1)}, u32[]{:S(2)}) copy-start(bf16[384,256]{0,1:T(8,128)(2,1)} %copy-done.7) | copy-start | bytes 589828
  277.9 9.4 %copy-start.10 = (bf16[256,384]{1,0:T(8,128)(2,1)S(1)}, bf16[256,384]{1,0:T(8,128)(2,1)}, u32[]{:S(2)}) copy-start(bf16[256,384]{1,0:T(8,128)(2,1)} %copy-done.9) | copy-start | bytes 589828
  278.6 1.3 collective-permute-start.17
  280.7 15.2 %all-to-all-start.16 = ((bf16[16,32,384]{2,1,0:T(8,128)(2,1)}), bf16[16,32,384]{2,1,0:T(8,128)(2,1)S(1)}, u32[]{:S(2)}, u32[]{:S(2)}) async-start(bf16[16,32,384]{2,1,0:T(8,128)(2,1)} %broadcast_in_dim.12), calls=%async_computation.16 | async-start | bytes 786432 | tf_op jit(solution)/shard_map/all_to_all | solution.py:46
  (13 other events, 45.0 us)

commit v6 on v5

--- a/solution.py
+++ b/solution.py
@@ -323,6 +323,10 @@
     spread_rank((SCALING * ranks).astype(BF).astype(F32), member, store)
     normed = (current[...].astype(F32) * inverse[...] * gain[...]).astype(BF)
     grad_a[...] = dot(store[...], normed, ((1,), (1,)))
+
+
+def reorder(weight, block):
+    block[0, 0, 0] = weight[0, 0, :, 0]
 
 
 def cost(flops, arrays):
@@ -362,6 +366,7 @@
     b_flat = adapter_b[0].reshape(adapters * rank, cols)
     a_turned, b_turned = a_flat.T, b_flat.T
     member, live = tables_of(seg_ids, live_counts, adapters)
+    gain, a_turned, b_turned = lax.optimization_barrier((gain, a_turned, b_turned))
     info = core.astype(jnp.int32).reshape(1)
     store = pltpu.VMEM((adapters * rank, total), BF)
     payload = ((XS, tall, total), BF)
@@ -370,7 +375,18 @@
     thin = ((rank, total), F32)
     kept_outs = [main, wide, thin, ((1, total), F32), ((rank, total), BF)]
 
-    block = base_weight[0].reshape(2, 2, 2, 2, CS * cols, cols).transpose(1, 3, 0, 2, 4, 5)
+    pair = CS * cols
+    block = pl.pallas_call(
+        reorder,
+        grid=(2, 2, 2),
+        in_specs=[
+            pl.BlockSpec((1, 1, 2, 1, pair, cols), lambda p, q, i: (i, p, 0, q, 0, 0)),
+        ],
+        out_specs=pl.BlockSpec((1, 1, 1, 2, pair, cols), lambda p, q, i: (p, q, i, 0, 0, 0)),
+        out_shape=jax.ShapeDtypeStruct((2, 2, 2, 2, pair, cols), BF),
+        compiler_params=PARAMS,
+        name="reorder",
+    )(base_weight[0].reshape(2, 2, 2, 2, pair, cols))
     block = exchange(block.reshape(XS, width // XS, cols), BLOCKS)
     halves = block.reshape(XS, YS, CS, cols, cols)
     tokens = tokens_in.reshape(total, cols).T
@@ -484,11 +500,8 @@
     def hop(value, pairs):
         return lax.ppermute(value, "section", pairs)
 
-    def switch(cases, outs):
-        nothing = lambda: tuple(zeros(*outs))
-        return lax.switch(
-            section, [(lambda f=cases.get(s): tuple(f())) if s in cases else nothing for s in range(4)]
-        )
+    def only(place, work, outs):
+        return lax.cond(section == place, lambda: tuple(work()), lambda: tuple(zeros(*outs)))
 
     single = ((1, tall, total), BF)
     gather = section < 2
@@ -507,34 +520,27 @@
 
     def run_first():
         outs = end_forward(exchange(product_forward(got), BLOCKS), tokens)
-        return [outs[0], outs[3], outs[4]] + zeros(wide, thin)
+        return outs[0], outs[3], outs[4]
 
     def run_target():
-        (ahead,) = whole_call(
+        return whole_call(
             functools.partial(post_target, rank),
             "post_target",
             [main],
             [backward(got), a_turned, member, gain],
             scratch=[store],
         )
-        return [ahead] + zeros(kept_outs[3], kept_outs[4], wide, thin)
-
-    def run_ready():
-        return zeros(main, kept_outs[3], kept_outs[4]) + list(sums_of(got))
-
-    vector, inverse_0, down_0, back_first, ranks_first = switch(
-        {0: run_first, 3: run_target, 2: run_ready}, [main, kept_outs[3], kept_outs[4], wide, thin]
-    )
-    received = hop(vector, [(0, 1), (3, 2)])
-
-    def run_second():
-        return list(end_forward(forward(received), received)) + zeros(wide, thin)
-
-    def run_late():
-        return zeros(*kept_outs) + list(sums_of(exchange(plain(received), BLOCKS)))
-
-    result_1, frozen_1, raw_1, inverse_1, down_1, back_late, ranks_late = switch(
-        {1: run_second, 2: run_late}, kept_outs + [wide, thin]
+
+    brief = [main] + kept_outs[3:]
+    result_0, inverse_0, down_0 = only(0, run_first, brief)
+    first = hop(result_0, [(0, 1)])
+    (ahead,) = only(3, run_target, [main])
+    ahead = hop(ahead, [(3, 2)])
+    back_first, ranks_first = only(2, lambda: sums_of(got), [wide, thin])
+
+    back_late, ranks_late = only(2, lambda: sums_of(exchange(plain(ahead), BLOCKS)), [wide, thin])
+    result_1, frozen_1, raw_1, inverse_1, down_1 = only(
+        1, lambda: end_forward(forward(first), first), kept_outs
     )
     second = hop(result_1, [(1, 2)])
 
@@ -543,44 +549,44 @@
             functools.partial(post_forward_turn, width),
             "post_forward_turn",
             kept_outs + [payload],
-            [target, received, b_flat, forward(second), second, b_turned, member],
+            [target, ahead, b_flat, forward(second), second, b_turned, member],
             scratch=[store],
         )
         grad, grad_in = whole_call(
             functools.partial(post_turn, width),
             "post_turn",
             [main, main],
-            [backward(exchange(sent, BLOCKS)), back_first, ranks_first, back_late, ranks_late, target, received]
+            [backward(exchange(sent, BLOCKS)), back_first, ranks_first, back_late, ranks_late, target, ahead]
             + [result, second, a_turned, member, raw, inverse, gain],
             scratch=[store],
         )
         return result, inverse, down, grad, grad_in
 
-    result_2, inverse_2, down_2, grad_2, grad_in = switch(
-        {2: run_turn}, [main, kept_outs[3], kept_outs[4], main, main]
-    )
+    result_2, inverse_2, down_2, grad_2, grad_in = only(2, run_turn, brief + [main, main])
+    grad_1 = hop(grad_in, [(2, 1)])
+    grad_1, result_2 = lax.optimization_barrier((grad_1, result_2))
     third = hop(result_2, [(2, 3)])
-    grad_1 = hop(grad_in, [(2, 1)])
 
     def run_back():
         (sent,) = whole_call(
             pre_backward, "pre_backward", [payload], [grad_1, frozen_1, b_flat, member]
         )
-        (grad_in,) = whole_call(
+        return whole_call(
             functools.partial(post_backward, width),
             "post_backward",
             [main],
-            [backward(exchange(sent, BLOCKS)), grad_1, received, a_turned, member, raw_1, inverse_1, gain],
+            [backward(exchange(sent, BLOCKS)), grad_1, first, a_turned, member, raw_1, inverse_1]
+            + [gain],
             scratch=[store],
         )
-        return [grad_in] + zeros(kept_outs[3], kept_outs[4])
 
     def run_last():
         outs = end_forward(forward(third), third)
         return outs[0], outs[3], outs[4]
 
-    vector_3, inverse_3, down_3 = switch({1: run_back, 3: run_last}, [main] + kept_outs[3:])
-    grad_0 = hop(vector_3, [(1, 0)])
+    (grad_in,) = only(1, run_back, [main])
+    grad_0 = hop(grad_in, [(1, 0)])
+    result_3, inverse_3, down_3 = only(3, run_last, brief)
 
     def choose(*values):
         return lax.select_n(section.astype(jnp.int32), *values)
@@ -594,11 +600,16 @@
         scalars=1,
     )
     ranks = (ranks + swap_cores(ranks)).astype(BF)
-    ranks = exchange(jnp.broadcast_to(ranks[None], (XS * YS,) + ranks.shape), ALONG_XY)
-    current = choose(tokens, received, second, third)
-    result = choose(vector, result_1, result_2, vector_3)
-    inverse = choose(inverse_0, inverse_1, inverse_2, inverse_3)
-    down = choose(down_0, down_1, down_2, down_3)
+    ranks = jnp.broadcast_to(ranks[None], (XS * YS,) + ranks.shape)
+    saved = [
+        [tokens, first, second, third],
+        [result_0, result_1, result_2, result_3],
+        [inverse_0, inverse_1, inverse_2, inverse_3],
+        [down_0, down_1, down_2, down_3],
+    ]
+    ranks, saved = lax.optimization_barrier((ranks, saved))
+    ranks = exchange(ranks, ALONG_XY)
+    current, result, inverse, down = [choose(*values) for values in saved]
     (grad_b,) = whole_call(
         outer_up,
         "outer_up",

time: 299 us -> 299 us (level)
  waiting for transfers between devices: 234 us -> 228 us
    ppermute x5 -> x6, waiting for transfers between devices: 188 us -> 183 us  [hop(): return lax.ppermute(value, 'section', pairs)]
    transpose x1 -> x0, local copies, waits for them, and re-layouts: 4.58 us -> none  [on_device(): base_weight[0].reshape(2, 2, 2, 2, CS * cols, cols)]
    unnamed x48 -> x42, local copies, waits for them, and re-layouts: 0.79 us -> 4.3 us
    another operation x18 -> x20, local copies, waits for them, and re-layouts: 8.73 us -> 11.5 us
    ppermute x5 -> x6, starting transfers between devices: 5.95 us -> 8.07 us  [hop(): return lax.ppermute(value, 'section', pairs)]
  transfers between devices with their start and end apart: 13 -> 14, of which waited for: 7 -> 7; matrix products, arithmetic and copies ran while one was open for 3% -> 5% of each run, Pallas kernels for 2% -> 2%
where the time goes in v6:
time: 299 us; the launch traced here: 298 us
  waiting for transfers between devices  228 us (76%)
  starting transfers between devices  28.3 us (9%)
  local copies, waits for them, and re-layouts  18.2 us (6%)
  Pallas kernels  15.7 us (5%)
  other arithmetic  6.29 us (2%)
    ppermute x6, waiting for transfers between devices, hop(): return lax.ppermute(value, 'section', pairs)  183 us
    ppermute x3, waiting for transfers between devices, on_device(): turns.append(lax.ppermute(first, ('section', 'dp'), pairs))  31.7 us
    all_to_all x3, starting transfers between devices, exchange(): return lax.all_to_all(chunks, 'dp', 0, 0, axis_index_groups=groups)  13.6 us
    all_to_all x3, waiting for transfers between devices, exchange(): return lax.all_to_all(chunks, 'dp', 0, 0, axis_index_groups=groups)  12.6 us
    another operation x20, local copies, waits for them, and re-layouts  11.5 us
    ppermute x6, starting transfers between devices, hop(): return lax.ppermute(value, 'section', pairs)  8.07 us
    pallas_call x6, Pallas kernels, whole_call(): pl.pallas_call(body, out_shape=[jax.ShapeDtypeStruct(s, d) for s, d in ou...  8 us
    pallas_call x2, Pallas kernels, mid_call(): pl.pallas_call(body, grid_spec=pltpu.PrefetchScalarGridSpec(num_scalar_pr...  6.87 us
  transfers between devices with their start and end apart: 14, of which 7 were waited for; matrix products, arithmetic and copies ran while one was open for 5% of the time, Pallas kernels for 2%

profile of v6, /device:TPU:0, one launch (start us, length us, event | category | flops | bytes accessed | tf_op | source)
XLA Modules:
  0.0 297.6 jit_solution(3899743378241383469)
XLA Ops:
  0.6 2.2 copy-done.1
  3.6 2.0 copy-done
  5.7 5.0 %all-to-all-start.15 = ((bf16[4,2048,256]{2,1,0:T(8,128)(2,1)}), bf16[4,2048,256]{2,1,0:T(8,128)(2,1)}, u32[]{:S(2)}, u32[]{:S(2)}) async-start(bf16[4,2048,256]{2,1,0:T(8,128)(2,1)} %bitcast.26), calls=%async_computation.15 | async-start | bytes 8388608 | tf_op jit(solution)/shard_map/all_to_all | solution.py:46
  13.5 3.2 %collective-permute-start.10 = (bf16[1,304,384]{2,1,0:T(8,128)(2,1)S(1)}, bf16[1,304,384]{2,1,0:T(8,128)(2,1)S(1)}, u32[]{:S(2)}, u32[]{:S(2)}) collective-permute-start(bf16[1,304,384]{2,1,0:T(8,128)(2,1)S(1)} %broadcast_select_fusion), channel_id=1, source_target_pairs={{0,16},{1,17},{2,18},{3,19},{4,20},{5,21},{6,22},{7,23},{8,24},{9,... | collective-permute-start | bytes 700424 | tf_op jit(solution)/shard_map/ppermute | solution.py:516
  16.7 3.1 %collective-permute-start.11 = (bf16[1,304,384]{2,1,0:T(8,128)(2,1)S(1)}, bf16[1,304,384]{2,1,0:T(8,128)(2,1)S(1)}, u32[]{:S(2)}, u32[]{:S(2)}) collective-permute-start(bf16[1,304,384]{2,1,0:T(8,128)(2,1)S(1)} %broadcast_select_fusion), channel_id=1, source_target_pairs={{0,20},{1,21},{2,22},{3,23},{4,16},{5,17},{6,18},{7,19},{8,28},{9,... | collective-permute-start | bytes 700424 | tf_op jit(solution)/shard_map/ppermute | solution.py:516
  20.1 26.6 %collective-permute-done.10 = bf16[1,304,384]{2,1,0:T(8,128)(2,1)S(1)} collective-permute-done((bf16[1,304,384]{2,1,0:T(8,128)(2,1)S(1)}, bf16[1,304,384]{2,1,0:T(8,128)(2,1)S(1)}, u32[]{:S(2)}, u32[]{:S(2)}) %collective-permute-start.10) | collective-permute-done | bytes 233504 | tf_op jit(solution)/shard_map/ppermute | solution.py:516
  46.6 5.1 %collective-permute-done.11 = bf16[1,304,384]{2,1,0:T(8,128)(2,1)S(1)} collective-permute-done((bf16[1,304,384]{2,1,0:T(8,128)(2,1)S(1)}, bf16[1,304,384]{2,1,0:T(8,128)(2,1)S(1)}, u32[]{:S(2)}, u32[]{:S(2)}) %collective-permute-start.11) | collective-permute-done | bytes 233504 | tf_op jit(solution)/shard_map/ppermute | solution.py:516
  53.1 20.8 %conditional.8 = (bf16[256,384]{1,0:T(8,128)(2,1)}, f32[1,384]{1,0:T(1,128)}, bf16[32,384]{1,0:T(8,128)(2,1)}) conditional(s32[]{:T(128)} %convert_element_type.52, () %tuple.71, (bf16[4,304,384]{2,1,0:T(8,128)(2,1)}, s32[1]{0:T(128)}, bf16[4,4,2,256,256]{4,3,2,1,0:T(8,128)(2,1)}, bf16[256,384]{1,0:T(8,128)(2,1)S(1)}, ...), branch_computations={%region_4.5_spmd, %region_5.6_spmd} | conditional | flops 2000000000 | bytes 23674976 | solution.py:504
  53.1 3.0 mid_forward_own.4.total
  56.1 3.9 %mid_forward.4 = bf16[4,304,384]{2,1,0:T(8,128)(2,1)} custom-call(s32[1]{0:T(128)} %get-tuple-element.94.info, bf16[4,304,384]{2,1,0:T(8,128)(2,1)} %get-tuple-element.120.got, bf16[4,304,384]{2,1,0:T(8,128)(2,1)S(1)} %collective-permute-done.other, bf16[4,4,2,256,256]{4,3,2,1,0:T(8,128)(2,1)} %get-tuple-element.128.weight, ...), custom_call_target="tpu_custom_call" | custom-call | flops 800000000 | bytes 7634944 | tf_op jit(solution)/shard_map/cond/branch_1_fun/mid_forward/pallas_call | solution.py:396
  60.0 3.5 %all-to-all-start = ((bf16[4,304,384]{2,1,0:T(8,128)(2,1)}), bf16[4,304,384]{2,1,0:T(8,128)(2,1)S(1)}, u32[]{:S(2)}, u32[]{:S(2)}) async-start(bf16[4,304,384]{2,1,0:T(8,128)(2,1)} %mid_forward.4), calls=%async_computation | async-start | bytes 1867776 | tf_op jit(solution)/shard_map/cond/branch_1_fun/all_to_all | solution.py:46
  64.2 8.1 %all-to-all-done.refs_0_ = bf16[4,304,384]{2,1,0:T(8,128)(2,1)S(1)} async-done(((bf16[4,304,384]{2,1,0:T(8,128)(2,1)}), bf16[4,304,384]{2,1,0:T(8,128)(2,1)S(1)}, u32[]{:S(2)}, u32[]{:S(2)}) %all-to-all-start) | async-done | bytes 933920 | tf_op jit(solution)/shard_map/cond/branch_1_fun/all_to_all | solution.py:46
  72.3 1.6 post_forward.3
  73.9 2.0 collective-permute-start.12
  77.3 3.4 %collective-permute-done.12 = bf16[256,384]{1,0:T(8,128)(2,1)} collective-permute-done((bf16[256,384]{1,0:T(8,128)(2,1)}, bf16[256,384]{1,0:T(8,128)(2,1)}, u32[]{:S(2)}, u32[]{:S(2)}) %collective-permute-start.12) | collective-permute-done | bytes 196640 | tf_op jit(solution)/shard_map/ppermute | solution.py:501
  80.7 3.3 %conditional.9 = ((bf16[256,384]{1,0:T(8,128)(2,1)}, f32[256,384]{1,0:T(8,128)}, f32[32,384]{1,0:T(8,128)}, f32[1,384]{1,0:T(1,128)}, bf16[32,384]{1,0:T(8,128)(2,1)})) conditional(s32[]{:T(128)} %convert_element_type.53, () %tuple.70, (bf16[256,384]{1,0:T(8,128)(2,1)}, f32[256,1]{0,1:T(1,128)S(1)}, bf16[2048,256]{1,0:T(8,128)(2,1)}, ...), branch_computations={%region_6.7_spmd, %region_7.8_spmd} | conditional | flops 2400000000 | bytes 26889296 | solution.py:504
  86.1 1.4 conditional.12
  87.6 3.3 %conditional.13 = (bf16[256,384]{1,0:T(8,128)(2,1)}, f32[1,384]{1,0:T(1,128)}, bf16[32,384]{1,0:T(8,128)(2,1)}, bf16[256,384]{1,0:T(8,128)(2,1)}, bf16[256,384]{1,0:T(8,128)(2,1)}) conditional(s32[]{:T(128)} %convert_element_type.54, () %tuple.69, (bf16[256,384]{1,0:T(8,128)(2,1)}, f32[256,1]{0,1:T(1,128)S(1)}, bf16[2048,256]{1,0:T(8,128)(2,1)S(1)}, ...), branch_computations={%region_14.15_spmd, %region_15.16_spmd} | conditional | flops 4400999936 | bytes 61511436 | solution.py:504
  94.2 1.4 collective-permute-start.16
  96.8 179.7 %collective-permute-done.16.received = bf16[256,384]{1,0:T(8,128)(2,1)S(1)} collective-permute-done((bf16[256,384]{1,0:T(8,128)(2,1)}, bf16[256,384]{1,0:T(8,128)(2,1)S(1)}, u32[]{:S(2)}, u32[]{:S(2)}) %collective-permute-start.16) | collective-permute-done | bytes 196640 | tf_op jit(solution)/shard_map/ppermute | solution.py:501
  280.2 5.1 %all-to-all-start.16 = ((bf16[16,32,384]{2,1,0:T(8,128)(2,1)}), bf16[16,32,384]{2,1,0:T(8,128)(2,1)S(1)}, u32[]{:S(2)}, u32[]{:S(2)}) async-start(bf16[16,32,384]{2,1,0:T(8,128)(2,1)} %broadcast_in_dim.12), calls=%async_computation.16 | async-start | bytes 786432 | tf_op jit(solution)/shard_map/all_to_all | solution.py:46
  288.2 2.1 outer_up.1
  291.0 4.5 %all-to-all-done.16.got = bf16[16,32,384]{2,1,0:T(8,128)(2,1)S(1)} async-done(((bf16[16,32,384]{2,1,0:T(8,128)(2,1)}), bf16[16,32,384]{2,1,0:T(8,128)(2,1)S(1)}, u32[]{:S(2)}, u32[]{:S(2)}) %all-to-all-start.16) | async-done | bytes 393248 | tf_op jit(solution)/shard_map/all_to_all | solution.py:46
  295.4 2.1 outer_down.1
  (108 shorter events, 31.9 us)
Async XLA Ops:
  5.6 5.1 %copy-start.19 = (s32[2,192]{1,0:T(2,128)S(1)}, s32[2,192]{1,0:T(2,128)}, u32[]{:S(2)}) copy-start(s32[2,192]{1,0:T(2,128)} %param.30) | copy-start | bytes 4612
  5.7 5.3 %copy-start.25 = (s32[2,64]{1,0:T(2,128)S(1)}, s32[2,64]{1,0:T(2,128)}, u32[]{:S(2)}) copy-start(s32[2,64]{1,0:T(2,128)} %param.31) | copy-start | bytes 1540
  5.7 5.6 %copy-start.11 = (bf16[2,192,256]{2,1,0:T(8,128)(2,1)S(1)}, bf16[2,192,256]{2,1,0:T(8,128)(2,1)}, u32[]{:S(2)}) copy-start(bf16[2,192,256]{2,1,0:T(8,128)(2,1)} %param.25) | copy-start | bytes 589828
  5.7 5.8 %copy-start.26 = (bf16[1,256]{1,0:T(2,128)(2,1)S(1)}, bf16[1,256]{1,0:T(2,128)(2,1)}, u32[]{:S(2)}) copy-start(bf16[1,256]{1,0:T(2,128)(2,1)} %param.27) | copy-start | bytes 1540
  5.7 6.0 %copy-start.12 = (bf16[2,192,256]{2,1,0:T(8,128)(2,1)S(1)}, bf16[2,192,256]{2,1,0:T(8,128)(2,1)}, u32[]{:S(2)}) copy-start(bf16[2,192,256]{2,1,0:T(8,128)(2,1)} %param.24) | copy-start | bytes 589828
  5.7 47.5 %all-to-all-start.15 = ((bf16[4,2048,256]{2,1,0:T(8,128)(2,1)}), bf16[4,2048,256]{2,1,0:T(8,128)(2,1)}, u32[]{:S(2)}, u32[]{:S(2)}) async-start(bf16[4,2048,256]{2,1,0:T(8,128)(2,1)} %bitcast.26), calls=%async_computation.15 | async-start | bytes 8388608 | tf_op jit(solution)/shard_map/all_to_all | solution.py:46
  11.5 76.1 %copy-start.16 = (f32[256,1]{0,1:T(1,128)}, f32[256,1]{0,1:T(1,128)S(1)}, u32[]{:S(2)}) copy-start(f32[256,1]{0,1:T(1,128)S(1)} %bitcast_convert_fusion) | copy-start | bytes 3076
  11.8 41.3 %copy-start.7 = (bf16[384,256]{0,1:T(8,128)(2,1)}, bf16[384,256]{0,1:T(8,128)(2,1)S(1)}, u32[]{:S(2)}) copy-start(bf16[384,256]{0,1:T(8,128)(2,1)S(1)} %copy.38) | copy-start | bytes 589828
  13.5 33.1 %collective-permute-start.10 = (bf16[1,304,384]{2,1,0:T(8,128)(2,1)S(1)}, bf16[1,304,384]{2,1,0:T(8,128)(2,1)S(1)}, u32[]{:S(2)}, u32[]{:S(2)}) collective-permute-start(bf16[1,304,384]{2,1,0:T(8,128)(2,1)S(1)} %broadcast_select_fusion), channel_id=1, source_target_pairs={{0,16},{1,17},{2,18},{3,19},{4,20},{5,21},{6,22},{7,23},{8,24},{9,... | collective-permute-start | bytes 700424 | tf_op jit(solution)/shard_map/ppermute | solution.py:516
  16.7 35.1 %collective-permute-start.11 = (bf16[1,304,384]{2,1,0:T(8,128)(2,1)S(1)}, bf16[1,304,384]{2,1,0:T(8,128)(2,1)S(1)}, u32[]{:S(2)}, u32[]{:S(2)}) collective-permute-start(bf16[1,304,384]{2,1,0:T(8,128)(2,1)S(1)} %broadcast_select_fusion), channel_id=1, source_target_pairs={{0,20},{1,21},{2,22},{3,23},{4,16},{5,17},{6,18},{7,19},{8,28},{9,... | collective-permute-start | bytes 700424 | tf_op jit(solution)/shard_map/ppermute | solution.py:516
  19.8 31.9 %collective-permute-start.9 = (bf16[1,304,384]{2,1,0:T(8,128)(2,1)S(1)}, bf16[1,304,384]{2,1,0:T(8,128)(2,1)S(1)}, u32[]{:S(2)}, u32[]{:S(2)}) collective-permute-start(bf16[1,304,384]{2,1,0:T(8,128)(2,1)S(1)} %broadcast_select_fusion), channel_id=1, source_target_pairs={{0,4},{1,5},{2,6},{3,7},{4,0},{5,1},{6,2},{7,3},{8,12},{9,13},{10,... | collective-permute-start | bytes 700424 | tf_op jit(solution)/shard_map/ppermute | solution.py:516
  53.1 3.0 %collective-permute-start = (bf16[4,304,384]{2,1,0:T(8,128)(2,1)}, bf16[4,304,384]{2,1,0:T(8,128)(2,1)S(1)}, u32[]{:S(2)}, u32[]{:S(2)}) collective-permute-start(bf16[4,304,384]{2,1,0:T(8,128)(2,1)} %get-tuple-element.120.got), channel_id=1, source_target_pairs={{0,1},{1,0},{2,3},{3,2},{4,5},{5,4},{6,7},{7,6},{8,9},{9,8},{10,11... | collective-permute-start | bytes 2801672 | tf_op jit(solution)/shard_map/cond/branch_1_fun/ppermute | solution.py:50
  60.0 12.3 %all-to-all-start = ((bf16[4,304,384]{2,1,0:T(8,128)(2,1)}), bf16[4,304,384]{2,1,0:T(8,128)(2,1)S(1)}, u32[]{:S(2)}, u32[]{:S(2)}) async-start(bf16[4,304,384]{2,1,0:T(8,128)(2,1)} %mid_forward.4), calls=%async_computation | async-start | bytes 1867776 | tf_op jit(solution)/shard_map/cond/branch_1_fun/all_to_all | solution.py:46
  73.9 6.7 %collective-permute-start.12 = (bf16[256,384]{1,0:T(8,128)(2,1)}, bf16[256,384]{1,0:T(8,128)(2,1)}, u32[]{:S(2)}, u32[]{:S(2)}) collective-permute-start(bf16[256,384]{1,0:T(8,128)(2,1)} %get-tuple-element.272), channel_id=1, source_target_pairs={{0,32},{1,33},{2,34},{3,35},{4,36},{5,37},{6,38},{7,39},{8,40},{9,... | collective-permute-start | bytes 589832 | tf_op jit(solution)/shard_map/ppermute | solution.py:501
  76.6 9.5 %collective-permute-start.14 = (bf16[256,384]{1,0:T(8,128)(2,1)}, bf16[256,384]{1,0:T(8,128)(2,1)S(1)}, u32[]{:S(2)}, u32[]{:S(2)}) collective-permute-start(bf16[256,384]{1,0:T(8,128)(2,1)} %get-tuple-element.498), channel_id=1, source_target_pairs={{96,64},{97,65},{98,66},{99,67},{100,68},{101,69},{102,70},{103,71... | collective-permute-start | bytes 589832 | tf_op jit(solution)/shard_map/ppermute | solution.py:501
  84.0 3.6 %collective-permute-start.13 = (bf16[256,384]{1,0:T(8,128)(2,1)}, bf16[256,384]{1,0:T(8,128)(2,1)}, u32[]{:S(2)}, u32[]{:S(2)}) collective-permute-start(bf16[256,384]{1,0:T(8,128)(2,1)} %get-tuple-element.273), channel_id=1, source_target_pairs={{32,64},{33,65},{34,66},{35,67},{36,68},{37,69},{38,70},{39,71},{4... | collective-permute-start | bytes 589832 | tf_op jit(solution)/shard_map/ppermute | solution.py:501
  90.8 1.4 collective-permute-start.15
  92.2 185.1 %collective-permute-start.18 = (bf16[256,384]{1,0:T(8,128)(2,1)}, bf16[256,384]{1,0:T(8,128)(2,1)}, u32[]{:S(2)}, u32[]{:S(2)}) collective-permute-start(bf16[256,384]{1,0:T(8,128)(2,1)} %get-tuple-element.274), channel_id=1, source_target_pairs={{64,96},{65,97},{66,98},{67,99},{68,100},{69,101},{70,102},{71,103... | collective-permute-start | bytes 589832 | tf_op jit(solution)/shard_map/ppermute | solution.py:501
  94.2 183.0 %copy-start.17 = (f32[256,1]{0,1:T(1,128)S(1)}, f32[256,1]{0,1:T(1,128)}, u32[]{:S(2)}) copy-start(f32[256,1]{0,1:T(1,128)} %copy-done.16) | copy-start | bytes 3076
  94.2 182.2 %collective-permute-start.16 = (bf16[256,384]{1,0:T(8,128)(2,1)}, bf16[256,384]{1,0:T(8,128)(2,1)S(1)}, u32[]{:S(2)}, u32[]{:S(2)}) collective-permute-start(bf16[256,384]{1,0:T(8,128)(2,1)} %get-tuple-element.501), channel_id=1, source_target_pairs={{32,0},{33,1},{34,2},{35,3},{36,4},{37,5},{38,6},{39,7},{40,8},{41... | collective-permute-start | bytes 589832 | tf_op jit(solution)/shard_map/ppermute | solution.py:501
  277.2 1.4 collective-permute-start.17
  279.4 7.2 %copy-start.14 = (bf16[32,384]{1,0:T(8,128)(2,1)S(1)}, bf16[32,384]{1,0:T(8,128)(2,1)}, u32[]{:S(2)}) copy-start(bf16[32,384]{1,0:T(8,128)(2,1)} %get-tuple-element.286) | copy-start | bytes 73732
  279.4 7.2 %copy-start.15 = (bf16[32,384]{1,0:T(8,128)(2,1)S(1)}, bf16[32,384]{1,0:T(8,128)(2,1)}, u32[]{:S(2)}) copy-start(bf16[32,384]{1,0:T(8,128)(2,1)} %get-tuple-element.285) | copy-start | bytes 73732
  280.2 15.2 %all-to-all-start.16 = ((bf16[16,32,384]{2,1,0:T(8,128)(2,1)}), bf16[16,32,384]{2,1,0:T(8,128)(2,1)S(1)}, u32[]{:S(2)}, u32[]{:S(2)}) async-start(bf16[16,32,384]{2,1,0:T(8,128)(2,1)} %broadcast_in_dim.12), calls=%async_computation.16 | async-start | bytes 786432 | tf_op jit(solution)/shard_map/all_to_all | solution.py:46
  (11 other events, 22.3 us)

commit v7 on v6

--- a/solution.py
+++ b/solution.py
@@ -209,10 +209,9 @@
 
 def row_product(got, weight):
     chips, cols = weight.shape[1], weight.shape[-1]
-    total = None
-    for j in range(XS):
-        part = dot(weight[j].reshape(chips * cols, cols), got[j, :cols])
-        total = part if total is None else total + part
+    left = [weight[j].reshape(chips * cols, cols) for j in range(XS)]
+    right = [got[j, :cols] for j in range(XS)]
+    total = dot(jnp.concatenate(left, axis=1), jnp.concatenate(right, axis=0))
     return total.reshape(chips, cols, total.shape[1])
 
 
@@ -311,6 +310,12 @@
     ranks[...] = select_rank(dot(b_flat[...], kept), member, ranks.shape[0])
 
 
+def both_cores(ranks, other, sent):
+    both = (ranks[...] + other[...]).astype(BF)
+    for j in range(sent.shape[0]):
+        sent[j] = both
+
+
 def outer_up(down, grad, member, grad_b, store):
     spread_rank(SCALING * down[...].astype(F32), member, store)
     grad_b[...] = dot(store[...], grad[...], ((1,), (1,)))
@@ -329,12 +334,22 @@
     block[0, 0, 0] = weight[0, 0, :, 0]
 
 
+def bring(block, kept, sem):
+    copy = pltpu.make_async_copy(block, kept, sem)
+    copy.start()
+    copy.wait()
+
+
 def cost(flops, arrays):
     return pl.CostEstimate(
         flops=int(flops),
         bytes_accessed=sum(x.size * x.dtype.itemsize for x in arrays),
         transcendentals=0,
     )
+
+
+def held(value):
+    return pltpu.with_memory_space_constraint(value, pltpu.VMEM)
 
 
 def whole_call(body, name, outs, ins, scratch=(), flops=4e8, scalars=0):
@@ -414,7 +429,19 @@
         (sent,) = whole_call(pre_forward, "pre_forward", [out], [current, gain, a_flat, member])
         return sent
 
-    def product_forward(got):
+    def near(value):
+        return pl.pallas_call(
+            bring,
+            out_shape=pltpu.VMEM(value.shape, value.dtype),
+            in_specs=[pl.BlockSpec(memory_space=pl.ANY)],
+            out_specs=VM,
+            scratch_shapes=[pltpu.SemaphoreType.DMA],
+            compiler_params=PARAMS,
+            cost_estimate=cost(8e8, [value]),
+            name="bring",
+        )(value)
+
+    def product_forward(got, held=held):
         shape = (2, YS, 1, cols, cols)
         other = swap_cores(got)
         own = mid_call(
@@ -422,7 +449,7 @@
             "mid_forward_own",
             2,
             [tall_full, pl.BlockSpec(shape, lambda i, c: (i, 0, c[0], 0, 0))],
-            [got, halves],
+            [got, held(halves)],
             F32,
             (total, cols),
             8e8,
@@ -438,7 +465,7 @@
                 pl.BlockSpec(shape, lambda i, c: (i, 0, 1 - c[0], 0, 0)),
                 pl.BlockSpec((2, total, cols), lambda i, c: (i, 0, 0)),
             ],
-            [got, other, halves, own],
+            [got, other, held(halves), own],
             BF,
             (tall, total),
             8e8,
@@ -458,14 +485,14 @@
         got = exchange(start_forward(current), APART)
         return exchange(product_forward(got), BLOCKS)
 
-    def product_backward(got):
+    def product_backward(got, held=held):
         shape = (XS, 2, 1, cols, cols)
         other = mid_call(
             mid_backward_other,
             "mid_backward_other",
             2,
             [tall_full, pl.BlockSpec(shape, lambda i, c: (0, i, 1 - c[0], 0, 0))],
-            [got, halves],
+            [got, held(halves)],
             BF,
             (tall, total),
             8e8,
@@ -475,7 +502,7 @@
             "mid_backward_own",
             2,
             [tall_full, pl.BlockSpec(shape, lambda i, c: (0, i, c[0], 0, 0))],
-            [got, halves],
+            [got, held(halves)],
             F32,
             (cols, total),
             8e8,
@@ -485,14 +512,14 @@
         )
         return sent
 
-    def backward(got):
-        return exchange(product_backward(got), APART)
+    def backward(got, held=held):
+        return exchange(product_backward(got, held), APART)
 
     def plain(vector, out=payload):
         return whole_call(pre_plain, "pre_plain", [out], [vector, b_flat, member])[0]
 
     def sums_of(got):
-        return whole_call(add_up, "add_up", [wide, thin], [backward(got)])
+        return whole_call(add_up, "add_up", [wide, thin], [backward(got, lambda x: x)])
 
     def zeros(*kinds):
         return [jnp.zeros(*kind) for kind in kinds]
@@ -519,7 +546,7 @@
     got = jnp.stack([lax.dynamic_index_in_dim(turns, own ^ j, 0, False) for j in range(4)])
 
     def run_first():
-        outs = end_forward(exchange(product_forward(got), BLOCKS), tokens)
+        outs = end_forward(exchange(product_forward(got, lambda x: x), BLOCKS), tokens)
         return outs[0], outs[3], outs[4]
 
     def run_target():
@@ -527,7 +554,7 @@
             functools.partial(post_target, rank),
             "post_target",
             [main],
-            [backward(got), a_turned, member, gain],
+            [backward(got, lambda x: x), a_turned, member, gain],
             scratch=[store],
         )
 
@@ -539,6 +566,8 @@
     back_first, ranks_first = only(2, lambda: sums_of(got), [wide, thin])
 
     back_late, ranks_late = only(2, lambda: sums_of(exchange(plain(ahead), BLOCKS)), [wide, thin])
+    halves, back_first = lax.optimization_barrier((halves, back_first))
+    halves = near(halves)
     result_1, frozen_1, raw_1, inverse_1, down_1 = only(
         1, lambda: end_forward(forward(first), first), kept_outs
     )
@@ -592,6 +621,7 @@
         return lax.select_n(section.astype(jnp.int32), *values)
 
     others = choose(target, grad_1, grad_2, target)
+    others, result_3 = lax.optimization_barrier((others, result_3))
     grad, ranks = whole_call(
         ranks_of,
         "ranks_of",
@@ -599,8 +629,13 @@
         [(section == 0).astype(jnp.int32).reshape(1), grad_0, others, b_flat, member],
         scalars=1,
     )
-    ranks = (ranks + swap_cores(ranks)).astype(BF)
-    ranks = jnp.broadcast_to(ranks[None], (XS * YS,) + ranks.shape)
+    (ranks,) = whole_call(
+        both_cores,
+        "both_cores",
+        [((XS * YS, rank, total), BF)],
+        [ranks, swap_cores(ranks)],
+        flops=1e6,
+    )
     saved = [
         [tokens, first, second, third],
         [result_0, result_1, result_2, result_3],

time: 299 us -> 290 us (0.970)
  waiting for transfers between devices: 228 us -> 213 us
  Pallas kernels: 15.7 us -> 20.6 us
    ppermute x6, waiting for transfers between devices: 183 us -> 171 us  [hop(): return lax.ppermute(value, 'section', pairs)]
    ppermute x3, waiting for transfers between devices: 31.7 us -> 28.2 us  [on_device(): turns.append(lax.ppermute(first, ('section', 'dp'), pairs))]
    pallas_call x6 -> x7, Pallas kernels: 8 us -> 10.6 us  [whole_call(): pl.pallas_call(body, out_shape=[jax.ShapeDtypeStruct(s, d) for s, d in ou...]
    unnamed x42 -> x46, local copies, waits for them, and re-layouts: 4.3 us -> 6.83 us
  transfers between devices with their start and end apart: 14 -> 14, of which waited for: 7 -> 5; matrix products, arithmetic and copies ran while one was open for 5% -> 5% of each run, Pallas kernels for 2% -> 3%
where the time goes in v7:
time: 290 us; the launch traced here: 289 us
  waiting for transfers between devices  213 us (73%)
  starting transfers between devices  29.4 us (10%)
  Pallas kernels  20.6 us (7%)
  local copies, waits for them, and re-layouts  19.8 us (7%)
  other arithmetic  5.38 us (2%)
    ppermute x6, waiting for transfers between devices, hop(): return lax.ppermute(value, 'section', pairs)  171 us
    ppermute x3, waiting for transfers between devices, on_device(): turns.append(lax.ppermute(first, ('section', 'dp'), pairs))  28.2 us
    all_to_all x3, starting transfers between devices, exchange(): return lax.all_to_all(chunks, 'dp', 0, 0, axis_index_groups=groups)  14.1 us
    all_to_all x3, waiting for transfers between devices, exchange(): return lax.all_to_all(chunks, 'dp', 0, 0, axis_index_groups=groups)  12.7 us
    another operation x20, local copies, waits for them, and re-layouts  11.4 us
    pallas_call x7, Pallas kernels, whole_call(): pl.pallas_call(body, out_shape=[jax.ShapeDtypeStruct(s, d) for s, d in ou...  10.6 us
    ppermute x6, starting transfers between devices, hop(): return lax.ppermute(value, 'section', pairs)  8.61 us
    pallas_call x2, Pallas kernels, mid_call(): pl.pallas_call(body, grid_spec=pltpu.PrefetchScalarGridSpec(num_scalar_pr...  6.87 us
  transfers between devices with their start and end apart: 14, of which 5 were waited for; matrix products, arithmetic and copies ran while one was open for 5% of the time, Pallas kernels for 3%

profile of v7, /device:TPU:0, one launch (start us, length us, event | category | flops | bytes accessed | tf_op | source)
XLA Modules:
  0.0 289.0 jit_solution(12971268401413912430)
XLA Ops:
  0.6 2.2 copy-done.7
  3.6 2.0 copy-done.6
  5.7 5.0 %all-to-all-start.15 = ((bf16[4,2048,256]{2,1,0:T(8,128)(2,1)}), bf16[4,2048,256]{2,1,0:T(8,128)(2,1)}, u32[]{:S(2)}, u32[]{:S(2)}) async-start(bf16[4,2048,256]{2,1,0:T(8,128)(2,1)} %bitcast.26), calls=%async_computation.15 | async-start | bytes 8388608 | tf_op jit(solution)/shard_map/all_to_all | solution.py:46
  13.5 5.8 %collective-permute-start.11 = (bf16[1,304,384]{2,1,0:T(8,128)(2,1)S(1)}, bf16[1,304,384]{2,1,0:T(8,128)(2,1)S(1)}, u32[]{:S(2)}, u32[]{:S(2)}) collective-permute-start(bf16[1,304,384]{2,1,0:T(8,128)(2,1)S(1)} %broadcast_select_fusion), channel_id=1, source_target_pairs={{0,20},{1,21},{2,22},{3,23},{4,16},{5,17},{6,18},{7,19},{8,28},{9,... | collective-permute-start | bytes 700424 | tf_op jit(solution)/shard_map/ppermute | solution.py:543
  20.1 28.2 %collective-permute-done.11 = bf16[1,304,384]{2,1,0:T(8,128)(2,1)S(1)} collective-permute-done((bf16[1,304,384]{2,1,0:T(8,128)(2,1)S(1)}, bf16[1,304,384]{2,1,0:T(8,128)(2,1)S(1)}, u32[]{:S(2)}, u32[]{:S(2)}) %collective-permute-start.11) | collective-permute-done | bytes 233504 | tf_op jit(solution)/shard_map/ppermute | solution.py:543
  49.6 21.8 %conditional.8 = (bf16[256,384]{1,0:T(8,128)(2,1)}, f32[1,384]{1,0:T(1,128)}, bf16[32,384]{1,0:T(8,128)(2,1)}) conditional(s32[]{:T(128)} %convert_element_type.49, () %tuple.73, (bf16[4,304,384]{2,1,0:T(8,128)(2,1)}, s32[1]{0:T(128)}, bf16[4,4,2,256,256]{4,3,2,1,0:T(8,128)(2,1)}, bf16[256,384]{1,0:T(8,128)(2,1)S(1)}, ...), branch_computations={%region_4.5_spmd, %region_5.6_spmd} | conditional | flops 2000000000 | bytes 24461436 | solution.py:531
  49.7 3.0 %mid_forward_own.4.total = f32[4,384,256]{2,1,0:T(8,128)S(1)} custom-call(s32[1]{0:T(128)} %get-tuple-element.94.info, bf16[4,304,384]{2,1,0:T(8,128)(2,1)} %get-tuple-element.120.got, bf16[4,4,2,256,256]{4,3,2,1,0:T(8,128)(2,1)} %get-tuple-element.128.weight), custom_call_target="tpu_custom_call" | custom-call | flops 800000000 | bytes 5128192 | tf_op jit(solution)/shard_map/cond/branch_1_fun/mid_forward_own/pallas_call | solution.py:411
  52.7 3.9 %mid_forward.4 = bf16[4,304,384]{2,1,0:T(8,128)(2,1)} custom-call(s32[1]{0:T(128)} %get-tuple-element.94.info, bf16[4,304,384]{2,1,0:T(8,128)(2,1)} %get-tuple-element.120.got, bf16[4,304,384]{2,1,0:T(8,128)(2,1)S(1)} %collective-permute-done.other, bf16[4,4,2,256,256]{4,3,2,1,0:T(8,128)(2,1)} %get-tuple-element.128.weight, ...), custom_call_target="tpu_custom_call" | custom-call | flops 800000000 | bytes 7634944 | tf_op jit(solution)/shard_map/cond/branch_1_fun/mid_forward/pallas_call | solution.py:411
  56.6 3.5 %all-to-all-start = ((bf16[4,304,384]{2,1,0:T(8,128)(2,1)}), bf16[4,304,384]{2,1,0:T(8,128)(2,1)S(1)}, u32[]{:S(2)}, u32[]{:S(2)}) async-start(bf16[4,304,384]{2,1,0:T(8,128)(2,1)} %mid_forward.4), calls=%async_computation | async-start | bytes 1867776 | tf_op jit(solution)/shard_map/cond/branch_1_fun/all_to_all | solution.py:46
  60.8 8.1 %all-to-all-done.refs_0_ = bf16[4,304,384]{2,1,0:T(8,128)(2,1)S(1)} async-done(((bf16[4,304,384]{2,1,0:T(8,128)(2,1)}), bf16[4,304,384]{2,1,0:T(8,128)(2,1)S(1)}, u32[]{:S(2)}, u32[]{:S(2)}) %all-to-all-start) | async-done | bytes 933920 | tf_op jit(solution)/shard_map/cond/branch_1_fun/all_to_all | solution.py:46
  68.9 2.5 post_forward.3
  71.5 2.0 collective-permute-start.12
  76.2 2.3 bring.1
  78.5 2.0 copy-done
  80.5 2.7 conditional.10
  86.0 3.3 %conditional.13 = (bf16[256,384]{1,0:T(8,128)(2,1)}, f32[1,384]{1,0:T(1,128)}, bf16[32,384]{1,0:T(8,128)(2,1)}, bf16[256,384]{1,0:T(8,128)(2,1)}, bf16[256,384]{1,0:T(8,128)(2,1)}) conditional(s32[]{:T(128)} %convert_element_type.51, () %tuple.71, (bf16[256,384]{1,0:T(8,128)(2,1)}, f32[256,1]{0,1:T(1,128)S(1)}, bf16[2048,256]{1,0:T(8,128)(2,1)S(1)}, ...), branch_computations={%region_14.15_spmd, %region_15.16_spmd} | conditional | flops 4400999936 | bytes 94082832 | solution.py:531
  92.6 1.3 collective-permute-start.17
  95.0 1.8 conditional.15
  96.9 170.5 %collective-permute-done.16.received = bf16[256,384]{1,0:T(8,128)(2,1)S(1)} collective-permute-done((bf16[256,384]{1,0:T(8,128)(2,1)}, bf16[256,384]{1,0:T(8,128)(2,1)S(1)}, u32[]{:S(2)}, u32[]{:S(2)}) %collective-permute-start.16) | collective-permute-done | bytes 196640 | tf_op jit(solution)/shard_map/ppermute | solution.py:528
  267.4 1.6 ranks_of.1
  271.1 5.6 %all-to-all-start.16 = ((bf16[16,32,384]{2,1,0:T(8,128)(2,1)}), bf16[16,32,384]{2,1,0:T(8,128)(2,1)S(1)}, u32[]{:S(2)}, u32[]{:S(2)}) async-start(bf16[16,32,384]{2,1,0:T(8,128)(2,1)} %both_cores.1), calls=%async_computation.16 | async-start | bytes 786432 | tf_op jit(solution)/shard_map/all_to_all | solution.py:46
  279.5 2.1 outer_up.1
  282.3 4.5 %all-to-all-done.16.got = bf16[16,32,384]{2,1,0:T(8,128)(2,1)S(1)} async-done(((bf16[16,32,384]{2,1,0:T(8,128)(2,1)}), bf16[16,32,384]{2,1,0:T(8,128)(2,1)S(1)}, u32[]{:S(2)}, u32[]{:S(2)}) %all-to-all-start.16) | async-done | bytes 393248 | tf_op jit(solution)/shard_map/all_to_all | solution.py:46
  286.8 2.1 outer_down.1
  (114 shorter events, 32.5 us)
Async XLA Ops:
  5.6 5.3 %copy-start.30 = (s32[2,64]{1,0:T(2,128)S(1)}, s32[2,64]{1,0:T(2,128)}, u32[]{:S(2)}) copy-start(s32[2,64]{1,0:T(2,128)} %param.31) | copy-start | bytes 1540
  5.6 5.8 %copy-start.21 = (bf16[2,192,256]{2,1,0:T(8,128)(2,1)S(1)}, bf16[2,192,256]{2,1,0:T(8,128)(2,1)}, u32[]{:S(2)}) copy-start(bf16[2,192,256]{2,1,0:T(8,128)(2,1)} %param.25) | copy-start | bytes 589828
  5.6 6.0 %copy-start.22 = (bf16[2,192,256]{2,1,0:T(8,128)(2,1)S(1)}, bf16[2,192,256]{2,1,0:T(8,128)(2,1)}, u32[]{:S(2)}) copy-start(bf16[2,192,256]{2,1,0:T(8,128)(2,1)} %param.24) | copy-start | bytes 589828
  5.7 44.0 %all-to-all-start.15 = ((bf16[4,2048,256]{2,1,0:T(8,128)(2,1)}), bf16[4,2048,256]{2,1,0:T(8,128)(2,1)}, u32[]{:S(2)}, u32[]{:S(2)}) async-start(bf16[4,2048,256]{2,1,0:T(8,128)(2,1)} %bitcast.26), calls=%async_computation.15 | async-start | bytes 8388608 | tf_op jit(solution)/shard_map/all_to_all | solution.py:46
  11.8 37.8 %copy-start.17 = (bf16[384,256]{0,1:T(8,128)(2,1)}, bf16[384,256]{0,1:T(8,128)(2,1)S(1)}, u32[]{:S(2)}) copy-start(bf16[384,256]{0,1:T(8,128)(2,1)S(1)} %copy.38) | copy-start | bytes 589828
  11.8 83.2 %copy-start.13 = (f32[64,384]{1,0:T(8,128)}, f32[64,384]{1,0:T(8,128)S(1)}, u32[]{:S(2)}) copy-start(f32[64,384]{1,0:T(8,128)S(1)} %convert_convert_fusion.member) | copy-start | bytes 294916
  13.5 34.8 %collective-permute-start.11 = (bf16[1,304,384]{2,1,0:T(8,128)(2,1)S(1)}, bf16[1,304,384]{2,1,0:T(8,128)(2,1)S(1)}, u32[]{:S(2)}, u32[]{:S(2)}) collective-permute-start(bf16[1,304,384]{2,1,0:T(8,128)(2,1)S(1)} %broadcast_select_fusion), channel_id=1, source_target_pairs={{0,20},{1,21},{2,22},{3,23},{4,16},{5,17},{6,18},{7,19},{8,28},{9,... | collective-permute-start | bytes 700424 | tf_op jit(solution)/shard_map/ppermute | solution.py:543
  19.3 29.0 %collective-permute-start.10 = (bf16[1,304,384]{2,1,0:T(8,128)(2,1)S(1)}, bf16[1,304,384]{2,1,0:T(8,128)(2,1)S(1)}, u32[]{:S(2)}, u32[]{:S(2)}) collective-permute-start(bf16[1,304,384]{2,1,0:T(8,128)(2,1)S(1)} %broadcast_select_fusion), channel_id=1, source_target_pairs={{0,16},{1,17},{2,18},{3,19},{4,20},{5,21},{6,22},{7,23},{8,24},{9,... | collective-permute-start | bytes 700424 | tf_op jit(solution)/shard_map/ppermute | solution.py:543
  19.8 28.5 %collective-permute-start.9 = (bf16[1,304,384]{2,1,0:T(8,128)(2,1)S(1)}, bf16[1,304,384]{2,1,0:T(8,128)(2,1)S(1)}, u32[]{:S(2)}, u32[]{:S(2)}) collective-permute-start(bf16[1,304,384]{2,1,0:T(8,128)(2,1)S(1)} %broadcast_select_fusion), channel_id=1, source_target_pairs={{0,4},{1,5},{2,6},{3,7},{4,0},{5,1},{6,2},{7,3},{8,12},{9,13},{10,... | collective-permute-start | bytes 700424 | tf_op jit(solution)/shard_map/ppermute | solution.py:543
  49.6 3.1 %collective-permute-start = (bf16[4,304,384]{2,1,0:T(8,128)(2,1)}, bf16[4,304,384]{2,1,0:T(8,128)(2,1)S(1)}, u32[]{:S(2)}, u32[]{:S(2)}) collective-permute-start(bf16[4,304,384]{2,1,0:T(8,128)(2,1)} %get-tuple-element.120.got), channel_id=1, source_target_pairs={{0,1},{1,0},{2,3},{3,2},{4,5},{5,4},{6,7},{7,6},{8,9},{9,8},{10,11... | collective-permute-start | bytes 2801672 | tf_op jit(solution)/shard_map/cond/branch_1_fun/ppermute | solution.py:50
  56.6 12.3 %all-to-all-start = ((bf16[4,304,384]{2,1,0:T(8,128)(2,1)}), bf16[4,304,384]{2,1,0:T(8,128)(2,1)S(1)}, u32[]{:S(2)}, u32[]{:S(2)}) async-start(bf16[4,304,384]{2,1,0:T(8,128)(2,1)} %mid_forward.4), calls=%async_computation | async-start | bytes 1867776 | tf_op jit(solution)/shard_map/cond/branch_1_fun/all_to_all | solution.py:46
  71.5 9.1 %collective-permute-start.12 = (bf16[256,384]{1,0:T(8,128)(2,1)}, bf16[256,384]{1,0:T(8,128)(2,1)}, u32[]{:S(2)}, u32[]{:S(2)}) collective-permute-start(bf16[256,384]{1,0:T(8,128)(2,1)} %get-tuple-element.280), channel_id=1, source_target_pairs={{0,32},{1,33},{2,34},{3,35},{4,36},{5,37},{6,38},{7,39},{8,40},{9,... | collective-permute-start | bytes 589832 | tf_op jit(solution)/shard_map/ppermute | solution.py:528
  74.1 10.5 %collective-permute-start.14 = (bf16[256,384]{1,0:T(8,128)(2,1)}, bf16[256,384]{1,0:T(8,128)(2,1)}, u32[]{:S(2)}, u32[]{:S(2)}) collective-permute-start(bf16[256,384]{1,0:T(8,128)(2,1)} %get-tuple-element.507), channel_id=1, source_target_pairs={{96,64},{97,65},{98,66},{99,67},{100,68},{101,69},{102,70},{103,71... | collective-permute-start | bytes 589832 | tf_op jit(solution)/shard_map/ppermute | solution.py:528
  83.3 7.3 %copy-start.27 = (f32[1,384]{1,0:T(1,128)}, f32[1,384]{1,0:T(1,128)S(1)}, u32[]{:S(2)}) copy-start(f32[1,384]{1,0:T(1,128)S(1)} %get-tuple-element.290) | copy-start | bytes 4612
  83.3 2.2 collective-permute-start.13
  89.3 1.3 collective-permute-start.15
  91.3 176.1 %collective-permute-start.16 = (bf16[256,384]{1,0:T(8,128)(2,1)}, bf16[256,384]{1,0:T(8,128)(2,1)S(1)}, u32[]{:S(2)}, u32[]{:S(2)}) collective-permute-start(bf16[256,384]{1,0:T(8,128)(2,1)} %get-tuple-element.509), channel_id=1, source_target_pairs={{32,0},{33,1},{34,2},{35,3},{36,4},{37,5},{38,6},{39,7},{40,8},{41... | collective-permute-start | bytes 589832 | tf_op jit(solution)/shard_map/ppermute | solution.py:528
  92.6 2.4 collective-permute-start.17
  96.9 179.8 %copy-start.18 = (bf16[384,256]{0,1:T(8,128)(2,1)S(1)}, bf16[384,256]{0,1:T(8,128)(2,1)}, u32[]{:S(2)}) copy-start(bf16[384,256]{0,1:T(8,128)(2,1)} %copy-done.17) | copy-start | bytes 589828
  269.0 8.9 %copy-start.24 = (bf16[32,384]{1,0:T(8,128)(2,1)S(1)}, bf16[32,384]{1,0:T(8,128)(2,1)}, u32[]{:S(2)}) copy-start(bf16[32,384]{1,0:T(8,128)(2,1)} %get-tuple-element.294) | copy-start | bytes 73732
  269.0 8.9 %copy-start.25 = (bf16[32,384]{1,0:T(8,128)(2,1)S(1)}, bf16[32,384]{1,0:T(8,128)(2,1)}, u32[]{:S(2)}) copy-start(bf16[32,384]{1,0:T(8,128)(2,1)} %get-tuple-element.293) | copy-start | bytes 73732
  269.0 1.3 collective-permute-start.18
  271.1 8.4 %copy-start.14 = (f32[64,384]{1,0:T(8,128)S(1)}, f32[64,384]{1,0:T(8,128)}, u32[]{:S(2)}) copy-start(f32[64,384]{1,0:T(8,128)} %copy-done.13) | copy-start | bytes 294916
  271.1 15.7 %all-to-all-start.16 = ((bf16[16,32,384]{2,1,0:T(8,128)(2,1)}), bf16[16,32,384]{2,1,0:T(8,128)(2,1)S(1)}, u32[]{:S(2)}, u32[]{:S(2)}) async-start(bf16[16,32,384]{2,1,0:T(8,128)(2,1)} %both_cores.1), calls=%async_computation.16 | async-start | bytes 786432 | tf_op jit(solution)/shard_map/all_to_all | solution.py:46
  (14 other events, 39.0 us)

commit v8 on v7

--- a/solution.py
+++ b/solution.py
@@ -32,6 +32,8 @@
     for y in range(2)
     for c in range(CS)
 ]
+ROUND = (0, 1, 3, 2)
+RING = [[group[k] for k in ROUND] for group in APART]
 BLOCKS = [
     [place(*partner(x, y, c, k), c) for k in range(4)]
     for x in range(0, XS, 2)
@@ -131,7 +133,8 @@
 def turn_rows(got, cols, turned):
     @pl.when(pl.program_id(0) == 0)
     def _():
-        turned[...] = got[:, :cols].reshape(got.shape[0] * cols, got.shape[2]).T
+        parts = [got[k, :cols] for k in ROUND]
+        turned[...] = jnp.concatenate(parts, axis=0).T
 
 
 def mid_forward_own(info, got, weight, total, turned):
@@ -482,7 +485,8 @@
         )
 
     def forward(current):
-        got = exchange(start_forward(current), APART)
+        sent = start_forward(current, ((1, tall, total), BF))
+        got = lax.all_gather(sent, "dp", axis_index_groups=RING, axis=0, tiled=True)
         return exchange(product_forward(got), BLOCKS)
 
     def product_backward(got, held=held):
@@ -543,7 +547,8 @@
         turns.append(lax.ppermute(first, ("section", "dp"), pairs))
     turns = jnp.concatenate(turns)
     own = jnp.where(gather, at_x // 2 * 2 + at_y // 2, at_x % 2 * 2 + at_y % 2)
-    got = jnp.stack([lax.dynamic_index_in_dim(turns, own ^ j, 0, False) for j in range(4)])
+    order = [own ^ jnp.where(gather, ROUND[j], j) for j in range(4)]
+    got = jnp.stack([lax.dynamic_index_in_dim(turns, j, 0, False) for j in order])
 
     def run_first():
         outs = end_forward(exchange(product_forward(got, lambda x: x), BLOCKS), tokens)
@@ -559,10 +564,11 @@
         )
 
     brief = [main] + kept_outs[3:]
+    (ahead,) = only(3, run_target, [main])
+    got, ahead = lax.optimization_barrier((got, ahead))
+    ahead = hop(ahead, [(3, 2)])
     result_0, inverse_0, down_0 = only(0, run_first, brief)
     first = hop(result_0, [(0, 1)])
-    (ahead,) = only(3, run_target, [main])
-    ahead = hop(ahead, [(3, 2)])
     back_first, ranks_first = only(2, lambda: sums_of(got), [wide, thin])
 
     back_late, ranks_late = only(2, lambda: sums_of(exchange(plain(ahead), BLOCKS)), [wide, thin])

time: 290 us -> 290 us (level)
    unnamed x46 -> x54, local copies, waits for them, and re-layouts: 6.83 us -> 7.67 us
  transfers between devices with their start and end apart: 14 -> 14, of which waited for: 5 -> 5; matrix products, arithmetic and copies ran while one was open for 5% -> 6% of each run, Pallas kernels for 3% -> 3%
where the time goes in v8:
time: 290 us; the launch traced here: 289 us
  waiting for transfers between devices  211 us (73%)
  starting transfers between devices  28.8 us (10%)
  local copies, waits for them, and re-layouts  21.8 us (8%)
  Pallas kernels  19.6 us (7%)
  other arithmetic  6.46 us (2%)
    ppermute x6, waiting for transfers between devices, hop(): return lax.ppermute(value, 'section', pairs)  169 us
    ppermute x3, waiting for transfers between devices, on_device(): turns.append(lax.ppermute(first, ('section', 'dp'), pairs))  28.2 us
    all_to_all x3, starting transfers between devices, exchange(): return lax.all_to_all(chunks, 'dp', 0, 0, axis_index_groups=groups)  14.2 us
    all_to_all x3, waiting for transfers between devices, exchange(): return lax.all_to_all(chunks, 'dp', 0, 0, axis_index_groups=groups)  12.7 us
    another operation x20, local copies, waits for them, and re-layouts  12.5 us
    pallas_call x7, Pallas kernels, whole_call(): pl.pallas_call(body, out_shape=[jax.ShapeDtypeStruct(s, d) for s, d in ou...  9.71 us
    ppermute x6, starting transfers between devices, hop(): return lax.ppermute(value, 'section', pairs)  7.9 us
    unnamed x54, local copies, waits for them, and re-layouts  7.67 us
  transfers between devices with their start and end apart: 14, of which 5 were waited for; matrix products, arithmetic and copies ran while one was open for 6% of the time, Pallas kernels for 3%

profile of v8, /device:TPU:0, one launch (start us, length us, event | category | flops | bytes accessed | tf_op | source)
XLA Modules:
  0.0 289.1 jit_solution(8495411818532893239)
XLA Ops:
  0.6 2.2 copy-done.7
  3.6 2.0 copy-done.6
  5.7 5.0 %all-to-all-start.12 = ((bf16[4,2048,256]{2,1,0:T(8,128)(2,1)}), bf16[4,2048,256]{2,1,0:T(8,128)(2,1)}, u32[]{:S(2)}, u32[]{:S(2)}) async-start(bf16[4,2048,256]{2,1,0:T(8,128)(2,1)} %bitcast.26), calls=%async_computation.12 | async-start | bytes 8388608 | tf_op jit(solution)/shard_map/all_to_all | solution.py:48
  13.5 5.8 %collective-permute-start.11 = (bf16[1,304,384]{2,1,0:T(8,128)(2,1)S(1)}, bf16[1,304,384]{2,1,0:T(8,128)(2,1)S(1)}, u32[]{:S(2)}, u32[]{:S(2)}) collective-permute-start(bf16[1,304,384]{2,1,0:T(8,128)(2,1)S(1)} %broadcast_select_fusion), channel_id=1, source_target_pairs={{0,20},{1,21},{2,22},{3,23},{4,16},{5,17},{6,18},{7,19},{8,28},{9,... | collective-permute-start | bytes 700424 | tf_op jit(solution)/shard_map/ppermute | solution.py:547
  20.1 28.2 %collective-permute-done.11 = bf16[1,304,384]{2,1,0:T(8,128)(2,1)S(1)} collective-permute-done((bf16[1,304,384]{2,1,0:T(8,128)(2,1)S(1)}, bf16[1,304,384]{2,1,0:T(8,128)(2,1)S(1)}, u32[]{:S(2)}, u32[]{:S(2)}) %collective-permute-start.11) | collective-permute-done | bytes 233504 | tf_op jit(solution)/shard_map/ppermute | solution.py:547
  52.8 20.9 %conditional.9 = (bf16[256,384]{1,0:T(8,128)(2,1)}, f32[1,384]{1,0:T(1,128)}, bf16[32,384]{1,0:T(8,128)(2,1)}) conditional(s32[]{:T(128)} %convert_element_type.49, () %tuple.74, (bf16[4,304,384]{2,1,0:T(8,128)(2,1)}, s32[1]{0:T(128)}, bf16[4,4,2,256,256]{4,3,2,1,0:T(8,128)(2,1)}, bf16[256,384]{1,0:T(8,128)(2,1)}, bf16[256,2048]{0,1:T(8,128)(2,1)S(1)}, ...), branch_computations={%region_6.7_spmd, %region_7.8_spmd} | conditional | flops 2000000000 | bytes 24461436 | solution.py:535
  52.8 2.9 %mid_forward_own.4.total = f32[4,384,256]{2,1,0:T(8,128)S(1)} custom-call(s32[1]{0:T(128)} %get-tuple-element.132.info, bf16[4,304,384]{2,1,0:T(8,128)(2,1)} %get-tuple-element.133.got, bf16[4,4,2,256,256]{4,3,2,1,0:T(8,128)(2,1)} %get-tuple-element.134.weight), custom_call_target="tpu_custom_call" | custom-call | flops 800000000 | bytes 5128192 | tf_op jit(solution)/shard_map/cond/branch_1_fun/mid_forward_own/pallas_call | solution.py:414
  55.8 3.9 %mid_forward.4 = bf16[4,304,384]{2,1,0:T(8,128)(2,1)} custom-call(s32[1]{0:T(128)} %get-tuple-element.132.info, bf16[4,304,384]{2,1,0:T(8,128)(2,1)} %get-tuple-element.133.got, bf16[4,304,384]{2,1,0:T(8,128)(2,1)S(1)} %collective-permute-done.1.other, bf16[4,4,2,256,256]{4,3,2,1,0:T(8,128)(2,1)} %get-tuple-element.134.weight, ...), custom_call_target="tpu_custom_call" | custom-call | flops 800000000 | bytes 7634944 | tf_op jit(solution)/shard_map/cond/branch_1_fun/mid_forward/pallas_call | solution.py:414
  59.7 3.6 %all-to-all-start.1 = ((bf16[4,304,384]{2,1,0:T(8,128)(2,1)}), bf16[4,304,384]{2,1,0:T(8,128)(2,1)S(1)}, u32[]{:S(2)}, u32[]{:S(2)}) async-start(bf16[4,304,384]{2,1,0:T(8,128)(2,1)} %mid_forward.4), calls=%async_computation.1 | async-start | bytes 1867776 | tf_op jit(solution)/shard_map/cond/branch_1_fun/all_to_all | solution.py:48
  64.0 8.1 %all-to-all-done.1.refs_0_ = bf16[4,304,384]{2,1,0:T(8,128)(2,1)S(1)} async-done(((bf16[4,304,384]{2,1,0:T(8,128)(2,1)}), bf16[4,304,384]{2,1,0:T(8,128)(2,1)S(1)}, u32[]{:S(2)}, u32[]{:S(2)}) %all-to-all-start.1) | async-done | bytes 933920 | tf_op jit(solution)/shard_map/cond/branch_1_fun/all_to_all | solution.py:48
  72.1 1.6 post_forward.3
  73.7 2.0 collective-permute-start.12
  77.2 2.3 bring.1
  79.5 2.0 copy-done
  81.5 3.3 %conditional.11 = ((bf16[256,384]{1,0:T(8,128)(2,1)}, f32[256,384]{1,0:T(8,128)}, f32[32,384]{1,0:T(8,128)}, f32[1,384]{1,0:T(1,128)}, bf16[32,384]{1,0:T(8,128)(2,1)})) conditional(s32[]{:T(128)} %convert_element_type.50, () %tuple.73, (bf16[256,384]{1,0:T(8,128)(2,1)}, f32[256,1]{0,1:T(1,128)S(1)}, bf16[2048,256]{1,0:T(8,128)(2,1)S(1)}, ...), branch_computations={%region_10.11_spmd, %region_11.12_spmd} | conditional | flops 2400000000 | bytes 42966124 | solution.py:535
  86.1 1.4 conditional.12
  87.5 3.2 %conditional.13 = (bf16[256,384]{1,0:T(8,128)(2,1)}, f32[1,384]{1,0:T(1,128)}, bf16[32,384]{1,0:T(8,128)(2,1)}, bf16[256,384]{1,0:T(8,128)(2,1)}, bf16[256,384]{1,0:T(8,128)(2,1)}) conditional(s32[]{:T(128)} %convert_element_type.51, () %tuple.72, (bf16[256,384]{1,0:T(8,128)(2,1)}, f32[256,1]{0,1:T(1,128)S(1)}, bf16[2048,256]{1,0:T(8,128)(2,1)S(1)}, ...), branch_computations={%region_14.15_spmd, %region_15.16_spmd} | conditional | flops 4400999936 | bytes 94365520 | solution.py:535
  96.5 1.8 conditional.15
  98.3 169.1 %collective-permute-done.16.received = bf16[256,384]{1,0:T(8,128)(2,1)S(1)} collective-permute-done((bf16[256,384]{1,0:T(8,128)(2,1)}, bf16[256,384]{1,0:T(8,128)(2,1)S(1)}, u32[]{:S(2)}, u32[]{:S(2)}) %collective-permute-start.16) | collective-permute-done | bytes 196640 | tf_op jit(solution)/shard_map/ppermute | solution.py:532
  267.5 1.6 ranks_of.1
  271.2 5.6 %all-to-all-start.13 = ((bf16[16,32,384]{2,1,0:T(8,128)(2,1)}), bf16[16,32,384]{2,1,0:T(8,128)(2,1)S(1)}, u32[]{:S(2)}, u32[]{:S(2)}) async-start(bf16[16,32,384]{2,1,0:T(8,128)(2,1)} %both_cores.1), calls=%async_computation.13 | async-start | bytes 786432 | tf_op jit(solution)/shard_map/all_to_all | solution.py:48
  279.6 2.1 outer_up.1
  282.3 4.6 %all-to-all-done.13.got = bf16[16,32,384]{2,1,0:T(8,128)(2,1)S(1)} async-done(((bf16[16,32,384]{2,1,0:T(8,128)(2,1)}), bf16[16,32,384]{2,1,0:T(8,128)(2,1)S(1)}, u32[]{:S(2)}, u32[]{:S(2)}) %all-to-all-start.13) | async-done | bytes 393248 | tf_op jit(solution)/shard_map/all_to_all | solution.py:48
  286.9 2.1 outer_down.1
  (122 shorter events, 35.3 us)
Async XLA Ops:
  5.6 5.3 %copy-start.39 = (s32[2,64]{1,0:T(2,128)S(1)}, s32[2,64]{1,0:T(2,128)}, u32[]{:S(2)}) copy-start(s32[2,64]{1,0:T(2,128)} %param.31) | copy-start | bytes 1540
  5.6 5.8 %copy-start.26 = (bf16[2,192,256]{2,1,0:T(8,128)(2,1)S(1)}, bf16[2,192,256]{2,1,0:T(8,128)(2,1)}, u32[]{:S(2)}) copy-start(bf16[2,192,256]{2,1,0:T(8,128)(2,1)} %param.25) | copy-start | bytes 589828
  5.7 6.0 %copy-start.27 = (bf16[2,192,256]{2,1,0:T(8,128)(2,1)S(1)}, bf16[2,192,256]{2,1,0:T(8,128)(2,1)}, u32[]{:S(2)}) copy-start(bf16[2,192,256]{2,1,0:T(8,128)(2,1)} %param.24) | copy-start | bytes 589828
  5.7 46.5 %all-to-all-start.12 = ((bf16[4,2048,256]{2,1,0:T(8,128)(2,1)}), bf16[4,2048,256]{2,1,0:T(8,128)(2,1)}, u32[]{:S(2)}, u32[]{:S(2)}) async-start(bf16[4,2048,256]{2,1,0:T(8,128)(2,1)} %bitcast.26), calls=%async_computation.12 | async-start | bytes 8388608 | tf_op jit(solution)/shard_map/all_to_all | solution.py:48
  10.7 76.8 %copy-start.31 = (f32[256,1]{0,1:T(1,128)}, f32[256,1]{0,1:T(1,128)S(1)}, u32[]{:S(2)}) copy-start(f32[256,1]{0,1:T(1,128)S(1)} %bitcast_convert_fusion) | copy-start | bytes 3076
  11.8 84.7 %copy-start.14 = (f32[64,384]{1,0:T(8,128)}, f32[64,384]{1,0:T(8,128)S(1)}, u32[]{:S(2)}) copy-start(f32[64,384]{1,0:T(8,128)S(1)} %convert_convert_fusion.member) | copy-start | bytes 294916
  13.5 34.7 %collective-permute-start.11 = (bf16[1,304,384]{2,1,0:T(8,128)(2,1)S(1)}, bf16[1,304,384]{2,1,0:T(8,128)(2,1)S(1)}, u32[]{:S(2)}, u32[]{:S(2)}) collective-permute-start(bf16[1,304,384]{2,1,0:T(8,128)(2,1)S(1)} %broadcast_select_fusion), channel_id=1, source_target_pairs={{0,20},{1,21},{2,22},{3,23},{4,16},{5,17},{6,18},{7,19},{8,28},{9,... | collective-permute-start | bytes 700424 | tf_op jit(solution)/shard_map/ppermute | solution.py:547
  19.3 28.9 %collective-permute-start.10 = (bf16[1,304,384]{2,1,0:T(8,128)(2,1)S(1)}, bf16[1,304,384]{2,1,0:T(8,128)(2,1)S(1)}, u32[]{:S(2)}, u32[]{:S(2)}) collective-permute-start(bf16[1,304,384]{2,1,0:T(8,128)(2,1)S(1)} %broadcast_select_fusion), channel_id=1, source_target_pairs={{0,16},{1,17},{2,18},{3,19},{4,20},{5,21},{6,22},{7,23},{8,24},{9,... | collective-permute-start | bytes 700424 | tf_op jit(solution)/shard_map/ppermute | solution.py:547
  19.8 29.8 %collective-permute-start.9 = (bf16[1,304,384]{2,1,0:T(8,128)(2,1)S(1)}, bf16[1,304,384]{2,1,0:T(8,128)(2,1)}, u32[]{:S(2)}, u32[]{:S(2)}) collective-permute-start(bf16[1,304,384]{2,1,0:T(8,128)(2,1)S(1)} %broadcast_select_fusion), channel_id=1, source_target_pairs={{0,4},{1,5},{2,6},{3,7},{4,0},{5,1},{6,2},{7,3},{8,12},{9,13},{10,... | collective-permute-start | bytes 700424 | tf_op jit(solution)/shard_map/ppermute | solution.py:547
  52.8 3.0 %collective-permute-start.1 = (bf16[4,304,384]{2,1,0:T(8,128)(2,1)}, bf16[4,304,384]{2,1,0:T(8,128)(2,1)S(1)}, u32[]{:S(2)}, u32[]{:S(2)}) collective-permute-start(bf16[4,304,384]{2,1,0:T(8,128)(2,1)} %get-tuple-element.133.got), channel_id=1, source_target_pairs={{0,1},{1,0},{2,3},{3,2},{4,5},{5,4},{6,7},{7,6},{8,9},{9,8},{10,11... | collective-permute-start | bytes 2801672 | tf_op jit(solution)/shard_map/cond/branch_1_fun/ppermute | solution.py:52
  59.7 12.4 %copy-start.20 = (bf16[256,384]{1,0:T(8,128)(2,1)S(1)}, bf16[256,384]{1,0:T(8,128)(2,1)}, u32[]{:S(2)}) copy-start(bf16[256,384]{1,0:T(8,128)(2,1)} %get-tuple-element.135.refs_1_) | copy-start | bytes 589828 | tf_op jit(solution)/shard_map/cond
  59.7 12.4 %all-to-all-start.1 = ((bf16[4,304,384]{2,1,0:T(8,128)(2,1)}), bf16[4,304,384]{2,1,0:T(8,128)(2,1)S(1)}, u32[]{:S(2)}, u32[]{:S(2)}) async-start(bf16[4,304,384]{2,1,0:T(8,128)(2,1)} %mid_forward.4), calls=%async_computation.1 | async-start | bytes 1867776 | tf_op jit(solution)/shard_map/cond/branch_1_fun/all_to_all | solution.py:48
  73.7 7.8 %collective-permute-start.12 = (bf16[256,384]{1,0:T(8,128)(2,1)}, bf16[256,384]{1,0:T(8,128)(2,1)}, u32[]{:S(2)}, u32[]{:S(2)}) collective-permute-start(bf16[256,384]{1,0:T(8,128)(2,1)} %get-tuple-element.284), channel_id=1, source_target_pairs={{0,32},{1,33},{2,34},{3,35},{4,36},{5,37},{6,38},{7,39},{8,40},{9,... | collective-permute-start | bytes 589832 | tf_op jit(solution)/shard_map/ppermute | solution.py:532
  75.7 10.4 %collective-permute-start.14 = (bf16[256,384]{1,0:T(8,128)(2,1)}, bf16[256,384]{1,0:T(8,128)(2,1)S(1)}, u32[]{:S(2)}, u32[]{:S(2)}) collective-permute-start(bf16[256,384]{1,0:T(8,128)(2,1)} %get-tuple-element.561), channel_id=1, source_target_pairs={{96,64},{97,65},{98,66},{99,67},{100,68},{101,69},{102,70},{103,71... | collective-permute-start | bytes 589832 | tf_op jit(solution)/shard_map/ppermute | solution.py:532
  84.8 2.7 collective-permute-start.13
  90.8 1.3 collective-permute-start.15
  92.8 174.7 %collective-permute-start.16 = (bf16[256,384]{1,0:T(8,128)(2,1)}, bf16[256,384]{1,0:T(8,128)(2,1)S(1)}, u32[]{:S(2)}, u32[]{:S(2)}) collective-permute-start(bf16[256,384]{1,0:T(8,128)(2,1)} %get-tuple-element.565), channel_id=1, source_target_pairs={{32,0},{33,1},{34,2},{35,3},{36,4},{37,5},{38,6},{39,7},{40,8},{41... | collective-permute-start | bytes 589832 | tf_op jit(solution)/shard_map/ppermute | solution.py:532
  94.1 2.4 collective-permute-start.17
  98.3 178.4 %copy-start.19 = (bf16[384,256]{0,1:T(8,128)(2,1)S(1)}, bf16[384,256]{0,1:T(8,128)(2,1)}, u32[]{:S(2)}) copy-start(bf16[384,256]{0,1:T(8,128)(2,1)} %copy-done.18) | copy-start | bytes 589828
  269.1 8.9 %copy-start.29 = (bf16[32,384]{1,0:T(8,128)(2,1)S(1)}, bf16[32,384]{1,0:T(8,128)(2,1)}, u32[]{:S(2)}) copy-start(bf16[32,384]{1,0:T(8,128)(2,1)} %get-tuple-element.298) | copy-start | bytes 73732
  269.1 8.9 %copy-start.30 = (bf16[32,384]{1,0:T(8,128)(2,1)S(1)}, bf16[32,384]{1,0:T(8,128)(2,1)}, u32[]{:S(2)}) copy-start(bf16[32,384]{1,0:T(8,128)(2,1)} %get-tuple-element.297) | copy-start | bytes 73732
  269.1 1.3 collective-permute-start.18
  271.2 8.4 %copy-start.15 = (f32[64,384]{1,0:T(8,128)S(1)}, f32[64,384]{1,0:T(8,128)}, u32[]{:S(2)}) copy-start(f32[64,384]{1,0:T(8,128)} %copy-done.14) | copy-start | bytes 294916
  271.2 15.7 %all-to-all-start.13 = ((bf16[16,32,384]{2,1,0:T(8,128)(2,1)}), bf16[16,32,384]{2,1,0:T(8,128)(2,1)S(1)}, u32[]{:S(2)}, u32[]{:S(2)}) async-start(bf16[16,32,384]{2,1,0:T(8,128)(2,1)} %both_cores.1), calls=%async_computation.13 | async-start | bytes 786432 | tf_op jit(solution)/shard_map/all_to_all | solution.py:48
  (18 other events, 44.5 us)

commit v9 on v8

--- a/solution.py
+++ b/solution.py
@@ -565,11 +565,11 @@
 
     brief = [main] + kept_outs[3:]
     (ahead,) = only(3, run_target, [main])
-    got, ahead = lax.optimization_barrier((got, ahead))
     ahead = hop(ahead, [(3, 2)])
+    back_first, ranks_first = only(2, lambda: sums_of(got), [wide, thin])
+    got, back_first = lax.optimization_barrier((got, back_first))
     result_0, inverse_0, down_0 = only(0, run_first, brief)
     first = hop(result_0, [(0, 1)])
-    back_first, ranks_first = only(2, lambda: sums_of(got), [wide, thin])
 
     back_late, ranks_late = only(2, lambda: sums_of(exchange(plain(ahead), BLOCKS)), [wide, thin])
     halves, back_first = lax.optimization_barrier((halves, back_first))

time: 290 us -> 286 us (0.986)
    unnamed x54 -> x48, local copies, waits for them, and re-layouts: 7.67 us -> 7.01 us
  transfers between devices with their start and end apart: 14 -> 14, of which waited for: 5 -> 5; matrix products, arithmetic and copies ran while one was open for 6% -> 4% of each run, Pallas kernels for 3% -> 3%
where the time goes in v9:
time: 286 us; the launch traced here: 285 us
  waiting for transfers between devices  210 us (73%)
  starting transfers between devices  29.5 us (10%)
  local copies, waits for them, and re-layouts  20.1 us (7%)
  Pallas kernels  20 us (7%)
  other arithmetic  4.44 us (2%)
    ppermute x6, waiting for transfers between devices, hop(): return lax.ppermute(value, 'section', pairs)  167 us
    ppermute x3, waiting for transfers between devices, on_device(): turns.append(lax.ppermute(first, ('section', 'dp'), pairs))  28.2 us
    all_to_all x3, starting transfers between devices, exchange(): return lax.all_to_all(chunks, 'dp', 0, 0, axis_index_groups=groups)  14.1 us
    all_to_all x3, waiting for transfers between devices, exchange(): return lax.all_to_all(chunks, 'dp', 0, 0, axis_index_groups=groups)  12.7 us
    another operation x20, local copies, waits for them, and re-layouts  11.5 us
    pallas_call x7, Pallas kernels, whole_call(): pl.pallas_call(body, out_shape=[jax.ShapeDtypeStruct(s, d) for s, d in ou...  10.6 us
    ppermute x6, starting transfers between devices, hop(): return lax.ppermute(value, 'section', pairs)  8.73 us
    unnamed x48, local copies, waits for them, and re-layouts  7.01 us
  transfers between devices with their start and end apart: 14, of which 5 were waited for; matrix products, arithmetic and copies ran while one was open for 4% of the time, Pallas kernels for 3%

profile of v9, /device:TPU:0, one launch (start us, length us, event | category | flops | bytes accessed | tf_op | source)
XLA Modules:
  0.0 284.7 jit_solution(17499198958971945126)
XLA Ops:
  0.6 2.2 copy-done.7
  3.6 2.0 copy-done.6
  5.7 5.0 %all-to-all-start.12 = ((bf16[4,2048,256]{2,1,0:T(8,128)(2,1)}), bf16[4,2048,256]{2,1,0:T(8,128)(2,1)}, u32[]{:S(2)}, u32[]{:S(2)}) async-start(bf16[4,2048,256]{2,1,0:T(8,128)(2,1)} %bitcast.26), calls=%async_computation.12 | async-start | bytes 8388608 | tf_op jit(solution)/shard_map/all_to_all | solution.py:48
  13.5 5.8 %collective-permute-start.11 = (bf16[1,304,384]{2,1,0:T(8,128)(2,1)S(1)}, bf16[1,304,384]{2,1,0:T(8,128)(2,1)S(1)}, u32[]{:S(2)}, u32[]{:S(2)}) collective-permute-start(bf16[1,304,384]{2,1,0:T(8,128)(2,1)S(1)} %broadcast_select_fusion), channel_id=1, source_target_pairs={{0,20},{1,21},{2,22},{3,23},{4,16},{5,17},{6,18},{7,19},{8,28},{9,... | collective-permute-start | bytes 700424 | tf_op jit(solution)/shard_map/ppermute | solution.py:547
  20.1 28.2 %collective-permute-done.11 = bf16[1,304,384]{2,1,0:T(8,128)(2,1)S(1)} collective-permute-done((bf16[1,304,384]{2,1,0:T(8,128)(2,1)S(1)}, bf16[1,304,384]{2,1,0:T(8,128)(2,1)S(1)}, u32[]{:S(2)}, u32[]{:S(2)}) %collective-permute-start.11) | collective-permute-done | bytes 233504 | tf_op jit(solution)/shard_map/ppermute | solution.py:547
  49.7 21.2 %conditional.9 = (bf16[256,384]{1,0:T(8,128)(2,1)}, f32[1,384]{1,0:T(1,128)}, bf16[32,384]{1,0:T(8,128)(2,1)}) conditional(s32[]{:T(128)} %convert_element_type.49, () %tuple.74, (bf16[4,304,384]{2,1,0:T(8,128)(2,1)S(1)}, s32[1]{0:T(128)}, bf16[4,4,2,256,256]{4,3,2,1,0:T(8,128)(2,1)}, bf16[256,384]{1,0:T(8,128)(2,1)S(1)}, ...), branch_computations={%region_6.7_spmd, %region_7.8_spmd} | conditional | flops 2000000000 | bytes 24461436 | solution.py:535
  49.7 2.7 mid_forward_own.4.total
  52.5 3.6 %mid_forward.4 = bf16[4,304,384]{2,1,0:T(8,128)(2,1)} custom-call(s32[1]{0:T(128)} %get-tuple-element.129.info, bf16[4,304,384]{2,1,0:T(8,128)(2,1)S(1)} %get-tuple-element.130.got, bf16[4,304,384]{2,1,0:T(8,128)(2,1)S(1)} %collective-permute-done.1.other, bf16[4,4,2,256,256]{4,3,2,1,0:T(8,128)(2,1)} %get-tuple-element.131.weight, ...), custom_call_target="tpu_custom_call" | custom-call | flops 800000000 | bytes 7634944 | tf_op jit(solution)/shard_map/cond/branch_1_fun/mid_forward/pallas_call | solution.py:414
  56.1 3.5 %all-to-all-start.1 = ((bf16[4,304,384]{2,1,0:T(8,128)(2,1)}), bf16[4,304,384]{2,1,0:T(8,128)(2,1)S(1)}, u32[]{:S(2)}, u32[]{:S(2)}) async-start(bf16[4,304,384]{2,1,0:T(8,128)(2,1)} %mid_forward.4), calls=%async_computation.1 | async-start | bytes 1867776 | tf_op jit(solution)/shard_map/cond/branch_1_fun/all_to_all | solution.py:48
  60.3 8.1 %all-to-all-done.1.refs_0_ = bf16[4,304,384]{2,1,0:T(8,128)(2,1)S(1)} async-done(((bf16[4,304,384]{2,1,0:T(8,128)(2,1)}), bf16[4,304,384]{2,1,0:T(8,128)(2,1)S(1)}, u32[]{:S(2)}, u32[]{:S(2)}) %all-to-all-start.1) | async-done | bytes 933920 | tf_op jit(solution)/shard_map/cond/branch_1_fun/all_to_all | solution.py:48
  68.4 2.5 post_forward.3
  71.0 2.0 collective-permute-start.12
  73.6 1.5 collective-permute-start.14
  75.1 2.2 bring.1
  77.3 2.0 copy-done
  79.3 2.7 conditional.10
  84.7 3.3 %conditional.13 = (bf16[256,384]{1,0:T(8,128)(2,1)}, f32[1,384]{1,0:T(1,128)}, bf16[32,384]{1,0:T(8,128)(2,1)}, bf16[256,384]{1,0:T(8,128)(2,1)}, bf16[256,384]{1,0:T(8,128)(2,1)}) conditional(s32[]{:T(128)} %convert_element_type.51, () %tuple.72, (bf16[256,384]{1,0:T(8,128)(2,1)}, f32[256,1]{0,1:T(1,128)S(1)}, bf16[2048,256]{1,0:T(8,128)(2,1)S(1)}, ...), branch_computations={%region_14.15_spmd, %region_15.16_spmd} | conditional | flops 4400999936 | bytes 93382416 | solution.py:535
  93.8 1.9 conditional.15
  95.7 167.4 %collective-permute-done.16.received = bf16[256,384]{1,0:T(8,128)(2,1)S(1)} collective-permute-done((bf16[256,384]{1,0:T(8,128)(2,1)}, bf16[256,384]{1,0:T(8,128)(2,1)S(1)}, u32[]{:S(2)}, u32[]{:S(2)}) %collective-permute-start.16) | collective-permute-done | bytes 196640 | tf_op jit(solution)/shard_map/ppermute | solution.py:532
  263.1 1.6 ranks_of.1
  266.9 5.6 %all-to-all-start.13 = ((bf16[16,32,384]{2,1,0:T(8,128)(2,1)}), bf16[16,32,384]{2,1,0:T(8,128)(2,1)S(1)}, u32[]{:S(2)}, u32[]{:S(2)}) async-start(bf16[16,32,384]{2,1,0:T(8,128)(2,1)} %both_cores.1), calls=%async_computation.13 | async-start | bytes 786432 | tf_op jit(solution)/shard_map/all_to_all | solution.py:48
  275.3 2.1 outer_up.1
  278.0 4.5 %all-to-all-done.13.got = bf16[16,32,384]{2,1,0:T(8,128)(2,1)S(1)} async-done(((bf16[16,32,384]{2,1,0:T(8,128)(2,1)}), bf16[16,32,384]{2,1,0:T(8,128)(2,1)S(1)}, u32[]{:S(2)}, u32[]{:S(2)}) %all-to-all-start.13) | async-done | bytes 393248 | tf_op jit(solution)/shard_map/all_to_all | solution.py:48
  282.6 2.1 outer_down.1
  (116 shorter events, 31.9 us)
Async XLA Ops:
  5.6 5.8 %copy-start.23 = (bf16[2,192,256]{2,1,0:T(8,128)(2,1)S(1)}, bf16[2,192,256]{2,1,0:T(8,128)(2,1)}, u32[]{:S(2)}) copy-start(bf16[2,192,256]{2,1,0:T(8,128)(2,1)} %param.25) | copy-start | bytes 589828
  5.7 6.0 %copy-start.24 = (bf16[2,192,256]{2,1,0:T(8,128)(2,1)S(1)}, bf16[2,192,256]{2,1,0:T(8,128)(2,1)}, u32[]{:S(2)}) copy-start(bf16[2,192,256]{2,1,0:T(8,128)(2,1)} %param.24) | copy-start | bytes 589828
  5.7 43.0 %all-to-all-start.12 = ((bf16[4,2048,256]{2,1,0:T(8,128)(2,1)}), bf16[4,2048,256]{2,1,0:T(8,128)(2,1)}, u32[]{:S(2)}, u32[]{:S(2)}) async-start(bf16[4,2048,256]{2,1,0:T(8,128)(2,1)} %bitcast.26), calls=%async_computation.12 | async-start | bytes 8388608 | tf_op jit(solution)/shard_map/all_to_all | solution.py:48
  11.8 37.8 %copy-start.19 = (bf16[384,256]{0,1:T(8,128)(2,1)}, bf16[384,256]{0,1:T(8,128)(2,1)S(1)}, u32[]{:S(2)}) copy-start(bf16[384,256]{0,1:T(8,128)(2,1)S(1)} %copy.55) | copy-start | bytes 589828
  11.8 81.9 %copy-start.15 = (f32[64,384]{1,0:T(8,128)}, f32[64,384]{1,0:T(8,128)S(1)}, u32[]{:S(2)}) copy-start(f32[64,384]{1,0:T(8,128)S(1)} %convert_convert_fusion.member) | copy-start | bytes 294916
  13.5 34.8 %collective-permute-start.11 = (bf16[1,304,384]{2,1,0:T(8,128)(2,1)S(1)}, bf16[1,304,384]{2,1,0:T(8,128)(2,1)S(1)}, u32[]{:S(2)}, u32[]{:S(2)}) collective-permute-start(bf16[1,304,384]{2,1,0:T(8,128)(2,1)S(1)} %broadcast_select_fusion), channel_id=1, source_target_pairs={{0,20},{1,21},{2,22},{3,23},{4,16},{5,17},{6,18},{7,19},{8,28},{9,... | collective-permute-start | bytes 700424 | tf_op jit(solution)/shard_map/ppermute | solution.py:547
  19.3 29.0 %collective-permute-start.10 = (bf16[1,304,384]{2,1,0:T(8,128)(2,1)S(1)}, bf16[1,304,384]{2,1,0:T(8,128)(2,1)S(1)}, u32[]{:S(2)}, u32[]{:S(2)}) collective-permute-start(bf16[1,304,384]{2,1,0:T(8,128)(2,1)S(1)} %broadcast_select_fusion), channel_id=1, source_target_pairs={{0,16},{1,17},{2,18},{3,19},{4,20},{5,21},{6,22},{7,23},{8,24},{9,... | collective-permute-start | bytes 700424 | tf_op jit(solution)/shard_map/ppermute | solution.py:547
  19.8 28.5 %collective-permute-start.9 = (bf16[1,304,384]{2,1,0:T(8,128)(2,1)S(1)}, bf16[1,304,384]{2,1,0:T(8,128)(2,1)S(1)}, u32[]{:S(2)}, u32[]{:S(2)}) collective-permute-start(bf16[1,304,384]{2,1,0:T(8,128)(2,1)S(1)} %broadcast_select_fusion), channel_id=1, source_target_pairs={{0,4},{1,5},{2,6},{3,7},{4,0},{5,1},{6,2},{7,3},{8,12},{9,13},{10,... | collective-permute-start | bytes 700424 | tf_op jit(solution)/shard_map/ppermute | solution.py:547
  49.7 2.8 collective-permute-start.1
  56.1 12.3 %all-to-all-start.1 = ((bf16[4,304,384]{2,1,0:T(8,128)(2,1)}), bf16[4,304,384]{2,1,0:T(8,128)(2,1)S(1)}, u32[]{:S(2)}, u32[]{:S(2)}) async-start(bf16[4,304,384]{2,1,0:T(8,128)(2,1)} %mid_forward.4), calls=%async_computation.1 | async-start | bytes 1867776 | tf_op jit(solution)/shard_map/cond/branch_1_fun/all_to_all | solution.py:48
  71.0 8.3 %collective-permute-start.12 = (bf16[256,384]{1,0:T(8,128)(2,1)}, bf16[256,384]{1,0:T(8,128)(2,1)}, u32[]{:S(2)}, u32[]{:S(2)}) collective-permute-start(bf16[256,384]{1,0:T(8,128)(2,1)} %get-tuple-element.284), channel_id=1, source_target_pairs={{0,32},{1,33},{2,34},{3,35},{4,36},{5,37},{6,38},{7,39},{8,40},{9,... | collective-permute-start | bytes 589832 | tf_op jit(solution)/shard_map/ppermute | solution.py:532
  73.6 5.7 %copy-start.12 = (bf16[1,64,32,256]{3,2,1,0:T(8,128)(2,1)S(1)}, bf16[1,64,32,256]{3,2,1,0:T(8,128)(2,1)}, u32[]{:S(2)}) copy-start(bf16[1,64,32,256]{3,2,1,0:T(8,128)(2,1)} %param.28) | copy-start | bytes 3145732
  73.6 9.7 %collective-permute-start.14 = (bf16[256,384]{1,0:T(8,128)(2,1)}, bf16[256,384]{1,0:T(8,128)(2,1)}, u32[]{:S(2)}, u32[]{:S(2)}) collective-permute-start(bf16[256,384]{1,0:T(8,128)(2,1)} %get-tuple-element.563), channel_id=1, source_target_pairs={{96,64},{97,65},{98,66},{99,67},{100,68},{101,69},{102,70},{103,71... | collective-permute-start | bytes 589832 | tf_op jit(solution)/shard_map/ppermute | solution.py:532
  82.0 7.4 %copy-start.29 = (f32[1,384]{1,0:T(1,128)}, f32[1,384]{1,0:T(1,128)S(1)}, u32[]{:S(2)}) copy-start(f32[1,384]{1,0:T(1,128)S(1)} %get-tuple-element.294) | copy-start | bytes 4612
  82.0 2.2 collective-permute-start.13
  88.0 1.3 collective-permute-start.15
  90.1 173.0 %collective-permute-start.16 = (bf16[256,384]{1,0:T(8,128)(2,1)}, bf16[256,384]{1,0:T(8,128)(2,1)S(1)}, u32[]{:S(2)}, u32[]{:S(2)}) collective-permute-start(bf16[256,384]{1,0:T(8,128)(2,1)} %get-tuple-element.565), channel_id=1, source_target_pairs={{32,0},{33,1},{34,2},{35,3},{36,4},{37,5},{38,6},{39,7},{40,8},{41... | collective-permute-start | bytes 589832 | tf_op jit(solution)/shard_map/ppermute | solution.py:532
  91.4 2.4 collective-permute-start.17
  95.7 176.7 %copy-start.20 = (bf16[384,256]{0,1:T(8,128)(2,1)S(1)}, bf16[384,256]{0,1:T(8,128)(2,1)}, u32[]{:S(2)}) copy-start(bf16[384,256]{0,1:T(8,128)(2,1)} %copy-done.19) | copy-start | bytes 589828
  264.7 8.9 %copy-start.26 = (bf16[32,384]{1,0:T(8,128)(2,1)S(1)}, bf16[32,384]{1,0:T(8,128)(2,1)}, u32[]{:S(2)}) copy-start(bf16[32,384]{1,0:T(8,128)(2,1)} %get-tuple-element.298) | copy-start | bytes 73732
  264.8 8.9 %copy-start.27 = (bf16[32,384]{1,0:T(8,128)(2,1)S(1)}, bf16[32,384]{1,0:T(8,128)(2,1)}, u32[]{:S(2)}) copy-start(bf16[32,384]{1,0:T(8,128)(2,1)} %get-tuple-element.297) | copy-start | bytes 73732
  264.8 1.3 collective-permute-start.18
  266.9 8.4 %copy-start.16 = (f32[64,384]{1,0:T(8,128)S(1)}, f32[64,384]{1,0:T(8,128)}, u32[]{:S(2)}) copy-start(f32[64,384]{1,0:T(8,128)} %copy-done.15) | copy-start | bytes 294916
  266.9 15.7 %all-to-all-start.13 = ((bf16[16,32,384]{2,1,0:T(8,128)(2,1)}), bf16[16,32,384]{2,1,0:T(8,128)(2,1)S(1)}, u32[]{:S(2)}, u32[]{:S(2)}) async-start(bf16[16,32,384]{2,1,0:T(8,128)(2,1)} %both_cores.1), calls=%async_computation.13 | async-start | bytes 786432 | tf_op jit(solution)/shard_map/all_to_all | solution.py:48
  (15 other events, 40.7 us)
